TPU v7x, 32 devices: a whole 2x2x4 slice. The times are simulated.
32 devices in a mesh: fsdp: 8 (over z, x), sp: 4 (over y, core).
Axes of the slice: x: 2, y: 2, z: 4, core: 2. Of those that a mesh axis runs over, the one named last changes fastest.
Arguments:
- tokens: bfloat16 [2, 12288, 768], P(None, ('fsdp', 'sp')), may hold values from -6 to 6
- cotangent: bfloat16 [2, 12288, 768], P(None, ('fsdp', 'sp')), may hold values from -6 to 6
- lengths: int32 [2, 8, 3], P(None, 'fsdp'), may hold values from 1 to 1024, 1536 in all within a row
- dealing: int32 [2, 8, 1536], P(None, 'fsdp'), may hold values from 0 to 1535, each once within a row
- gain_attn: bfloat16 [768], P('fsdp'), may hold values from 0.099609375 to 1.8984375
- w_query: bfloat16 [768, 768], P('fsdp'), may hold values from -0.0546875 to 0.0546875
- w_key: bfloat16 [768, 768], P('fsdp'), may hold values from -0.21875 to 0.21875
- w_value: bfloat16 [768, 768], P('fsdp'), may hold values from -0.21875 to 0.21875
- w_out: bfloat16 [768, 768], P('fsdp'), may hold values from -0.875 to 0.875
- bias_table: bfloat16 [32, 12], P(None, 'sp'), may hold values from -4 to 4
- gain_ff: bfloat16 [768], P('fsdp'), may hold values from 0.099609375 to 1.8984375
- w_gate: bfloat16 [768, 2048], P('fsdp'), may hold values from -0.21875 to 0.21875
- w_up: bfloat16 [768, 2048], P('fsdp'), may hold values from -0.21875 to 0.21875
- w_down: bfloat16 [2048, 768], P('fsdp'), may hold values from -0.25 to 0.25
Outputs:
- output: bfloat16 [2, 12288, 768], P(None, ('fsdp', 'sp'))
- grad_tokens: bfloat16 [2, 12288, 768], P(None, ('fsdp', 'sp'))
- grad_gain_attn: float32 [768], P('fsdp')
- grad_query: float32 [768, 768], P('fsdp')
- grad_key: float32 [768, 768], P('fsdp')
- grad_value: float32 [768, 768], P('fsdp')
- grad_out: float32 [768, 768], P('fsdp')
- grad_bias: float32 [32, 12], P(None, 'sp')
- grad_gain_ff: float32 [768], P('fsdp')
- grad_gate: float32 [768, 2048], P('fsdp')
- grad_up: float32 [768, 2048], P('fsdp')
- grad_down: float32 [2048, 768], P('fsdp')
Inputs may be any that keep to these rules, and one draw needn't show every extreme that they name: In every micro-batch and group the 3 lengths sum to 1536, and the longest is exactly 1024. Each row dealing[m, g] is a permutation of the 1536 arrival indices.
All inputs are finite; a program needn't handle non-finite values.
Results may differ from a plain program's by a relative error of at most 0.018.
Values may be sent and summed in bfloat16 or wider, within the bound.
A program may use at most 192 MiB of HBM per device.

v0:
```python
import math

import jax
import jax.numpy as jnp
from jax import lax
from jax.sharding import PartitionSpec as P

bucket_edges = (1, 2, 3, 4, 5, 6, 7, 8, 12, 16, 23, 32, 46, 64, 91)
epsilon = 1e-06


def bucket_index(offset, half_count):
    distance = jnp.abs(offset)
    bucket_sum = jnp.where(offset > 0, half_count, 0).astype(jnp.int32)
    for border in bucket_edges:
        bucket_sum = bucket_sum + (distance >= border).astype(jnp.int32)
    return bucket_sum


def rms_norm(values, gain):
    return values * lax.rsqrt(jnp.mean(values * values, axis=-1, keepdims=True) + epsilon) * gain


def gated_unit(gate_proj, up_proj):
    return jax.nn.gelu(gate_proj, approximate=True) * up_proj


def matmul(left, right):
    return jnp.dot(left, right, preferred_element_type=jnp.float32)


def matmul_tn(left, right):
    return lax.dot_general(
        left, right, (((0,), (0,)), ((), ())), preferred_element_type=jnp.float32
    )


def matmul_nt(left, right):
    return lax.dot_general(
        left, right, (((1,), (1,)), ((), ())), preferred_element_type=jnp.float32
    )


def block_buckets(row_start, block_len, group_rows, bucket_count):
    key_slot = jnp.arange(group_rows, dtype=jnp.int32)
    query_slot = row_start + jnp.arange(block_len, dtype=jnp.int32)
    return bucket_index(key_slot[None, :] - query_slot[:, None], bucket_count // 2)


def block_logits(row_start, query_all, key_rows, segment, table, block_len):
    group_rows = key_rows.shape[0]
    bucket_count = table.shape[0]
    query_block = lax.dynamic_slice_in_dim(query_all, row_start, block_len, 0)
    seg_block = lax.dynamic_slice_in_dim(segment, row_start, block_len, 0)
    buckets = block_buckets(row_start, block_len, group_rows, bucket_count)[None]
    logits = jnp.einsum("qhd,khd->hqk", query_block, key_rows, preferred_element_type=jnp.float32)
    for label in range(bucket_count):
        logits = logits + jnp.where(buckets == label, table[label][:, None, None], 0.0)
    inside = (seg_block[:, None] == segment[None, :])[None]
    return (jnp.where(inside, logits, -1e30), query_block, buckets)


def attend(query_all, key_rows, value_rows, segment, table, block_len):
    group_rows, head_count, head_dim = key_rows.shape
    blocks = group_rows // block_len

    def one_block(block_idx):
        logits = block_logits(
            block_idx * block_len, query_all, key_rows, segment, table, block_len
        )[0]
        row_max = jnp.max(logits, axis=-1, keepdims=True)
        exponent = jnp.exp(logits - row_max)
        row_total = jnp.sum(exponent, axis=-1, keepdims=True)
        weights = (exponent / row_total).astype(jnp.bfloat16)
        context = jnp.einsum(
            "hqk,khd->qhd", weights, value_rows, preferred_element_type=jnp.float32
        )
        return (context.astype(jnp.bfloat16), (row_max + jnp.log(row_total))[..., 0])

    context, log_total = lax.map(one_block, jnp.arange(blocks, dtype=jnp.int32))
    return (context.reshape(group_rows, head_count * head_dim), log_total)


def attend_back(query_all, key_rows, value_rows, d_context, segment, table, log_total, block_len):
    group_rows, head_count, head_dim = key_rows.shape
    bucket_count = table.shape[0]
    blocks = group_rows // block_len

    def one_block(carried, block_idx):
        d_key, d_value, d_table = carried
        row_start = block_idx * block_len
        logits, query_block, buckets = block_logits(
            row_start, query_all, key_rows, segment, table, block_len
        )
        weights = jnp.exp(logits - log_total[block_idx][:, :, None])
        grad_block = lax.dynamic_slice_in_dim(d_context, row_start, block_len, 0)
        d_value = d_value + jnp.einsum(
            "hqk,qhd->khd",
            weights.astype(jnp.bfloat16),
            grad_block,
            preferred_element_type=jnp.float32,
        )
        d_weights = jnp.einsum(
            "qhd,khd->hqk", grad_block, value_rows, preferred_element_type=jnp.float32
        )
        row_dot = jnp.sum(weights * d_weights, axis=-1, keepdims=True)
        d_logits = weights * (d_weights - row_dot)
        bucket_grads = jnp.stack(
            [
                jnp.sum(jnp.where(buckets == label, d_logits, 0.0), axis=(1, 2))
                for label in range(bucket_count)
            ]
        )
        d_table = d_table + bucket_grads
        d_low = d_logits.astype(jnp.bfloat16)
        d_query = jnp.einsum("hqk,khd->qhd", d_low, key_rows, preferred_element_type=jnp.float32)
        d_key = d_key + jnp.einsum(
            "hqk,qhd->khd", d_low, query_block, preferred_element_type=jnp.float32
        )
        return ((d_key, d_value, d_table), d_query)

    zeros_kv = jnp.zeros((group_rows, head_count, head_dim), jnp.float32)
    zeros_table = jnp.zeros((bucket_count, head_count), jnp.float32)
    carried, d_query = lax.scan(
        one_block, (zeros_kv, zeros_kv, zeros_table), jnp.arange(blocks, dtype=jnp.int32)
    )
    return (d_query.reshape(group_rows, head_count, head_dim), carried[0], carried[1], carried[2])


def shards(
    tokens,
    cotangent,
    lengths,
    dealing,
    gain_attn,
    w_query,
    w_key,
    w_value,
    w_out,
    bias_table,
    gain_ff,
    w_gate,
    w_up,
    w_down,
):
    fsdp_count = lax.axis_size("fsdp")
    sp_count = lax.axis_size("sp")
    micro_count, token_rows, model_width = tokens.shape
    piece_rows = token_rows // fsdp_count
    group_rows = token_rows * sp_count
    head_count = bias_table.shape[1]
    local_width = model_width // sp_count
    head_dim = local_width // head_count
    block_len = math.gcd(group_rows, 512)
    table = bias_table.astype(jnp.float32)
    position = jnp.arange(group_rows, dtype=jnp.int32)
    stacked = jnp.stack((tokens, cotangent)).reshape(
        2, micro_count, fsdp_count, piece_rows, model_width
    )
    dealt = lax.all_to_all(stacked, "fsdp", split_axis=2, concat_axis=2, tiled=True).reshape(
        2, micro_count, token_rows, model_width
    )

    def collect():
        return (
            lax.all_gather(gain_attn, "fsdp", axis=0, tiled=True),
            lax.all_gather(w_query, "fsdp", axis=0, tiled=True),
            lax.all_gather(w_key, "fsdp", axis=0, tiled=True),
            lax.all_gather(w_value, "fsdp", axis=0, tiled=True),
            lax.all_gather(w_out, "fsdp", axis=0, tiled=True),
            lax.all_gather(gain_ff, "fsdp", axis=0, tiled=True),
            lax.all_gather(w_gate, "fsdp", axis=0, tiled=True),
            lax.all_gather(w_up, "fsdp", axis=0, tiled=True),
            lax.all_gather(w_down, "fsdp", axis=0, tiled=True),
        )

    totals = None
    table_grad = jnp.zeros((table.shape[0], head_count), jnp.float32)
    outputs = []
    input_grads = []
    for micro_idx in range(micro_count):
        gathered = collect()
        gain_one, query_w, key_w, value_w, out_w, gain_two, gate_w, up_w, down_w = gathered
        residual = dealt[0, micro_idx].astype(jnp.float32)
        upstream = dealt[1, micro_idx]
        normed = rms_norm(residual, gain_one.astype(jnp.float32)).astype(jnp.bfloat16)
        query_rows = matmul(normed, query_w).astype(jnp.bfloat16)
        key_rows = matmul(normed, key_w).astype(jnp.bfloat16)
        value_rows = matmul(normed, value_w).astype(jnp.bfloat16)
        packed = jnp.stack((query_rows, key_rows, value_rows)).reshape(
            3, token_rows, sp_count, local_width
        )
        head_rows = lax.all_to_all(packed, "sp", split_axis=2, concat_axis=1, tiled=True).reshape(
            3, group_rows, head_count, head_dim
        )
        slot_order = dealing[micro_idx, 0]
        inverse = jnp.zeros_like(slot_order).at[slot_order].set(position)
        slotted = head_rows[:, slot_order]
        bounds = jnp.cumsum(lengths[micro_idx, 0])
        segment = jnp.sum((position[:, None] >= bounds[None, :]).astype(jnp.int32), axis=1)
        context, log_total = attend(slotted[0], slotted[1], slotted[2], segment, table, block_len)
        arrival = context[inverse].reshape(sp_count, token_rows, 1, local_width)
        mixed = lax.all_to_all(arrival, "sp", split_axis=0, concat_axis=2, tiled=True).reshape(
            token_rows, model_width
        )
        middle = residual + matmul(mixed, out_w)
        normed_ff = rms_norm(middle, gain_two.astype(jnp.float32)).astype(jnp.bfloat16)
        gate_proj = matmul(normed_ff, gate_w)
        up_proj = matmul(normed_ff, up_w)
        hidden = gated_unit(gate_proj, up_proj).astype(jnp.bfloat16)
        outputs.append((middle + matmul(hidden, down_w)).astype(jnp.bfloat16))
        gain_one, query_w, key_w, value_w, out_w, gain_two, gate_w, up_w, down_w = collect()
        grad_down = matmul_tn(hidden, upstream)
        d_hidden = matmul_nt(upstream, down_w)
        d_gate, d_up = jax.vjp(gated_unit, gate_proj, up_proj)[1](d_hidden)
        d_gate = d_gate.astype(jnp.bfloat16)
        d_up = d_up.astype(jnp.bfloat16)
        grad_gate = matmul_tn(normed_ff, d_gate)
        grad_up = matmul_tn(normed_ff, d_up)
        d_normed_ff = matmul_nt(d_gate, gate_w) + matmul_nt(d_up, up_w)
        d_middle, grad_gain_two = jax.vjp(rms_norm, middle, gain_two.astype(jnp.float32))[1](
            d_normed_ff
        )
        d_middle = d_middle + upstream.astype(jnp.float32)
        d_attended = d_middle.astype(jnp.bfloat16)
        grad_out = matmul_tn(mixed, d_attended)
        d_mixed = (
            matmul_nt(d_attended, out_w)
            .astype(jnp.bfloat16)
            .reshape(token_rows, sp_count, local_width)
        )
        d_heads = lax.all_to_all(d_mixed, "sp", split_axis=1, concat_axis=0, tiled=True).reshape(
            group_rows, head_count, head_dim
        )
        d_query, d_key, d_value, d_table = attend_back(
            slotted[0],
            slotted[1],
            slotted[2],
            d_heads[slot_order],
            segment,
            table,
            log_total,
            block_len,
        )
        table_grad = table_grad + d_table
        d_packed = (
            jnp.stack((d_query, d_key, d_value))
            .astype(jnp.bfloat16)[:, inverse]
            .reshape(3, sp_count, token_rows, 1, local_width)
        )
        d_rows = lax.all_to_all(d_packed, "sp", split_axis=1, concat_axis=3, tiled=True).reshape(
            3, token_rows, model_width
        )
        grad_query = matmul_tn(normed, d_rows[0])
        grad_key = matmul_tn(normed, d_rows[1])
        grad_value = matmul_tn(normed, d_rows[2])
        d_normed = (
            matmul_nt(d_rows[0], query_w)
            + matmul_nt(d_rows[1], key_w)
            + matmul_nt(d_rows[2], value_w)
        )
        d_residual, grad_gain_one = jax.vjp(rms_norm, residual, gain_one.astype(jnp.float32))[1](
            d_normed
        )
        input_grads.append((d_middle + d_residual).astype(jnp.bfloat16))
        local_grads = (
            grad_gain_one,
            grad_query,
            grad_key,
            grad_value,
            grad_out,
            grad_gain_two,
            grad_gate,
            grad_up,
            grad_down,
        )
        summed = (
            lax.psum_scatter(local_grads[0], "fsdp", scatter_dimension=0, tiled=True),
            lax.psum_scatter(local_grads[1], "fsdp", scatter_dimension=0, tiled=True),
            lax.psum_scatter(local_grads[2], "fsdp", scatter_dimension=0, tiled=True),
            lax.psum_scatter(local_grads[3], "fsdp", scatter_dimension=0, tiled=True),
            lax.psum_scatter(local_grads[4], "fsdp", scatter_dimension=0, tiled=True),
            lax.psum_scatter(local_grads[5], "fsdp", scatter_dimension=0, tiled=True),
            lax.psum_scatter(local_grads[6], "fsdp", scatter_dimension=0, tiled=True),
            lax.psum_scatter(local_grads[7], "fsdp", scatter_dimension=0, tiled=True),
            lax.psum_scatter(local_grads[8], "fsdp", scatter_dimension=0, tiled=True),
        )
        if totals is None:
            totals = summed
        else:
            totals = tuple((earlier + later for earlier, later in zip(totals, summed)))
    totals = (
        lax.psum(totals[0].astype(jnp.bfloat16), "sp").astype(jnp.float32),
        lax.psum(totals[1].astype(jnp.bfloat16), "sp").astype(jnp.float32),
        lax.psum(totals[2].astype(jnp.bfloat16), "sp").astype(jnp.float32),
        lax.psum(totals[3].astype(jnp.bfloat16), "sp").astype(jnp.float32),
        lax.psum(totals[4].astype(jnp.bfloat16), "sp").astype(jnp.float32),
        lax.psum(totals[5].astype(jnp.bfloat16), "sp").astype(jnp.float32),
        lax.psum(totals[6].astype(jnp.bfloat16), "sp").astype(jnp.float32),
        lax.psum(totals[7].astype(jnp.bfloat16), "sp").astype(jnp.float32),
        lax.psum(totals[8].astype(jnp.bfloat16), "sp").astype(jnp.float32),
    )
    table_total = lax.psum(table_grad, "fsdp")
    returning = jnp.stack((jnp.stack(outputs), jnp.stack(input_grads))).reshape(
        2, micro_count, fsdp_count, piece_rows, model_width
    )
    returned = lax.all_to_all(returning, "fsdp", split_axis=2, concat_axis=2, tiled=True).reshape(
        2, micro_count, token_rows, model_width
    )
    return (
        returned[0],
        returned[1],
        totals[0],
        totals[1],
        totals[2],
        totals[3],
        totals[4],
        table_total,
        totals[5],
        totals[6],
        totals[7],
        totals[8],
    )


def solution(mesh):
    return jax.shard_map(
        shards,
        mesh=mesh,
        in_specs=(
            P(None, ("fsdp", "sp"), None),
            P(None, ("fsdp", "sp"), None),
            P(None, "fsdp", None),
            P(None, "fsdp", None),
            P("fsdp"),
            P("fsdp", None),
            P("fsdp", None),
            P("fsdp", None),
            P("fsdp", None),
            P(None, "sp"),
            P("fsdp"),
            P("fsdp", None),
            P("fsdp", None),
            P("fsdp", None),
        ),
        out_specs=(
            P(None, ("fsdp", "sp"), None),
            P(None, ("fsdp", "sp"), None),
            P("fsdp"),
            P("fsdp", None),
            P("fsdp", None),
            P("fsdp", None),
            P("fsdp", None),
            P(None, "sp"),
            P("fsdp"),
            P("fsdp", None),
            P("fsdp", None),
            P("fsdp", None),
        ),
        check_vma=False,
    )
```

profile of v0, /device:TPU:14, one launch (start us, length us, event | category | flops | bytes accessed | tf_op | source)
XLA Modules:
  0.0 2651.7 jit_solution(5734325011640672465)
XLA Ops:
  23.6 71.5 %all-reduce.5 = (bf16[768]{0:T(1024)(128)(2,1)S(1)}, bf16[768]{0:T(1024)(128)(2,1)S(1)}) all-reduce(bf16[768]{0:T(1024)(128)(2,1)S(1)} %dynamic-update-slice, bf16[768]{0:T(1024)(128)(2,1)S(1)} %dynamic-update-slice.1), channel_id=1, replica_groups=mesh['fsdp'=8,'sp'=4] {'fsdp'}, use_global_device_ids=true, to_apply=%add | all-reduce | flops 1536 | bytes 6144
  126.6 37.9 %all-gather.12.cloned.1.call-done = bf16[768,768]{1,0:T(8,128)(2,1)} async-done(((bf16[96,768]{1,0:T(8,128)(2,1)}), bf16[768,768]{1,0:T(8,128)(2,1)}) %all-gather.12.cloned.1.call-update) | async-done | bytes 1179664 | tf_op jit(solution)/shard_map/all_gather | solution.py:169
  237.5 272.0 %while.58 = (s32[]{:T(128)}, bf16[3,512,3,64]{1,3,2,0:T(8,128)(2,1)}, f32[3,3,512]{2,1,0:T(4,128)}, s32[3]{0:T(128)}, s32[1536]{0:T(1024)}, /*index=5*/bf16[1536...) while((s32[]{:T(128)}, ...), condition=%wide.region_6.7_spmd, body=%wide.region_3.0_spmd.sunk | while | flops 836074496 | bytes 119648248 | solution.py:80
  280.4 47.4 %fusion.345 = (f32[3,512]{1,0:T(4,128)}, f32[3,512,1536]{2,1,0:T(8,128)}) fusion(f32[3]{0:T(128)} %get-tuple-element.1611, pred[512,1536]{1,0:T(8,128)(4,1)} %get-tuple-element.1612, f32[3]{0:T(128)} %get-tuple-element.1613, pred[512,1536]{1,0:T(8,128)(4,1)} %get-tuple-element.1614, f32[3]{0:T(128)} %get-tuple-element.1615, ...), kind=kOutput, calls=%fused_computation.650.clone.1 | convolution fusion | flops 457701888 | bytes 36198404 | tf_op jit(solution)/shard_map/while/body/eval_jaxpr/qhd,khd->hqk/dot_general | solution.py:56
  366.4 47.4 %fusion.345 = (f32[3,512]{1,0:T(4,128)}, f32[3,512,1536]{2,1,0:T(8,128)}) fusion(f32[3]{0:T(128)} %get-tuple-element.1611, pred[512,1536]{1,0:T(8,128)(4,1)} %get-tuple-element.1612, f32[3]{0:T(128)} %get-tuple-element.1613, pred[512,1536]{1,0:T(8,128)(4,1)} %get-tuple-element.1614, f32[3]{0:T(128)} %get-tuple-element.1615, ...), kind=kOutput, calls=%fused_computation.650.clone.1 | convolution fusion | flops 457701888 | bytes 36198404 | tf_op jit(solution)/shard_map/while/body/eval_jaxpr/qhd,khd->hqk/dot_general | solution.py:56
  452.4 47.4 %fusion.345 = (f32[3,512]{1,0:T(4,128)}, f32[3,512,1536]{2,1,0:T(8,128)}) fusion(f32[3]{0:T(128)} %get-tuple-element.1611, pred[512,1536]{1,0:T(8,128)(4,1)} %get-tuple-element.1612, f32[3]{0:T(128)} %get-tuple-element.1613, pred[512,1536]{1,0:T(8,128)(4,1)} %get-tuple-element.1614, f32[3]{0:T(128)} %get-tuple-element.1615, ...), kind=kOutput, calls=%fused_computation.650.clone.1 | convolution fusion | flops 457701888 | bytes 36198404 | tf_op jit(solution)/shard_map/while/body/eval_jaxpr/qhd,khd->hqk/dot_general | solution.py:56
  557.6 258.7 %while.59 = (s32[]{:T(128)}, bf16[3,512,3,64]{1,3,2,0:T(8,128)(2,1)}, f32[3,3,512]{2,1,0:T(4,128)}, s32[3]{0:T(128)}, s32[1536]{0:T(1024)}, /*index=5*/bf16[1536...) while((s32[]{:T(128)}, ...), condition=%wide.region_15.16_spmd, body=%wide.region_12.15_spmd.sunk | while | flops 836074496 | bytes 119648248 | solution.py:80
  559.7 23.2 broadcast_compare_fusion.142
  587.1 47.4 %fusion.350 = (f32[3,512]{1,0:T(4,128)}, f32[3,512,1536]{2,1,0:T(8,128)}) fusion(f32[3]{0:T(128)} %get-tuple-element.1686, pred[512,1536]{1,0:T(8,128)(4,1)} %get-tuple-element.1687, f32[3]{0:T(128)} %get-tuple-element.1688, pred[512,1536]{1,0:T(8,128)(4,1)} %get-tuple-element.1689, f32[3]{0:T(128)} %get-tuple-element.1690, ...), kind=kOutput, calls=%fused_computation.651.clone.1 | convolution fusion | flops 457701888 | bytes 36198404 | tf_op jit(solution)/shard_map/while/body/eval_jaxpr/qhd,khd->hqk/dot_general | solution.py:56
  673.2 47.4 %fusion.350 = (f32[3,512]{1,0:T(4,128)}, f32[3,512,1536]{2,1,0:T(8,128)}) fusion(f32[3]{0:T(128)} %get-tuple-element.1686, pred[512,1536]{1,0:T(8,128)(4,1)} %get-tuple-element.1687, f32[3]{0:T(128)} %get-tuple-element.1688, pred[512,1536]{1,0:T(8,128)(4,1)} %get-tuple-element.1689, f32[3]{0:T(128)} %get-tuple-element.1690, ...), kind=kOutput, calls=%fused_computation.651.clone.1 | convolution fusion | flops 457701888 | bytes 36198404 | tf_op jit(solution)/shard_map/while/body/eval_jaxpr/qhd,khd->hqk/dot_general | solution.py:56
  759.2 47.4 %fusion.350 = (f32[3,512]{1,0:T(4,128)}, f32[3,512,1536]{2,1,0:T(8,128)}) fusion(f32[3]{0:T(128)} %get-tuple-element.1686, pred[512,1536]{1,0:T(8,128)(4,1)} %get-tuple-element.1687, f32[3]{0:T(128)} %get-tuple-element.1688, pred[512,1536]{1,0:T(8,128)(4,1)} %get-tuple-element.1689, f32[3]{0:T(128)} %get-tuple-element.1690, ...), kind=kOutput, calls=%fused_computation.651.clone.1 | convolution fusion | flops 457701888 | bytes 36198404 | tf_op jit(solution)/shard_map/while/body/eval_jaxpr/qhd,khd->hqk/dot_general | solution.py:56
  918.2 477.6 %while.60 = (s32[]{:T(128)}, f32[1536,3,64]{0,2,1:T(8,128)}, f32[1536,3,64]{0,2,1:T(8,128)}, f32[32,3]{0,1:T(4,128)}, bf16[3,512,3,64]{1,3,2,0:T(8,128)(2,1)}, /...) while((s32[]{:T(128)}, f32[1536,3,64]{0,2,1:T(8,128)}, ...), condition=%wide.region_53.54_spmd.clone, body=%wide.region_19.53_spmd.clone.sunk | while | flops 1898839296 | bytes 315215104 | solution.py:124
  955.6 49.2 %multiply_reduce_fusion.10 = (f32[3,512]{1,0:T(4,128)S(1)}, f32[3,512,1536]{2,1,0:T(8,128)}) fusion(f32[3,512,1536]{2,1,0:T(8,128)} %fusion.362, f32[3,512]{1,0:T(4,128)S(1)} %dynamic-slice_bitcast_fusion.4, f32[3]{0:T(128)S(1)} %get-tuple-element.1783, pred[512,1536]{1,0:T(8,128)(4,1)} %get-tuple-element.1765, f32[3]{0:T(128)S(1)} %get-tuple-element.1784, ...), kind=kOutput, calls=%fused_computation.235.clone.1 | convolution fusion | flops 462420480 | bytes 45625732 | tf_op jit(solution)/shard_map/while/body/eval_jaxpr/qhd,khd->hqk/dot_general | solution.py:56
  1004.9 33.0 %select_reduce_fusion.68 = (f32[3]{0:T(128)S(1)}, f32[3]{0:T(128)S(1)}, f32[3]{0:T(128)S(1)}, f32[3]{0:T(128)S(1)}, f32[3]{0:T(128)S(1)}, /*index=5*/f32[3]{0:T(...) fusion(pred[512,1536]{1,0:T(8,128)(4,1)} %get-tuple-element.176, ...), kind=kLoop, calls=%fused_computation.202.clone.1 | loop fusion | flops 89653200 | bytes 42473688 | tf_op jit(solution)/shard_map/while/body/eval_jaxpr/reduce_sum | solution.py:110
  1113.9 49.3 %multiply_reduce_fusion.10 = (f32[3,512]{1,0:T(4,128)S(1)}, f32[3,512,1536]{2,1,0:T(8,128)}) fusion(f32[3,512,1536]{2,1,0:T(8,128)} %fusion.362, f32[3,512]{1,0:T(4,128)S(1)} %dynamic-slice_bitcast_fusion.4, f32[3]{0:T(128)S(1)} %get-tuple-element.1783, pred[512,1536]{1,0:T(8,128)(4,1)} %get-tuple-element.1765, f32[3]{0:T(128)S(1)} %get-tuple-element.1784, ...), kind=kOutput, calls=%fused_computation.235.clone.1 | convolution fusion | flops 462420480 | bytes 45625732 | tf_op jit(solution)/shard_map/while/body/eval_jaxpr/qhd,khd->hqk/dot_general | solution.py:56
  1163.3 33.0 %select_reduce_fusion.68 = (f32[3]{0:T(128)S(1)}, f32[3]{0:T(128)S(1)}, f32[3]{0:T(128)S(1)}, f32[3]{0:T(128)S(1)}, f32[3]{0:T(128)S(1)}, /*index=5*/f32[3]{0:T(...) fusion(pred[512,1536]{1,0:T(8,128)(4,1)} %get-tuple-element.176, ...), kind=kLoop, calls=%fused_computation.202.clone.1 | loop fusion | flops 89653200 | bytes 42473688 | tf_op jit(solution)/shard_map/while/body/eval_jaxpr/reduce_sum | solution.py:110
  1273.2 49.3 %multiply_reduce_fusion.10 = (f32[3,512]{1,0:T(4,128)S(1)}, f32[3,512,1536]{2,1,0:T(8,128)}) fusion(f32[3,512,1536]{2,1,0:T(8,128)} %fusion.362, f32[3,512]{1,0:T(4,128)S(1)} %dynamic-slice_bitcast_fusion.4, f32[3]{0:T(128)S(1)} %get-tuple-element.1783, pred[512,1536]{1,0:T(8,128)(4,1)} %get-tuple-element.1765, f32[3]{0:T(128)S(1)} %get-tuple-element.1784, ...), kind=kOutput, calls=%fused_computation.235.clone.1 | convolution fusion | flops 462420480 | bytes 45625732 | tf_op jit(solution)/shard_map/while/body/eval_jaxpr/qhd,khd->hqk/dot_general | solution.py:56
  1322.6 33.0 %select_reduce_fusion.68 = (f32[3]{0:T(128)S(1)}, f32[3]{0:T(128)S(1)}, f32[3]{0:T(128)S(1)}, f32[3]{0:T(128)S(1)}, f32[3]{0:T(128)S(1)}, /*index=5*/f32[3]{0:T(...) fusion(pred[512,1536]{1,0:T(8,128)(4,1)} %get-tuple-element.176, ...), kind=kLoop, calls=%fused_computation.202.clone.1 | loop fusion | flops 89653200 | bytes 42473688 | tf_op jit(solution)/shard_map/while/body/eval_jaxpr/reduce_sum | solution.py:110
  1447.1 467.4 %while.61 = (s32[]{:T(128)}, f32[1536,3,64]{0,2,1:T(8,128)}, f32[1536,3,64]{0,2,1:T(8,128)}, f32[32,3]{0,1:T(4,128)S(1)}, bf16[3,512,3,64]{1,3,2,0:T(8,128)(2,1)...) while((s32[]{:T(128)}, f32[1536,3,64]{0,2,1:T(8,128)}, ...), condition=%wide.region_90.91_spmd.clone, body=%wide.region_56.90_spmd.clone.sunk | while | flops 1898839296 | bytes 315215232 | solution.py:124
  1482.3 49.0 %multiply_reduce_fusion.11 = (f32[3,512]{1,0:T(4,128)S(1)}, f32[3,512,1536]{2,1,0:T(8,128)}) fusion(f32[3,512,1536]{2,1,0:T(8,128)} %fusion.375, f32[3,512]{1,0:T(4,128)S(1)} %dynamic-slice_bitcast_fusion.5, f32[3]{0:T(128)S(1)} %get-tuple-element.1895, pred[512,1536]{1,0:T(8,128)(4,1)} %get-tuple-element.1877, f32[3]{0:T(128)S(1)} %get-tuple-element.1896, ...), kind=kOutput, calls=%fused_computation.377.clone.1 | convolution fusion | flops 462420480 | bytes 45625732 | tf_op jit(solution)/shard_map/while/body/eval_jaxpr/qhd,khd->hqk/dot_general | solution.py:56
  1531.5 33.0 %select_reduce_fusion.70 = (f32[3]{0:T(128)S(1)}, f32[3]{0:T(128)S(1)}, f32[3]{0:T(128)S(1)}, f32[3]{0:T(128)S(1)}, f32[3]{0:T(128)S(1)}, /*index=5*/f32[3]{0:T(...) fusion(pred[512,1536]{1,0:T(8,128)(4,1)} %get-tuple-element.187, ...), kind=kLoop, calls=%fused_computation.344.clone.1 | loop fusion | flops 89653200 | bytes 42473688 | tf_op jit(solution)/shard_map/while/body/eval_jaxpr/reduce_sum | solution.py:110
  1637.7 49.1 %multiply_reduce_fusion.11 = (f32[3,512]{1,0:T(4,128)S(1)}, f32[3,512,1536]{2,1,0:T(8,128)}) fusion(f32[3,512,1536]{2,1,0:T(8,128)} %fusion.375, f32[3,512]{1,0:T(4,128)S(1)} %dynamic-slice_bitcast_fusion.5, f32[3]{0:T(128)S(1)} %get-tuple-element.1895, pred[512,1536]{1,0:T(8,128)(4,1)} %get-tuple-element.1877, f32[3]{0:T(128)S(1)} %get-tuple-element.1896, ...), kind=kOutput, calls=%fused_computation.377.clone.1 | convolution fusion | flops 462420480 | bytes 45625732 | tf_op jit(solution)/shard_map/while/body/eval_jaxpr/qhd,khd->hqk/dot_general | solution.py:56
  1687.0 33.0 %select_reduce_fusion.70 = (f32[3]{0:T(128)S(1)}, f32[3]{0:T(128)S(1)}, f32[3]{0:T(128)S(1)}, f32[3]{0:T(128)S(1)}, f32[3]{0:T(128)S(1)}, /*index=5*/f32[3]{0:T(...) fusion(pred[512,1536]{1,0:T(8,128)(4,1)} %get-tuple-element.187, ...), kind=kLoop, calls=%fused_computation.344.clone.1 | loop fusion | flops 89653200 | bytes 42473688 | tf_op jit(solution)/shard_map/while/body/eval_jaxpr/reduce_sum | solution.py:110
  1793.6 48.9 %multiply_reduce_fusion.11 = (f32[3,512]{1,0:T(4,128)S(1)}, f32[3,512,1536]{2,1,0:T(8,128)}) fusion(f32[3,512,1536]{2,1,0:T(8,128)} %fusion.375, f32[3,512]{1,0:T(4,128)S(1)} %dynamic-slice_bitcast_fusion.5, f32[3]{0:T(128)S(1)} %get-tuple-element.1895, pred[512,1536]{1,0:T(8,128)(4,1)} %get-tuple-element.1877, f32[3]{0:T(128)S(1)} %get-tuple-element.1896, ...), kind=kOutput, calls=%fused_computation.377.clone.1 | convolution fusion | flops 462420480 | bytes 45625732 | tf_op jit(solution)/shard_map/while/body/eval_jaxpr/qhd,khd->hqk/dot_general | solution.py:56
  1842.6 33.0 %select_reduce_fusion.70 = (f32[3]{0:T(128)S(1)}, f32[3]{0:T(128)S(1)}, f32[3]{0:T(128)S(1)}, f32[3]{0:T(128)S(1)}, f32[3]{0:T(128)S(1)}, /*index=5*/f32[3]{0:T(...) fusion(pred[512,1536]{1,0:T(8,128)(4,1)} %get-tuple-element.187, ...), kind=kLoop, calls=%fused_computation.344.clone.1 | loop fusion | flops 89653200 | bytes 42473688 | tf_op jit(solution)/shard_map/while/body/eval_jaxpr/reduce_sum | solution.py:110
  2036.1 39.1 %reduce-scatter.12.cloned.1.call-done = f32[96,768]{1,0:T(8,128)} async-done(((f32[768,768]{1,0:T(8,128)}), f32[96,768]{1,0:T(8,128)}) %reduce-scatter.12.cloned.1.call-update) | async-done | bytes 294928 | tf_op jit(solution)/shard_map/reduce_scatter | solution.py:281
  2076.8 75.3 %reduce-scatter.10.cloned.1.call-done = f32[96,768]{1,0:T(8,128)} async-done(((f32[768,768]{1,0:T(8,128)}), f32[96,768]{1,0:T(8,128)}) %reduce-scatter.10.cloned.1.call-update) | async-done | bytes 294928 | tf_op jit(solution)/shard_map/reduce_scatter | solution.py:280
  2153.8 70.1 %reduce-scatter.8.cloned.1.call-done = f32[96,768]{1,0:T(8,128)} async-done(((f32[768,768]{1,0:T(8,128)}), f32[96,768]{1,0:T(8,128)}) %reduce-scatter.8.cloned.1.call-update) | async-done | bytes 294928 | tf_op jit(solution)/shard_map/reduce_scatter | solution.py:279
  2225.5 118.8 %reduce-scatter.18.cloned.1.call-done = f32[96,2048]{1,0:T(8,128)} async-done(((f32[768,2048]{1,0:T(8,128)}), f32[96,2048]{1,0:T(8,128)}) %reduce-scatter.18.cloned.1.call-update) | async-done | bytes 786448 | tf_op jit(solution)/shard_map/reduce_scatter | solution.py:285
  2346.2 118.8 %reduce-scatter.16.cloned.1.call-done = f32[96,2048]{1,0:T(8,128)} async-done(((f32[768,2048]{1,0:T(8,128)}), f32[96,2048]{1,0:T(8,128)}) %reduce-scatter.16.cloned.1.call-update) | async-done | bytes 786448 | tf_op jit(solution)/shard_map/reduce_scatter | solution.py:284
  2466.9 118.6 %reduce-scatter.20.cloned.1.call-done = f32[256,768]{1,0:T(8,128)} async-done(((f32[2048,768]{1,0:T(8,128)}), f32[256,768]{1,0:T(8,128)}) %reduce-scatter.20.cloned.1.call-update) | async-done | bytes 786448 | tf_op jit(solution)/shard_map/reduce_scatter | solution.py:286
  2588.8 29.6 %all-reduce.4 = (bf16[768]{0:T(1024)(128)(2,1)S(1)}, f32[32,3]{0,1:T(4,128)}, bf16[768]{0:T(1024)(128)(2,1)S(1)}) all-reduce(f32[768]{0:T(1024)S(1)} %add.6766, f32[32,3]{0,1:T(4,128)S(1)} %add.6761, f32[768]{0:T(1024)S(1)} %add.6771), channel_id=11, replica_groups=mesh['fsdp'=8,'sp'=4] {'fsdp'}, use_global_device_ids=true, to_apply=%region_93.94.clone | all-reduce | flops 1632 | bytes 9984
  (1056 shorter events, 1117.3 us)
Async XLA Ops:
  7.2 108.3 %all-gather.8.cloned.1.call-start = ((), (), s32[]{:S(2)}) async-start(), calls=%async_computation.17 | async-start | bytes 1327104 | tf_op jit(solution)/shard_map/all_gather | solution.py:167
  7.9 114.6 %all-gather.10.cloned.1.call-start = ((), (), s32[]{:S(2)}) async-start(), calls=%async_computation.18 | async-start | bytes 1327104 | tf_op jit(solution)/shard_map/all_gather | solution.py:168
  8.7 155.9 %all-gather.12.cloned.1.call-start = ((), (), s32[]{:S(2)}) async-start(), calls=%async_computation.19 | async-start | bytes 1327104 | tf_op jit(solution)/shard_map/all_gather | solution.py:169
  9.4 819.0 %all-gather.20.cloned.1.call-start = ((), (), s32[]{:S(2)}) async-start(), calls=%async_computation.23 | async-start | bytes 3538944 | tf_op jit(solution)/shard_map/all_gather | solution.py:174
  10.0 830.2 %all-gather.14.cloned.1.call-start = ((), (), s32[]{:S(2)}) async-start(), calls=%async_computation.20 | async-start | bytes 1327104 | tf_op jit(solution)/shard_map/all_gather | solution.py:170
  10.6 840.9 %all-gather.16.cloned.1.call-start = ((), (), s32[]{:S(2)}) async-start(), calls=%async_computation.21 | async-start | bytes 3538944 | tf_op jit(solution)/shard_map/all_gather | solution.py:172
  14.6 80.5 %copy-start.129 = (bf16[32,3]{0,1:T(4,128)(2,1)S(1)}, bf16[32,3]{0,1:T(4,128)(2,1)}, u32[]{:S(2)}) copy-start(bf16[32,3]{0,1:T(4,128)(2,1)} %param.31) | copy-start | bytes 580
  14.7 80.6 %copy-start.130 = (s32[2,1,3]{2,1,0:T(1,128)S(1)}, s32[2,1,3]{2,1,0:T(1,128)}, u32[]{:S(2)}) copy-start(s32[2,1,3]{2,1,0:T(1,128)} %param.24) | copy-start | bytes 76
  14.7 81.6 %copy-start.126 = (s32[2,1,1536]{2,1,0:T(1,128)S(1)}, s32[2,1,1536]{2,1,0:T(1,128)}, u32[]{:S(2)}) copy-start(s32[2,1,1536]{2,1,0:T(1,128)} %param.25) | copy-start | bytes 36868
  14.7 97.8 %all-to-all-start = ((bf16[2,2,8,48,768]{4,3,1,0,2:T(8,128)(2,1)}), bf16[2,2,8,48,768]{4,3,1,0,2:T(8,128)(2,1)}, u32[]{:S(2)}, u32[]{:S(2)}) async-start(bf16[2,2,8,48,768]{4,3,1,0,2:T(8,128)(2,1)} %copy.438), calls=%async_computation | async-start | bytes 4718592 | tf_op jit(solution)/shard_map/all_to_all | solution.py:160
  21.0 835.6 %all-gather.18.cloned.1.call-start = ((), (), s32[]{:S(2)}) async-start(), calls=%async_computation.22 | async-start | bytes 3538944 | tf_op jit(solution)/shard_map/all_gather | solution.py:173
  114.3 74.0 %copy-start.34 = (bf16[2,2,8,48,768]{4,3,2,1,0:T(8,128)(2,1)}, bf16[2,2,8,48,768]{4,3,2,1,0:T(8,128)(2,1)S(1)}, u32[]{:S(2)}) copy-start(bf16[2,2,8,48,768]{4,3,2,1,0:T(8,128)(2,1)S(1)} %copy.439) | copy-start | bytes 7077892
  172.2 25.6 all-to-all-start.1
  197.8 322.2 %all-to-all-start.3 = ((bf16[3,384,4,192]{1,3,0,2:T(8,128)(2,1)}), bf16[3,384,4,192]{1,3,0,2:T(8,128)(2,1)}, u32[]{:S(2)}, u32[]{:S(2)}) async-start(bf16[3,384,4,192]{1,3,0,2:T(8,128)(2,1)} %copy.456), calls=%async_computation.3 | async-start | bytes 3538944 | tf_op jit(solution)/shard_map/all_to_all | solution.py:193
  520.0 316.7 %all-to-all-start.2 = ((bf16[4,384,1,192]{1,3,2,0:T(8,128)(2,1)}), bf16[4,384,1,192]{1,3,2,0:T(8,128)(2,1)}, u32[]{:S(2)}, u32[]{:S(2)}) async-start(bf16[4,384,1,192]{1,3,2,0:T(8,128)(2,1)} %copy.452), calls=%async_computation.2 | async-start | bytes 1179648 | tf_op jit(solution)/shard_map/all_to_all | solution.py:203
  836.7 11.4 all-to-all-start.4
  888.4 13.8 all-to-all-start.5
  894.2 1140.3 %reduce-scatter.14.cloned.1.call-start = ((), (), s32[]{:S(2)}) async-start(), calls=%async_computation.27 | async-start | bytes 2654208 | tf_op jit(solution)/shard_map/reduce_scatter | solution.py:282
  902.2 530.5 %all-to-all-start.7 = ((bf16[384,4,192]{0,2,1:T(8,128)(2,1)}), bf16[384,4,192]{0,2,1:T(8,128)(2,1)}, u32[]{:S(2)}, u32[]{:S(2)}) async-start(bf16[384,4,192]{0,2,1:T(8,128)(2,1)} %bitcast.130), calls=%async_computation.7 | async-start | bytes 1179648 | tf_op jit(solution)/shard_map/all_to_all | solution.py:232
  1432.7 518.9 %all-to-all-start.6 = ((bf16[3,4,384,1,192]{2,4,0,3,1:T(8,128)(2,1)}), bf16[3,4,384,1,192]{2,4,0,3,1:T(8,128)(2,1)}, u32[]{:S(2)}, u32[]{:S(2)}) async-start(bf16[3,4,384,1,192]{2,4,0,3,1:T(8,128)(2,1)} %copy.477), calls=%async_computation.6 | async-start | bytes 3538944 | tf_op jit(solution)/shard_map/all_to_all | solution.py:251
  1951.5 24.1 all-to-all-start.8
  1955.1 120.1 %reduce-scatter.12.cloned.1.call-start = ((), (), s32[]{:S(2)}) async-start(), calls=%async_computation.26 | async-start | bytes 2654208 | tf_op jit(solution)/shard_map/reduce_scatter | solution.py:281
  1982.8 169.4 %reduce-scatter.10.cloned.1.call-start = ((), (), s32[]{:S(2)}) async-start(), calls=%async_computation.25 | async-start | bytes 2654208 | tf_op jit(solution)/shard_map/reduce_scatter | solution.py:280
  1986.2 237.7 %reduce-scatter.8.cloned.1.call-start = ((), (), s32[]{:S(2)}) async-start(), calls=%async_computation.24 | async-start | bytes 2654208 | tf_op jit(solution)/shard_map/reduce_scatter | solution.py:279
  1989.8 354.5 %reduce-scatter.18.cloned.1.call-start = ((), (), s32[]{:S(2)}) async-start(), calls=%async_computation.29 | async-start | bytes 7077888 | tf_op jit(solution)/shard_map/reduce_scatter | solution.py:285
  1998.1 466.9 %reduce-scatter.16.cloned.1.call-start = ((), (), s32[]{:S(2)}) async-start(), calls=%async_computation.28 | async-start | bytes 7077888 | tf_op jit(solution)/shard_map/reduce_scatter | solution.py:284
  2006.1 579.4 %reduce-scatter.20.cloned.1.call-start = ((), (), s32[]{:S(2)}) async-start(), calls=%async_computation.30 | async-start | bytes 7077888 | tf_op jit(solution)/shard_map/reduce_scatter | solution.py:286
  2029.1 596.6 %all-to-all-start.9 = ((bf16[2,2,8,48,768]{4,3,1,0,2:T(8,128)(2,1)}), bf16[2,2,8,48,768]{4,3,1,0,2:T(8,128)(2,1)S(1)}, u32[]{:S(2)}, u32[]{:S(2)}) async-start(bf16[2,2,8,48,768]{4,3,1,0,2:T(8,128)(2,1)} %maximum_maximum_fusion), calls=%async_computation.9 | async-start | bytes 4718592 | tf_op jit(solution)/shard_map/all_to_all | solution.py:307
  2034.4 601.5 %all-reduce.10.cloned.1.call-start = ((), (), s32[]{:S(2)}) async-start(), calls=%async_computation.31 | async-start | bytes 3538944 | tf_op jit(solution)/shard_map/psum | solution.py:294
  2076.8 511.2 %copy-start.125 = (f32[768]{0:T(1024)S(1)}, f32[768]{0:T(1024)}, u32[]{:S(2)}) copy-start(f32[768]{0:T(1024)} %get-tuple-element.636) | copy-start | bytes 9220
  2076.8 511.2 %copy-start.127 = (f32[768]{0:T(1024)S(1)}, f32[768]{0:T(1024)}, u32[]{:S(2)}) copy-start(f32[768]{0:T(1024)} %get-tuple-element.634) | copy-start | bytes 9220
  2076.8 511.3 %copy-start.109 = (f32[32,3]{0,1:T(4,128)S(1)}, f32[32,3]{0,1:T(4,128)}, u32[]{:S(2)}) copy-start(f32[32,3]{0,1:T(4,128)} %copy-done.108) | copy-start | bytes 1156
  (228 other events, 3874.4 us)
Sparse Core Ops, SparseCore 0:
  10.2 70.7 all-gather.7
  83.2 39.2 all-gather.9
  124.7 39.8 all-gather.11
  166.6 59.7 all-gather.19
  228.4 39.1 all-gather.13
  269.7 59.6 all-gather.15
  331.6 59.1 all-gather.17
  898.5 68.5 reduce-scatter.13
  1982.9 92.2 reduce-scatter.11
  2078.5 73.5 reduce-scatter.9
  2155.7 68.1 reduce-scatter.7
  2227.3 116.9 reduce-scatter.17
  2347.9 117.0 reduce-scatter.15
  2468.5 117.0 reduce-scatter.19
  2589.4 46.4 all-reduce.9
where the time goes:
time: 2670 us; the launch traced here: 2650 us
  matrix products  819 us (31%)
  other arithmetic  701 us (26%)
  waiting for transfers between devices  623 us (23%)
  local copies, waits for them, and re-layouts  295 us (11%)
  blocking collectives  107 us (4%)
  starting transfers between devices  51.3 us (2%)
  loops' own time  37.4 us (1%)
    dot_general x12, matrix products, block_logits(): jnp.einsum('qhd,khd->hqk', query_block, key_rows, preferred_element_type=...  579 us
    reduce_sum x12, other arithmetic, one_block(): jnp.sum(jnp.where(buckets == label, d_logits, 0.0), axis=(1, 2))  320 us
    eq x12, other arithmetic, block_logits(): buckets == label  279 us
    reduce_scatter x1, waiting for transfers between devices, shards(): lax.psum_scatter(local_grads[6], 'fsdp', scatter_dimension=0, tiled=True)  119 us
    reduce_scatter x1, waiting for transfers between devices, shards(): lax.psum_scatter(local_grads[7], 'fsdp', scatter_dimension=0, tiled=True)  119 us
    reduce_scatter x1, waiting for transfers between devices, shards(): lax.psum_scatter(local_grads[8], 'fsdp', scatter_dimension=0, tiled=True)  119 us
    unnamed x2, blocking collectives  101 us
    reduce_scatter x1, waiting for transfers between devices, shards(): lax.psum_scatter(local_grads[2], 'fsdp', scatter_dimension=0, tiled=True)  75.3 us
  transfers between devices with their start and end apart: 25, of which 13 were waited for; matrix products, arithmetic and copies ran while one was open for 66% of the time, Pallas kernels for 0%

commit v1 on v0

v1 whole, which is shorter than its diff:
```python
import functools
import math

import jax
import jax.numpy as jnp
from jax import lax
from jax.experimental import pallas as pl
from jax.experimental.pallas import tpu as pltpu
from jax.sharding import PartitionSpec as P

bucket_edges = (1, 2, 3, 4, 5, 6, 7, 8, 12, 16, 23, 32, 46, 64, 91)
epsilon = 1e-06
longest = 1024
lanes = 128
block = 256
far = 768
reach = 1792
MESH = pl.DeviceIdType.MESH
f32 = jnp.float32
bf16 = jnp.bfloat16
vmem_limit = 60 * 2**20


def nn(left, right):
    return jnp.dot(left, right, preferred_element_type=f32)


def nt(left, right):
    return lax.dot_general(left, right, (((1,), (1,)), ((), ())), preferred_element_type=f32)


def tn(left, right):
    return lax.dot_general(left, right, (((0,), (0,)), ((), ())), preferred_element_type=f32)


def iota(shape, dim):
    return lax.broadcasted_iota(jnp.int32, shape, dim)


def one_hot(column, row):
    return jnp.where(column == row, 1.0, 0.0).astype(bf16)


def inverse_rms(values):
    return lax.rsqrt(jnp.mean(values * values, axis=-1, keepdims=True) + epsilon)


def bucket_index(offset):
    distance = jnp.abs(offset)
    bucket_sum = jnp.where(offset > 0, 16, 0).astype(jnp.int32)
    for border in bucket_edges:
        bucket_sum = bucket_sum + (distance >= border).astype(jnp.int32)
    return bucket_sum


def band_buckets():
    shape = (3 * lanes, lanes)
    return bucket_index(iota(shape, 0) - lanes - iota(shape, 1))


def whole_spec(shape, space=pltpu.VMEM):
    return pl.BlockSpec(shape, lambda *_: (0,) * len(shape), memory_space=space,
                        pipeline_mode=pl.Buffered(1))


def deal_kernel(fsdp_count, tok_ref, cot_ref, xa_ref, ca_ref, send, recv, pass_send, pass_recv, own):
    f = lax.axis_index("fsdp")
    s = lax.axis_index("sp")
    p, c = s // 2, s % 2
    mine = p * fsdp_count + f
    peers = 2 * fsdp_count
    barrier = pltpu.get_barrier_semaphore()

    def where(k):
        return {"fsdp": k % fsdp_count, "sp": (k // fsdp_count) * 2 + c}

    def greet(i, carry):
        k = lax.rem(mine + i, peers)
        pl.semaphore_signal(barrier, inc=1, device_id=where(k), device_id_type=MESH)
        return carry

    lax.fori_loop(1, peers, greet, 0)
    sibling = {"fsdp": f, "sp": 2 * p + 1 - c}
    pl.semaphore_signal(barrier, inc=1, device_id=sibling, device_id_type=MESH)
    pl.semaphore_wait(barrier, peers)

    def piece(which, src, dst, k):
        return pltpu.make_async_remote_copy(
            src_ref=src.at[k // fsdp_count, k % fsdp_count],
            dst_ref=dst.at[c, p, f],
            send_sem=send.at[which, k],
            recv_sem=recv.at[which, mine],
            device_id=where(k),
            device_id_type=MESH,
        )

    def arrived(which, src, dst, k):
        return pltpu.make_async_remote_copy(
            src_ref=src.at[k // fsdp_count, k % fsdp_count],
            dst_ref=dst.at[c, k // fsdp_count, k % fsdp_count],
            send_sem=send.at[which, k],
            recv_sem=recv.at[which, k],
            device_id=where(k),
            device_id_type=MESH,
        )

    def onward(which, dst, k, side):
        return pltpu.make_async_remote_copy(
            src_ref=dst.at[side, k // fsdp_count, k % fsdp_count],
            dst_ref=dst.at[side, k // fsdp_count, k % fsdp_count],
            send_sem=pass_send.at[which, k],
            recv_sem=pass_recv.at[which, k],
            device_id=sibling,
            device_id_type=MESH,
        )

    pairs = ((0, tok_ref, xa_ref), (1, cot_ref, ca_ref))
    for which, src, dst in pairs:

        def start(i, carry):
            piece(which, src, dst, lax.rem(mine + i, peers)).start()
            return carry

        lax.fori_loop(1, peers, start, 0)
    for which, src, dst in pairs:
        local = pltpu.make_async_copy(src.at[p, f], dst.at[c, p, f], own.at[which])
        local.start()
        local.wait()
        onward(which, dst, mine, c).start()

        def forward(i, carry):
            k = lax.rem(mine + peers - i, peers)
            arrived(which, src, dst, k).wait_recv()
            onward(which, dst, k, c).start()
            return carry

        lax.fori_loop(1, peers, forward, 0)
    for which, src, dst in pairs:

        def finish(k, carry):
            onward(which, dst, k, c).wait_send()
            onward(which, dst, k, 1 - c).wait_recv()
            return carry

        lax.fori_loop(0, peers, finish, 0)

        def sent(i, carry):
            piece(which, src, dst, lax.rem(mine + i, peers)).wait_send()
            return carry

        lax.fori_loop(1, peers, sent, 0)


def deal(tokens, cotangent, fsdp_count):
    micro, fsdp_count, piece, width = tokens.shape
    out = jax.ShapeDtypeStruct((2, 2, fsdp_count, piece, width), bf16)
    hbm = pl.BlockSpec(memory_space=pl.ANY)
    sem = pltpu.SemaphoreType.DMA((2, 2 * fsdp_count))
    return pl.pallas_call(
        functools.partial(deal_kernel, fsdp_count),
        out_shape=(out, out),
        in_specs=[hbm, hbm],
        out_specs=(hbm, hbm),
        scratch_shapes=[sem, sem, sem, sem, pltpu.SemaphoreType.DMA((2,))],
        compiler_params=pltpu.CompilerParams(collective_id=0, has_side_effects=True),
        name="deal",
    )(tokens, cotangent)


def home_kernel(fsdp_count, a_ref, b_ref, ra_ref, rb_ref, send, recv, own):
    f = lax.axis_index("fsdp")
    s = lax.axis_index("sp")
    p, c = s // 2, s % 2
    mine = p * fsdp_count + f
    peers = 2 * fsdp_count
    barrier = pltpu.get_barrier_semaphore()

    def where(k):
        return {"fsdp": k % fsdp_count, "sp": (k // fsdp_count) * 2 + c}

    def greet(i, carry):
        k = lax.rem(mine + i, peers)
        pl.semaphore_signal(barrier, inc=1, device_id=where(k), device_id_type=MESH)
        return carry

    lax.fori_loop(1, peers, greet, 0)
    pl.semaphore_wait(barrier, peers - 1)

    def piece(which, src, dst, k):
        return pltpu.make_async_remote_copy(
            src_ref=src.at[k // fsdp_count, k % fsdp_count],
            dst_ref=dst.at[p, f],
            send_sem=send.at[which, k],
            recv_sem=recv.at[which, mine],
            device_id=where(k),
            device_id_type=MESH,
        )

    def arrived(which, src, dst, k):
        return pltpu.make_async_remote_copy(
            src_ref=src.at[k // fsdp_count, k % fsdp_count],
            dst_ref=dst.at[k // fsdp_count, k % fsdp_count],
            send_sem=send.at[which, k],
            recv_sem=recv.at[which, k],
            device_id=where(k),
            device_id_type=MESH,
        )

    pairs = ((0, a_ref, ra_ref), (1, b_ref, rb_ref))
    for which, src, dst in pairs:

        def start(i, carry):
            piece(which, src, dst, lax.rem(mine + i, peers)).start()
            return carry

        lax.fori_loop(1, peers, start, 0)
        local = pltpu.make_async_copy(src.at[p, f], dst.at[p, f], own.at[which])
        local.start()
        local.wait()
    for which, src, dst in pairs:

        def finish(i, carry):
            k = lax.rem(mine + i, peers)
            arrived(which, src, dst, k).wait_recv()
            piece(which, src, dst, k).wait_send()
            return carry

        lax.fori_loop(1, peers, finish, 0)


def home(first, second):
    fsdp_count, piece, width = first.shape[1:]
    out = jax.ShapeDtypeStruct((2, fsdp_count, piece, width), bf16)
    hbm = pl.BlockSpec(memory_space=pl.ANY)
    sem = pltpu.SemaphoreType.DMA((2, 2 * fsdp_count))
    return pl.pallas_call(
        functools.partial(home_kernel, fsdp_count),
        out_shape=(out, out),
        in_specs=[hbm, hbm],
        out_specs=(hbm, hbm),
        scratch_shapes=[sem, sem, pltpu.SemaphoreType.DMA((2,))],
        compiler_params=pltpu.CompilerParams(collective_id=1, has_side_effects=True),
        name="home",
    )(first, second)


def build_diagonals(table_ref, band):
    left = jnp.broadcast_to(band[0:1, :], (lanes, lanes))
    right = jnp.broadcast_to(band[3 * lanes - 1 : 3 * lanes, :], (lanes, lanes))
    for half in range(2):
        cols = slice(half * lanes, (half + 1) * lanes)
        first = far - lanes + half * lanes
        for row in range(0, first, lanes):
            table_ref[row : row + lanes, cols] = left
        table_ref[first : first + 3 * lanes, cols] = band
        for row in range(first + 3 * lanes, reach, lanes):
            table_ref[row : row + lanes, cols] = right


def attend_kernel(
    bound_ref, idx_ref, x_ref, ct_ref, gain_ref, w_ref, band_ref,
    xs_ref, cs_ref, qkv_ref, pl_ref, ps_ref, ctx_ref, ctx32_ref, linv_ref,
    table, mask, km, vt, ctx_t, linv_t,
):
    rows_all, width = x_ref.shape
    pairs = pl.num_programs(0)
    part = pairs * lanes
    step = pl.program_id(0)
    short = rows_all - longest

    @pl.when(step == 0)
    def _():
        def tile(i, carry):
            rows = pl.ds(pl.multiple_of(i * block, block), block)
            chosen = one_hot(idx_ref[rows, :], iota((block, rows_all), 1))
            x = nn(chosen, x_ref[...])
            xs_ref[rows, :] = x.astype(bf16)
            normed = (x * inverse_rms(x) * gain_ref[...]).astype(bf16)
            for k in range(3):
                cols = slice(k * part, (k + 1) * part)
                qkv_ref[rows, cols] = nn(normed, w_ref[:, cols]).astype(bf16)
            cs_ref[rows, :] = nn(chosen, ct_ref[...]).astype(bf16)
            return carry

        lax.fori_loop(0, rows_all // block, tile, 0)
        bound = bound_ref[0]
        inside = (iota((short, short), 0) < bound) == (iota((short, short), 1) < bound)
        mask[...] = jnp.where(inside, 0.0, -1e30)

    def columns(kind):
        return pl.ds(pl.multiple_of(kind * part + step * lanes, lanes), lanes)

    keys = qkv_ref[:, columns(1)]
    vt[...] = jnp.transpose(qkv_ref[:, columns(2)].astype(f32)).astype(bf16)
    own = iota((rows_all, lanes), 1) < lanes // 2
    half = lanes // 2
    for h in range(2):
        build_diagonals(table, band_ref[h])
        km[...] = jnp.where(own == (h == 0), keys, jnp.zeros_like(keys))

        def strip(base, count, out_ref, masked, b, carry):
            here = pl.ds(pl.multiple_of(base + b * block, block), block)
            queries = qkv_ref[here, columns(0)]
            logits = nt(km[base : base + count, :], queries)
            first = pl.multiple_of(far - b * block, block)
            logits = logits + table[pl.ds(first, count), :]
            cols = pl.ds(pl.multiple_of(b * block, block), block)
            if masked:
                logits = logits + mask[:, cols]
            top = jnp.max(logits, axis=0, keepdims=True)
            weights = jnp.exp(logits - top)
            inv = 1.0 / jnp.sum(weights, axis=0, keepdims=True)
            low = weights.astype(bf16)
            spot = pl.ds(pl.multiple_of(h * count + b * block, block), block)
            out_ref[0, :, spot] = low
            part_rows = slice(h * half, (h + 1) * half)
            ctx_t[part_rows, here] = nn(vt[part_rows, base : base + count], low) * inv
            linv_t[part_rows, here] = jnp.broadcast_to(inv, (half, block))
            return carry

        lax.fori_loop(
            0, longest // block, functools.partial(strip, 0, longest, pl_ref, False), 0)
        lax.fori_loop(
            0, short // block, functools.partial(strip, longest, short, ps_ref, True), 0)
    context = jnp.transpose(ctx_t[...])
    ctx32_ref[...] = context
    ctx_ref[...] = context.astype(bf16)
    linv_ref[...] = jnp.transpose(linv_t[...])


def attend(bound, idx_col, arrived, cot_arrived, gain, w_qkv, band):
    rows, width = arrived.shape
    part = w_qkv.shape[1] // 3
    pairs = part // lanes
    short = rows - longest
    lane_block = pl.BlockSpec((rows, lanes), lambda i: (0, i))
    return pl.pallas_call(
        attend_kernel,
        grid=(pairs,),
        in_specs=[
            pl.BlockSpec(memory_space=pltpu.SMEM),
            whole_spec((rows, 1)),
            whole_spec((rows, width)),
            whole_spec((rows, width)),
            whole_spec((1, width)),
            whole_spec(w_qkv.shape),
            pl.BlockSpec((2, 3 * lanes, lanes), lambda i: (i, 0, 0)),
        ],
        out_specs=(
            whole_spec((rows, width)),
            whole_spec((rows, width)),
            whole_spec((rows, 3 * part)),
            pl.BlockSpec((1, longest, 2 * longest), lambda i: (i, 0, 0)),
            pl.BlockSpec((1, short, 2 * short), lambda i: (i, 0, 0)),
            lane_block, lane_block, lane_block,
        ),
        out_shape=(
            jax.ShapeDtypeStruct((rows, width), bf16),
            jax.ShapeDtypeStruct((rows, width), bf16),
            jax.ShapeDtypeStruct((rows, 3 * part), bf16),
            jax.ShapeDtypeStruct((pairs, longest, 2 * longest), bf16),
            jax.ShapeDtypeStruct((pairs, short, 2 * short), bf16),
            jax.ShapeDtypeStruct((rows, part), bf16),
            jax.ShapeDtypeStruct((rows, part), f32),
            jax.ShapeDtypeStruct((rows, part), f32),
        ),
        scratch_shapes=[
            pltpu.VMEM((reach, block), f32),
            pltpu.VMEM((short, short), f32),
            pltpu.VMEM((rows, lanes), bf16),
            pltpu.VMEM((lanes, rows), bf16),
            pltpu.VMEM((lanes, rows), f32),
            pltpu.VMEM((lanes, rows), f32),
        ],
        compiler_params=pltpu.CompilerParams(
            dimension_semantics=("arbitrary",), vmem_limit_bytes=vmem_limit),
        name="attend",
    )(bound, idx_col, arrived, cot_arrived, gain, w_qkv, band)


def feed_kernel(
    own_ref, sib_ref, xs_ref, cs_ref, wo_ref, gains_ref, wgu_ref, wd_ref,
    out_ref, ggu_ref, gd_ref, datt_ref, dctx_ref, go_own_ref, go_sib_ref, ggain_ref,
    mid, nff, hid, dgu, dn, dn_sib, send, recv,
):
    rows_all, width = xs_ref.shape
    ff = wd_ref.shape[0]
    part = width // 2
    lift = math.sqrt(2 / math.pi)
    tiles = rows_all // block
    s = lax.axis_index("sp")
    sibling = {"fsdp": lax.axis_index("fsdp"), "sp": (s // 2) * 2 + 1 - s % 2}
    gain = gains_ref[1:2, :]
    barrier = pltpu.get_barrier_semaphore()
    pl.semaphore_signal(barrier, inc=1, device_id=sibling, device_id_type=MESH)
    pl.semaphore_wait(barrier, 1)

    def exchange(i):
        rows = pl.ds(pl.multiple_of(i * block, block), block)
        return pltpu.make_async_remote_copy(
            src_ref=dn.at[rows, :], dst_ref=dn_sib.at[rows, :], send_sem=send.at[i],
            recv_sem=recv.at[i], device_id=sibling, device_id_type=MESH)

    def tile(i, carry):
        rows = pl.ds(pl.multiple_of(i * block, block), block)
        mixed = jnp.concatenate((own_ref[rows, :], sib_ref[rows, :]), axis=1)
        middle = xs_ref[rows, :].astype(f32) + nn(mixed, wo_ref[...])
        mid[rows, :] = middle
        normed = (middle * inverse_rms(middle) * gain).astype(bf16)
        nff[rows, :] = normed
        upstream = cs_ref[rows, :]
        gate = nn(normed, wgu_ref[:, :ff])
        up = nn(normed, wgu_ref[:, ff:])
        d_hidden = nt(upstream, wd_ref[...])
        square = gate * gate
        bent = jnp.tanh(lift * gate * (1.0 + 0.044715 * square))
        halved = 0.5 * (1.0 + bent)
        gelu = gate * halved
        slope = halved + 0.5 * gate * (1.0 - bent * bent) * (
            lift * (1.0 + 3 * 0.044715 * square))
        hidden = (gelu * up).astype(bf16)
        hid[rows, :] = hidden
        d_gate = (d_hidden * up * slope).astype(bf16)
        d_up = (d_hidden * gelu).astype(bf16)
        dgu[rows, :ff] = d_gate
        dgu[rows, ff:] = d_up
        dn[rows, :] = (nt(d_gate, wgu_ref[:, :ff]) + nt(d_up, wgu_ref[:, ff:])).astype(bf16)
        exchange(i).start()
        out_ref[rows, :] = (0.5 * middle + nn(hidden, wd_ref[...])).astype(bf16)
        return carry

    lax.fori_loop(0, tiles, tile, 0)

    def down(i, carry):
        cols = pl.ds(pl.multiple_of(i * block, block), block)
        gd_ref[cols, :] = tn(hid[:, cols], cs_ref[...]).astype(bf16)
        return carry

    lax.fori_loop(0, ff // block, down, 0)

    def settle(i, total):
        rows = pl.ds(pl.multiple_of(i * block, block), block)
        exchange(i).wait()
        mine = dn[rows, :].astype(f32)
        grad = mine + dn_sib[rows, :].astype(f32)
        middle = mid[rows, :]
        s = inverse_rms(middle)
        unit = middle * s
        scaled = gain * grad
        d_middle = cs_ref[rows, :].astype(f32) + s * (
            scaled - unit * jnp.mean(scaled * unit, axis=-1, keepdims=True))
        low = d_middle.astype(bf16)
        datt_ref[rows, :] = low
        dctx_ref[rows, :] = nt(low, wo_ref[0:part, :]).astype(bf16)
        return total + jnp.sum(mine * unit, axis=0, keepdims=True)

    ggain_ref[...] = lax.fori_loop(0, tiles, settle, jnp.zeros((1, width), f32))
    c = lax.axis_index("sp") % 2
    cols = pl.ds(pl.multiple_of(c * part, lanes), part)
    go_own_ref[...] = tn(own_ref[...], datt_ref[:, cols]).astype(bf16)
    go_sib_ref[...] = tn(sib_ref[...], datt_ref[:, cols]).astype(bf16)

    def gate_up(i, carry):
        cols = pl.ds(pl.multiple_of(i * block, block), block)
        ggu_ref[cols, :] = tn(nff[:, cols], dgu[...]).astype(bf16)
        return carry

    lax.fori_loop(0, width // block, gate_up, 0)


def feed(own, sib, xs, cs, w_out, gains, w_gu, w_down):
    rows, width = xs.shape
    ff = w_down.shape[0]
    part = width // 2
    vm = pl.BlockSpec(memory_space=pltpu.VMEM)
    return pl.pallas_call(
        feed_kernel,
        in_specs=[vm] * 8,
        out_specs=(vm,) * 8,
        out_shape=(
            jax.ShapeDtypeStruct((rows, width), bf16),
            jax.ShapeDtypeStruct((width, 2 * ff), bf16),
            jax.ShapeDtypeStruct((ff, width), bf16),
            jax.ShapeDtypeStruct((rows, width), bf16),
            jax.ShapeDtypeStruct((rows, part), bf16),
            jax.ShapeDtypeStruct((part, part), bf16),
            jax.ShapeDtypeStruct((part, part), bf16),
            jax.ShapeDtypeStruct((1, width), f32),
        ),
        scratch_shapes=[
            pltpu.VMEM((rows, width), f32),
            pltpu.VMEM((rows, width), bf16),
            pltpu.VMEM((rows, ff), bf16),
            pltpu.VMEM((rows, 2 * ff), bf16),
            pltpu.VMEM((rows, width), bf16),
            pltpu.VMEM((rows, width), bf16),
            pltpu.SemaphoreType.DMA((rows // block,)),
            pltpu.SemaphoreType.DMA((rows // block,)),
        ],
        compiler_params=pltpu.CompilerParams(
            vmem_limit_bytes=vmem_limit, collective_id=2, has_side_effects=True),
        name="feed",
    )(own, sib, xs, cs, w_out, gains, w_gu, w_down)


def back_kernel(
    xs_ref, gain_ref, w_ref, datt_ref, dctx_ref, qkv_ref, pl_ref, ps_ref, ctx32_ref, linv_ref,
    y_ref, gqkv_ref, ggain_ref, band_ref,
    normed, dqkv, table, dos, qs, ds_l, ds_s, va, kt, dq_t,
):
    rows_all, width = xs_ref.shape
    pairs = pl.num_programs(0)
    part = pairs * lanes
    step = pl.program_id(0)
    short = rows_all - longest
    half = lanes // 2
    gain_attn = gain_ref[0:1, :]

    def columns(kind):
        return pl.ds(pl.multiple_of(kind * part + step * lanes, lanes), lanes)

    lane = iota((rows_all, lanes), 1)
    queries = qkv_ref[:, columns(0)]
    keys = qkv_ref[:, columns(1)]
    values = qkv_ref[:, columns(2)]
    none = jnp.zeros_like(keys)
    kt[...] = jnp.transpose(keys.astype(f32)).astype(bf16)
    scaled = (dctx_ref[:, columns(0)].astype(f32) * linv_ref[...]).astype(bf16)
    against = scaled.astype(f32) * ctx32_ref[...]
    for h in range(2):
        mine = (lane < half) if h == 0 else (lane >= half)
        spare = half if h == 0 else 0
        delta = jnp.sum(jnp.where(mine, against, 0.0), axis=1, keepdims=True)
        high = delta.astype(bf16).astype(f32)
        rest = delta - high
        extra = jnp.where(lane == spare, -high, jnp.where(lane == spare + 1, -rest, 0.0))
        dos[h] = jnp.where(mine, scaled.astype(f32), extra).astype(bf16)
        qs[h] = jnp.where(mine, queries, none)
        ones = jnp.where((lane == spare) | (lane == spare + 1), 1.0, 0.0)
        va[...] = jnp.where(mine, values.astype(f32), ones).astype(bf16)
        table[...] = jnp.zeros_like(table)

        def strip(base, count, p_ref, ds_ref, b, carry):
            here = pl.ds(pl.multiple_of(base + b * block, block), block)
            spot = pl.ds(pl.multiple_of(h * count + b * block, block), block)
            d_weights = nt(va[base : base + count, :], dos[h, here, :])
            d_logits = p_ref[0, :, spot].astype(f32) * d_weights
            window = pl.ds(pl.multiple_of(far - b * block, block), count)
            table[window, :] = table[window, :] + d_logits
            low = d_logits.astype(bf16)
            ds_ref[:, spot] = low
            part_rows = slice(h * half, (h + 1) * half)
            dq_t[part_rows, here] = nn(kt[part_rows, base : base + count], low)
            return carry

        lax.fori_loop(
            0, longest // block, functools.partial(strip, 0, longest, pl_ref, ds_l), 0)
        lax.fori_loop(
            0, short // block, functools.partial(strip, longest, short, ps_ref, ds_s), 0)
        before = far - lanes
        after = far + 3 * lanes
        band = table[before : before + 3 * lanes, :lanes] + table[far : far + 3 * lanes, lanes:]
        left = jnp.sum(table[:before, :lanes] + table[:before, lanes:], axis=0, keepdims=True)
        left = left + jnp.sum(table[before:far, lanes:], axis=0, keepdims=True)
        right = jnp.sum(table[after:, :lanes] + table[after:, lanes:], axis=0, keepdims=True)
        right = right + jnp.sum(table[after - lanes : after, :lanes], axis=0, keepdims=True)
        row = iota((3 * lanes, lanes), 0)
        band = band + jnp.where(row == 0, left, 0.0) + jnp.where(row == 3 * lanes - 1, right, 0.0)
        band_ref[h] = band

    dqkv[:, columns(0)] = jnp.transpose(dq_t[...]).astype(bf16)
    own = iota((rows_all, lanes), 1) < half
    for base, count, p_ref, ds_ref in ((0, longest, pl_ref, ds_l), (longest, short, ps_ref, ds_s)):
        rows = slice(base, base + count)
        clean = [
            jnp.where(own[rows] == (h == 0), dos[h, rows, :].astype(f32), 0.0).astype(bf16)
            for h in range(2)
        ]
        dqkv[rows, columns(2)] = nn(p_ref[0], jnp.concatenate(clean, axis=0)).astype(bf16)
        both = jnp.concatenate((qs[0, rows, :], qs[1, rows, :]), axis=0)
        dqkv[rows, columns(1)] = nn(ds_ref[...], both).astype(bf16)

    @pl.when(step == pairs - 1)
    def _():
        def tile(i, total):
            rows = pl.ds(pl.multiple_of(i * block, block), block)
            x = xs_ref[rows, :].astype(f32)
            s = inverse_rms(x)
            unit = x * s
            grad = nt(dqkv[rows, :], w_ref[...])
            scaled = gain_attn * grad
            y = 0.5 * datt_ref[rows, :].astype(f32) + s * (
                scaled - unit * jnp.mean(scaled * unit, axis=-1, keepdims=True))
            y_ref[rows, :] = y.astype(bf16)
            normed[rows, :] = (unit * gain_attn).astype(bf16)
            return total + jnp.sum(grad * unit, axis=0, keepdims=True)

        zero = jnp.zeros((1, width), f32)
        ggain_ref[...] = lax.fori_loop(0, rows_all // block, tile, zero)

        def weight(i, carry):
            cols = pl.ds(pl.multiple_of(i * block, block), block)
            gqkv_ref[cols, :] = tn(normed[:, cols], dqkv[...]).astype(bf16)
            return carry

        lax.fori_loop(0, width // block, weight, 0)


def back(xs, gain, w_qkv, datt, dctx, qkv, p_long, p_short, ctx32, linv):
    rows, width = xs.shape
    part = w_qkv.shape[1] // 3
    pairs = part // lanes
    short = rows - longest
    lane_block = pl.BlockSpec((rows, lanes), lambda i: (0, i))
    return pl.pallas_call(
        back_kernel,
        grid=(pairs,),
        in_specs=[
            *(whole_spec(a.shape) for a in (xs, gain, w_qkv, datt, dctx, qkv)),
            pl.BlockSpec((1, longest, 2 * longest), lambda i: (i, 0, 0)),
            pl.BlockSpec((1, short, 2 * short), lambda i: (i, 0, 0)),
            lane_block, lane_block,
        ],
        out_specs=(
            whole_spec((rows, width)),
            whole_spec((width, 3 * part)),
            whole_spec((1, width)),
            pl.BlockSpec((2, 3 * lanes, lanes), lambda i: (i, 0, 0)),
        ),
        out_shape=(
            jax.ShapeDtypeStruct((rows, width), bf16),
            jax.ShapeDtypeStruct((width, 3 * part), bf16),
            jax.ShapeDtypeStruct((1, width), f32),
            jax.ShapeDtypeStruct((2 * pairs, 3 * lanes, lanes), f32),
        ),
        scratch_shapes=[
            pltpu.VMEM((rows, width), bf16),
            pltpu.VMEM((rows, 3 * part), bf16),
            pltpu.VMEM((reach, block), f32),
            pltpu.VMEM((2, rows, lanes), bf16),
            pltpu.VMEM((2, rows, lanes), bf16),
            pltpu.VMEM((longest, 2 * longest), bf16),
            pltpu.VMEM((short, 2 * short), bf16),
            pltpu.VMEM((rows, lanes), bf16),
            pltpu.VMEM((lanes, rows), bf16),
            pltpu.VMEM((lanes, rows), f32),
        ],
        compiler_params=pltpu.CompilerParams(
            dimension_semantics=("arbitrary",), vmem_limit_bytes=vmem_limit),
        name="back",
    )(xs, gain, w_qkv, datt, dctx, qkv, p_long, p_short, ctx32, linv)


def unslot_kernel(idx_ref, a_ref, b_ref, oa_ref, ob_ref):
    rows_all = a_ref.shape[0]

    def tile(i, carry):
        rows = pl.ds(pl.multiple_of(i * block, block), block)
        chosen = one_hot(iota((block, rows_all), 0) + i * block, idx_ref[...])
        oa_ref[rows, :] = nn(chosen, a_ref[...]).astype(bf16)
        ob_ref[rows, :] = nn(chosen, b_ref[...]).astype(bf16)
        return carry

    lax.fori_loop(0, rows_all // block, tile, 0)


def unslot(idx_row, first, second):
    vm = pl.BlockSpec(memory_space=pltpu.VMEM)
    out = jax.ShapeDtypeStruct(first.shape, bf16)
    return pl.pallas_call(
        unslot_kernel,
        in_specs=[vm] * 3,
        out_specs=(vm, vm),
        out_shape=(out, out),
        compiler_params=pltpu.CompilerParams(vmem_limit_bytes=vmem_limit),
        name="unslot",
    )(idx_row, first, second)


def shards(
    tokens, cotangent, lengths, dealing, gain_attn, w_query, w_key, w_value, w_out, bias_table,
    gain_ff, w_gate, w_up, w_down,
):
    fsdp_count = lax.axis_size("fsdp")
    sp_count = lax.axis_size("sp")
    micro_count, token_rows, width = tokens.shape
    piece = token_rows // fsdp_count
    group_rows = token_rows * sp_count
    local_heads = bias_table.shape[1]
    heads = local_heads * sp_count
    part = width // 2
    s = lax.axis_index("sp")
    p, c = s // 2, s % 2
    sibling = [(0, 1), (1, 0), (2, 3), (3, 2)]
    across = [(0, 2), (2, 0), (1, 3), (3, 1)]

    def swap(value):
        return lax.ppermute(value, "sp", sibling)

    shape = (micro_count, fsdp_count, piece, width)
    xa, ca = deal(tokens.reshape(shape), cotangent.reshape(shape), fsdp_count)
    xa = xa.reshape(group_rows, width)
    ca = ca.reshape(group_rows, width)

    order = lax.dynamic_index_in_dim(dealing[:, 0], p, 0, keepdims=False)
    length = lax.dynamic_index_in_dim(lengths[:, 0], p, 0, keepdims=False)
    first_long = length[0] == longest
    start = jnp.where(first_long, 0, jnp.where(length[1] == longest, length[0],
                                               length[0] + length[1]))
    bound = jnp.where(first_long, length[1], length[0]).reshape(1)
    short = group_rows - longest
    head_part = lax.dynamic_slice_in_dim(order, start, longest, 0)
    tail = jnp.where(jnp.arange(short) < start, order[:short], order[longest:])
    order = jnp.concatenate((head_part, tail))
    source = order // token_rows
    idx = (source % 2) * (group_rows // 2) + (source // 2) * token_rows + order % token_rows

    def half_cols(weight):
        return lax.dynamic_slice_in_dim(weight, c * part, part, 1)

    def half_ff(weight):
        split = weight.reshape(weight.shape[0], fsdp_count, 2, -1)
        return lax.dynamic_index_in_dim(split, c, 2, keepdims=False).reshape(weight.shape[0], -1)

    def gather(value, axis=0):
        return lax.all_gather(value, "fsdp", axis=axis, tiled=True)

    gains = gather(jnp.stack((gain_attn, gain_ff)), 1).astype(f32)
    table = lax.all_gather(bias_table, "sp", axis=1, tiled=True).astype(f32)
    table = lax.dynamic_slice_in_dim(table, c * (heads // 2), heads // 2, 1)
    w_qkv = gather(jnp.concatenate([half_cols(w) for w in (w_query, w_key, w_value)], axis=1))
    down_rows = w_down.shape[0] // 2
    wd_half = lax.dynamic_slice_in_dim(w_down, c * down_rows, down_rows, 0)
    model_rows = w_out.shape[0]
    rest = gather(jnp.concatenate(
        [half_ff(w_gate), half_ff(w_up), w_out, wd_half.reshape(model_rows, -1)], axis=1))
    ff_wide = w_gate.shape[1] // 2
    w_gu = rest[:, : 2 * ff_wide]
    wo = rest[:, 2 * ff_wide : 2 * ff_wide + width]
    wo = jnp.where(c == 0, wo, jnp.concatenate((wo[part:], wo[:part])))
    wd = rest[:, 2 * ff_wide + width :].reshape(-1, width)

    buckets = band_buckets()
    band = jnp.zeros((heads // 2, *buckets.shape), f32)
    for label in range(table.shape[0]):
        band = band + jnp.where(buckets[None] == label, table[label][:, None, None], 0.0)

    xs, cs, qkv, p_long, p_short, ctx, ctx32, linv = attend(
        bound, idx.reshape(-1, 1), xa, ca, gains[0:1], w_qkv, band)
    ctx_sib = swap(ctx)
    out_part, grad_gu, grad_d, datt, dctx, go_own, go_sib, grad_gain_ff = feed(
        ctx, ctx_sib, xs, cs, wo, gains, w_gu, wd)
    grad_o = jnp.where(c == 0, jnp.concatenate((go_own, go_sib)),
                       jnp.concatenate((go_sib, go_own)))
    y, grad_qkv, grad_gain_attn, grad_band = back(
        xs, gains[0:1], w_qkv, datt, dctx, qkv, p_long, p_short, ctx32, linv)
    grad_gain = jnp.concatenate((grad_gain_attn, grad_gain_ff))
    back_rows = unslot(idx.reshape(1, -1), out_part, y)
    mine = group_rows // 2

    def join(value):
        kept = lax.dynamic_slice_in_dim(value, c * mine, mine, 0)
        given = lax.dynamic_slice_in_dim(value, (1 - c) * mine, mine, 0)
        return (kept.astype(f32) + swap(given).astype(f32)).astype(bf16).reshape(shape)

    output, grad_tokens = home(join(back_rows[0]), join(back_rows[1]))

    def packed(values, unit):
        cut = [v.reshape(fsdp_count, v.shape[0] // fsdp_count, -1, unit) for v in values]
        cut = [jnp.swapaxes(v, 1, 2).reshape(fsdp_count, -1, unit) for v in cut]
        return jnp.concatenate(cut, axis=1)

    def scatter(values, unit):
        whole = packed(values, unit)
        share = lax.psum_scatter(whole, "fsdp", scatter_dimension=0, tiled=True)[0]
        out, at = [], 0
        for v in values:
            rows, count = v.shape[0] // fsdp_count, v.shape[1] // unit
            one = share[at : at + rows * count].reshape(count, rows, unit)
            out.append(jnp.swapaxes(one, 0, 1).reshape(rows, -1))
            at += rows * count
        return out

    shares = scatter((grad_gu, grad_d), 256) + scatter((grad_qkv, grad_o), 384)
    flat = jnp.concatenate([v.reshape(-1) for v in shares])
    flat = (flat.astype(f32) + lax.ppermute(flat, "sp", across).astype(f32)).astype(bf16)
    flat_sib = swap(flat)
    low = jnp.where(c == 0, flat, flat_sib).astype(f32)
    high = jnp.where(c == 0, flat_sib, flat).astype(f32)
    pieces = []
    at = 0
    for v in shares:
        pieces.append([x[at : at + v.size].reshape(v.shape) for x in (low, high)])
        at += v.size
    gu, gd, gqkv, go = pieces
    ff = gu[0].shape[1] // 2

    def ff_cols(which):
        sides = [x[:, which * ff : (which + 1) * ff].reshape(x.shape[0], fsdp_count, 1, -1)
                 for x in gu]
        return jnp.concatenate(sides, axis=2).reshape(gu[0].shape[0], -1)

    def proj(which):
        return jnp.concatenate([x[:, which * part : (which + 1) * part] for x in gqkv], axis=1)

    sums = jnp.stack([
        jnp.sum(jnp.where(buckets[None] == label, grad_band, 0.0), axis=(1, 2))
        for label in range(table.shape[0])
    ])
    spread = jnp.zeros((table.shape[0], heads), f32)
    spread = lax.dynamic_update_slice(spread, sums, (0, c * (heads // 2)))
    small = lax.psum(jnp.concatenate((grad_gain.reshape(-1), spread.reshape(-1))), ("fsdp", "sp"))
    own_gain = width // fsdp_count
    f = lax.axis_index("fsdp")
    gains_grad = lax.dynamic_slice_in_dim(small[: 2 * width].reshape(2, width), f * own_gain,
                                          own_gain, 1)
    bias_grad = lax.dynamic_slice_in_dim(small[2 * width :].reshape(-1, heads), s * local_heads,
                                         local_heads, 1)
    return (
        output.reshape(tokens.shape), grad_tokens.reshape(tokens.shape), gains_grad[0],
        proj(0), proj(1), proj(2), jnp.concatenate(go, axis=1), bias_grad, gains_grad[1],
        ff_cols(0), ff_cols(1), jnp.concatenate(gd, axis=0),
    )


def solution(mesh):
    return jax.shard_map(
        shards,
        mesh=mesh,
        in_specs=(
            P(None, ("fsdp", "sp"), None), P(None, ("fsdp", "sp"), None),
            P(None, "fsdp", None), P(None, "fsdp", None),
            P("fsdp"), P("fsdp", None), P("fsdp", None), P("fsdp", None), P("fsdp", None),
            P(None, "sp"), P("fsdp"), P("fsdp", None), P("fsdp", None), P("fsdp", None),
        ),
        out_specs=(
            P(None, ("fsdp", "sp"), None), P(None, ("fsdp", "sp"), None),
            P("fsdp"), P("fsdp", None), P("fsdp", None), P("fsdp", None), P("fsdp", None),
            P(None, "sp"), P("fsdp"), P("fsdp", None), P("fsdp", None), P("fsdp", None),
        ),
        check_vma=False,
    )
```

time: 2670 us -> 639 us (0.24)
  matrix products: 819 us -> 0 us
  other arithmetic: 701 us -> 35.8 us
  waiting for transfers between devices: 623 us -> 137 us
  Pallas kernels: 0 us -> 311 us
  local copies, waits for them, and re-layouts: 295 us -> 60.5 us
  starting transfers between devices: 51.3 us -> 1.74 us
  blocking collectives: 107 us -> 68.8 us
  loops' own time: 37.4 us -> 0 us
    dot_general x84 -> x0, matrix products: 819 us -> none  [the longest x12 579 us: block_logits(): jnp.einsum('qhd,khd->hqk', query_block, key_rows, preferred_element_type=...]
    reduce_scatter x7 -> x2, waiting for transfers between devices: 541 us -> 137 us  [scatter(): share = lax.psum_scatter(whole, 'fsdp', scatter_dimension=0, tiled=True)[0]]
    reduce_sum x21 -> x2, other arithmetic: 354 us -> 6.47 us  [shards(): jnp.sum(jnp.where(buckets[None] == label, grad_band, 0.0), axis=(1, 2))]
    pallas_call x0 -> x6, Pallas kernels: none -> 311 us  [the longest x1 92.6 us: deal(): pl.pallas_call(functools.partial(deal_kernel, fsdp_count), out_shape=(out...]
    eq x24 -> x1, other arithmetic: 302 us -> 1.44 us  [shards(): buckets[None] == label]
    unnamed x2 -> x0, blocking collectives: 101 us -> none
    gather x8 -> x0, local copies, waits for them, and re-layouts: 71.8 us -> none  [the longest x2 25.7 us: shards(): slotted = head_rows[:, slot_order]]
    all_to_all x10 -> x0, starting transfers between devices: 50.3 us -> none  [the longest x2 11.6 us: shards(): lax.all_to_all(d_mixed, 'sp', split_axis=1, concat_axis=0, tiled=True)]
  transfers between devices with their start and end apart: 25 -> 9, of which waited for: 13 -> 2; matrix products, arithmetic and copies ran while one was open for 66% -> 9% of each run, Pallas kernels for 0% -> 34%
where the time goes in v1:
time: 639 us; the launch traced here: 634 us
  Pallas kernels  311 us (49%)
  waiting for transfers between devices  137 us (21%)
  blocking collectives  68.8 us (11%)
  local copies, waits for them, and re-layouts  60.5 us (9%)
  other arithmetic  35.8 us (6%)
  between operations  20.3 us (3%)
    reduce_scatter x2, waiting for transfers between devices, scatter(): share = lax.psum_scatter(whole, 'fsdp', scatter_dimension=0, tiled=True)[0]  137 us
    pallas_call x1, Pallas kernels, deal(): pl.pallas_call(functools.partial(deal_kernel, fsdp_count), out_shape=(out...  92.6 us
    pallas_call x1, Pallas kernels, home(): pl.pallas_call(functools.partial(home_kernel, fsdp_count), out_shape=(out...  57.2 us
    pallas_call x1, Pallas kernels, attend(): pl.pallas_call(attend_kernel, grid=(pairs,), in_specs=[pl.BlockSpec(memor...  51.9 us
    pallas_call x1, Pallas kernels, back(): pl.pallas_call(back_kernel, grid=(pairs,), in_specs=[*(whole_spec(a.shape...  49.5 us
    psum x1, blocking collectives, shards(): lax.psum(jnp.concatenate((grad_gain.reshape(-1), spread.reshape(-1))), ('...  49.2 us
    pallas_call x1, Pallas kernels, feed(): pl.pallas_call(feed_kernel, in_specs=[vm] * 8, out_specs=(vm,) * 8, out_s...  46.9 us
    all_gather x1, blocking collectives, gather(): return lax.all_gather(value, 'fsdp', axis=axis, tiled=True)  14.2 us
  transfers between devices with their start and end apart: 9, of which 2 were waited for; matrix products, arithmetic and copies ran while one was open for 9% of the time, Pallas kernels for 34%

profile of v1, /device:TPU:14, one launch (start us, length us, event | category | flops | bytes accessed | tf_op | source)
XLA Modules:
  0.0 634.5 jit_solution(11746353335977328461)
XLA Ops:
  10.8 2.3 dynamic-slice_reduce_fusion
  20.5 14.2 %all-gather = bf16[8,96,2]{1,2,0:T(2,128)(2,1)S(1)} all-gather(bf16[1,96,2]{1,2,0:T(2,128)(2,1)S(1)} %maximum_bitcast_fusion), channel_id=1, replica_groups=mesh['fsdp'=8,'sp'=4] {'fsdp'}, dimensions={0}, use_global_device_ids=true | all-gather | bytes 3456 | tf_op jit(solution)/shard_map/all_gather | solution.py:726
  35.4 5.3 all-gather.1
  40.8 92.6 %deal.1 = (bf16[2,2,8,48,768]{4,3,2,1,0:T(8,128)(2,1)}, bf16[2,2,8,48,768]{4,3,2,1,0:T(8,128)(2,1)}) custom-call(bf16[2,8,48,768]{3,2,1,0:T(8,128)(2,1)} %bitcast.127, bf16[2,8,48,768]{3,2,1,0:T(8,128)(2,1)} %bitcast.128), custom_call_target="tpu_custom_call" | custom-call | tf_op jit(solution)/shard_map/deal/pallas_call | solution.py:159
  134.3 1.4 broadcast_compare_fusion.31
  136.1 2.3 fusion.2.idx_ref
  138.7 5.2 select_add_fusion.band_ref
  143.8 51.9 %attend.1 = (bf16[1536,768]{1,0:T(8,128)(2,1)}, bf16[1536,768]{1,0:T(8,128)(2,1)}, bf16[1536,1152]{1,0:T(8,128)(2,1)}, bf16[3,1024,2048]{2,1,0:T(8,128)(2,1)}, b...) custom-call(s32[1]{0:T(128)} %bitcast.6.bound_ref, ...), custom_call_target="tpu_custom_call" | custom-call | tf_op jit(solution)/shard_map/attend/pallas_call | solution.py:337
  196.1 1.4 slice-done
  197.5 2.1 reshape.1133.wd_ref
  199.6 4.2 slice.394.wgu_ref
  203.9 1.3 slice_select_fusion.wo_ref
  206.3 46.9 %feed.1 = (bf16[1536,768]{1,0:T(8,128)(2,1)}, bf16[768,2048]{1,0:T(8,128)(2,1)}, bf16[1024,768]{1,0:T(8,128)(2,1)}, bf16[1536,768]{1,0:T(8,128)(2,1)}, bf16[1536...) custom-call(bf16[1536,384]{1,0:T(8,128)(2,1)} %get-tuple-element.40.own_ref, ...), custom_call_target="tpu_custom_call" | custom-call | tf_op jit(solution)/shard_map/feed/pallas_call | solution.py:476
  253.2 49.5 %back.1 = (bf16[1536,768]{1,0:T(8,128)(2,1)}, bf16[768,1152]{1,0:T(8,128)(2,1)}, f32[1,768]{1,0:T(1,128)}, f32[6,384,128]{2,1,0:T(8,128)}) custom-call(bf16[1536,768]{1,0:T(8,128)(2,1)} %get-tuple-element.41.xs_ref, f32[1,768]{1,0:T(1,128)} %slice.390.gain_ref, bf16[768,1152]{1,0:T(8,128)(2,1)} %all-gather.5.cloned.1.call-done.w_ref, ...), custom_call_target="tpu_custom_call" | custom-call | tf_op jit(solution)/shard_map/back/pallas_call | solution.py:615
  302.7 3.9 copy.141
  306.6 4.0 reshape.1147
  310.6 2.6 copy.142
  313.5 3.1 pad_maximum_fusion.1
  320.6 3.0 copy.151
  324.4 2.4 pad_maximum_fusion
  327.6 12.5 %unslot.1 = (bf16[1536,768]{1,0:T(8,128)(2,1)}, bf16[1536,768]{1,0:T(8,128)(2,1)}) custom-call(s32[1,1536]{1,0:T(1,128)} %fusion.27.idx_ref, bf16[1536,768]{1,0:T(8,128)(2,1)} %get-tuple-element.43.a_ref, bf16[1536,768]{1,0:T(8,128)(2,1)} %get-tuple-element.51.b_ref), custom_call_target="tpu_custom_call" | custom-call | tf_op jit(solution)/shard_map/unslot/pallas_call | solution.py:670
  340.1 2.5 constant_dynamic-slice_fusion.4
  344.8 2.7 select_reduce_fusion.18
  347.5 39.2 %reduce-scatter.5.cloned.1.call-done = bf16[1,384,384]{2,1,0:T(8,128)(2,1)} async-done(((bf16[8,384,384]{2,1,0:T(8,128)(2,1)}), bf16[1,384,384]{2,1,0:T(8,128)(2,1)}) %reduce-scatter.5.cloned.1.call-update) | async-done | bytes 294928 | tf_op jit(solution)/shard_map/reduce_scatter | solution.py:775
  388.1 97.6 %reduce-scatter.3.cloned.1.call-done = bf16[1,1152,256]{2,1,0:T(8,128)(2,1)} async-done(((bf16[8,1152,256]{2,1,0:T(8,128)(2,1)}), bf16[1,1152,256]{2,1,0:T(8,128)(2,1)}) %reduce-scatter.3.cloned.1.call-update) | async-done | bytes 589840 | tf_op jit(solution)/shard_map/reduce_scatter | solution.py:775
  489.0 3.8 select_reduce_fusion
  493.4 49.2 %psum.7 = f32[1920]{0:T(1024)S(1)} all-reduce(f32[1920]{0:T(1024)S(1)} %pad_maximum_fusion.11), channel_id=1, replica_groups=mesh['fsdp'=8,'sp'=4] {'fsdp','sp'}, use_global_device_ids=true, to_apply=%region_32.33 | all-reduce | flops 1920 | bytes 15360 | tf_op jit(solution)/shard_map/psum | solution.py:812
  545.2 2.6 add_convert_fusion.1
  547.8 2.6 add_convert_fusion
  550.4 57.2 %home.1 = (bf16[2,8,48,768]{3,2,1,0:T(8,128)(2,1)}, bf16[2,8,48,768]{3,2,1,0:T(8,128)(2,1)}) custom-call(bf16[2,8,48,768]{3,2,1,0:T(8,128)(2,1)} %bitcast.118, bf16[2,8,48,768]{3,2,1,0:T(8,128)(2,1)} %bitcast.119), custom_call_target="tpu_custom_call" | custom-call | tf_op jit(solution)/shard_map/home/pallas_call | solution.py:236
  615.4 1.5 reshape.1153
  618.6 1.5 reshape.1156
  (313 shorter events, 41.4 us)
Async XLA Ops:
  7.2 2.8 copy-start
  7.2 3.0 copy-start.72
  7.2 136.6 %all-gather.5.cloned.1.call-start = ((), (), s32[]{:S(2)}) async-start(), calls=%async_computation.2 | async-start | bytes 1990656 | tf_op jit(solution)/shard_map/all_gather | solution.py:726
  9.9 186.2 %all-gather.7.cloned.1.call-start = ((), (), s32[]{:S(2)}) async-start(), calls=%async_computation.3 | async-start | bytes 6635520 | tf_op jit(solution)/shard_map/all_gather | solution.py:726
  13.2 6.2 copy-start.78
  14.2 372.5 %reduce-scatter.5.cloned.1.call-start = ((), (), s32[]{:S(2)}) async-start(), calls=%async_computation.5 | async-start | bytes 2654208 | tf_op jit(solution)/shard_map/reduce_scatter | solution.py:775
  19.6 15.8 %copy-start.91 = (bf16[32,3]{0,1:T(4,128)(2,1)S(1)}, bf16[32,3]{0,1:T(4,128)(2,1)}, u32[]{:S(2)}) copy-start(bf16[32,3]{0,1:T(4,128)(2,1)} %param.23) | copy-start | bytes 580
  34.8 98.5 %copy-start.77 = (f32[768,2]{0,1:T(2,128)}, f32[768,2]{0,1:T(2,128)S(1)}, u32[]{:S(2)}) copy-start(f32[768,2]{0,1:T(2,128)S(1)} %reshape.1161) | copy-start | bytes 18436
  195.7 9.6 %collective-permute-start = (bf16[1536,384]{1,0:T(8,128)(2,1)}, bf16[1536,384]{1,0:T(8,128)(2,1)S(1)}, u32[]{:S(2)}, u32[]{:S(2)}) collective-permute-start(bf16[1536,384]{1,0:T(8,128)(2,1)} %get-tuple-element.40.own_ref), channel_id=1, source_target_pairs={{0,1},{1,0},{2,3},{3,2},{4,5},{5,4},{6,7},{7,6},{8,9},{9,8},{10,11... | collective-permute-start | bytes 3538952 | tf_op jit(solution)/shard_map/ppermute | solution.py:698
  199.6 4.2 copy-start.2
  316.6 169.0 %reduce-scatter.3.cloned.1.call-start = ((), (), s32[]{:S(2)}) async-start(), calls=%async_computation.4 | async-start | bytes 5308416 | tf_op jit(solution)/shard_map/reduce_scatter | solution.py:775
  340.1 2.9 copy-start.4
  342.6 201.8 %collective-permute-start.1 = (bf16[768,768]{1,0:T(8,128)(2,1)}, bf16[768,768]{1,0:T(8,128)(2,1)}, u32[]{:S(2)}, u32[]{:S(2)}) collective-permute-start(bf16[768,768]{1,0:T(8,128)(2,1)} %constant_dynamic-slice_fusion.4), channel_id=1, source_target_pairs={{0,1},{1,0},{2,3},{3,2},{4,5},{5,4},{6,7},{7,6},{8,9},{9,8},{10,11... | collective-permute-start | bytes 3538952 | tf_op jit(solution)/shard_map/ppermute | solution.py:698
  344.2 203.6 %collective-permute-start.2 = (bf16[768,768]{1,0:T(8,128)(2,1)}, bf16[768,768]{1,0:T(8,128)(2,1)}, u32[]{:S(2)}, u32[]{:S(2)}) collective-permute-start(bf16[768,768]{1,0:T(8,128)(2,1)} %constant_dynamic-slice_fusion.3), channel_id=1, source_target_pairs={{0,1},{1,0},{2,3},{3,2},{4,5},{5,4},{6,7},{7,6},{8,9},{9,8},{10,11... | collective-permute-start | bytes 3538952 | tf_op jit(solution)/shard_map/ppermute | solution.py:698
  488.2 4.6 copy-start.81
  488.2 4.6 copy-start.82
  488.3 4.6 copy-start.83
  488.3 4.6 copy-start.84
  488.3 4.6 copy-start.85
  488.3 4.6 copy-start.86
  488.3 4.6 copy-start.87
  488.3 4.6 copy-start.88
  488.3 4.6 copy-start.89
  488.3 4.5 copy-start.90
  488.4 5.0 copy-start.79
  488.4 5.0 copy-start.80
  488.4 55.1 %collective-permute-start.3 = (bf16[442368]{0:T(1024)(128)(2,1)S(1)}, bf16[442368]{0:T(1024)(128)(2,1)S(1)}, u32[]{:S(2)}, u32[]{:S(2)}) collective-permute-start(bf16[442368]{0:T(1024)(128)(2,1)S(1)} %constant_dynamic-update-slice_fusion), channel_id=1, source_target_pairs={{0,2},{2,0},{1,3},{3,1},{4,6},{6,4},{5,7},{7,5},{8,10},{10,8},{9,1... | collective-permute-start | bytes 2654216 | tf_op jit(solution)/shard_map/ppermute | solution.py:786
  543.7 63.9 %collective-permute-start.4 = (bf16[442368]{0:T(1024)(128)(2,1)S(1)}, bf16[442368]{0:T(1024)(128)(2,1)S(1)}, u32[]{:S(2)}, u32[]{:S(2)}) collective-permute-start(bf16[442368]{0:T(1024)(128)(2,1)S(1)} %add_convert_fusion.2), channel_id=1, source_target_pairs={{0,1},{1,0},{2,3},{3,2},{4,5},{5,4},{6,7},{7,6},{8,9},{9,8},{10,11... | collective-permute-start | bytes 2654216 | tf_op jit(solution)/shard_map/ppermute | solution.py:698
  544.4 3.4 copy-start.5
  620.2 3.1 copy-start.18
  620.2 3.1 copy-start.19
  625.0 2.7 copy-start.1
  (75 other events, 150.8 us)
Sparse Core Ops, SparseCore 0:
  10.8 50.9 all-gather.4
  64.5 118.5 all-gather.6
  316.8 69.8 reduce-scatter.4
  390.2 95.4 reduce-scatter.2

commit v2 on v1

v2 whole, which is shorter than its diff:
```python
import functools
import math

import jax
import jax.numpy as jnp
from jax import lax
from jax.experimental import pallas as pl
from jax.experimental.pallas import tpu as pltpu
from jax.sharding import PartitionSpec as P

bucket_edges = (1, 2, 3, 4, 5, 6, 7, 8, 12, 16, 23, 32, 46, 64, 91)
epsilon = 1e-06
longest = 1024
lanes = 128
block = 256
far = 768
reach = 1792
MESH = pl.DeviceIdType.MESH
f32 = jnp.float32
bf16 = jnp.bfloat16
vmem_limit = 60 * 2**20


def nn(left, right):
    return jnp.dot(left, right, preferred_element_type=f32)


def nt(left, right):
    return lax.dot_general(left, right, (((1,), (1,)), ((), ())), preferred_element_type=f32)


def tn(left, right):
    return lax.dot_general(left, right, (((0,), (0,)), ((), ())), preferred_element_type=f32)


def iota(shape, dim):
    return lax.broadcasted_iota(jnp.int32, shape, dim)


def one_hot(column, row):
    return jnp.where(column == row, 1.0, 0.0).astype(bf16)


def inverse_rms(values):
    return lax.rsqrt(jnp.mean(values * values, axis=-1, keepdims=True) + epsilon)


def bucket_index(offset):
    distance = jnp.abs(offset)
    bucket_sum = jnp.where(offset > 0, 16, 0).astype(jnp.int32)
    for border in bucket_edges:
        bucket_sum = bucket_sum + (distance >= border).astype(jnp.int32)
    return bucket_sum


def band_buckets():
    shape = (3 * lanes, lanes)
    return bucket_index(iota(shape, 0) - lanes - iota(shape, 1))


def whole_spec(shape, space=pltpu.VMEM):
    return pl.BlockSpec(shape, lambda *_: (0,) * len(shape), memory_space=space,
                        pipeline_mode=pl.Buffered(1))


def place():
    f = lax.axis_index("fsdp")
    s = lax.axis_index("sp")
    return f, s // 2, s % 2


def device(f, p, c):
    return {"fsdp": f, "sp": 2 * p + c}


def signal(barrier, where):
    pl.semaphore_signal(barrier, inc=1, device_id=where, device_id_type=MESH)


def greet_all(fsdp_count):
    f, p, c = place()
    barrier = pltpu.get_barrier_semaphore()
    peers = 2 * fsdp_count
    mine = p * fsdp_count + f

    def greet(i, carry):
        k = lax.rem(mine + i, peers)
        signal(barrier, device(k % fsdp_count, k // fsdp_count, c))
        return carry

    lax.fori_loop(1, peers, greet, 0)
    signal(barrier, device(f, p, 1 - c))
    pl.semaphore_wait(barrier, peers)


def push(src, dst, send, recv, where):
    return pltpu.make_async_remote_copy(
        src_ref=src, dst_ref=dst, send_sem=send, recv_sem=recv, device_id=where,
        device_id_type=MESH)


def looped(first, last, body):
    def step(i, carry):
        body(i)
        return carry

    lax.fori_loop(first, last, step, 0)


class Dealing:
    def __init__(self, fsdp_count, src, dst, send, recv, pass_send, pass_recv, own):
        self.f, self.p, self.c = place()
        self.count = fsdp_count
        self.peers = 2 * fsdp_count
        self.mine = self.p * fsdp_count + self.f
        self.src, self.dst, self.send, self.recv = src, dst, send, recv
        self.pass_send, self.pass_recv, self.own = pass_send, pass_recv, own

    def source(self, k):
        return self.src.at[k // self.count, k % self.count] if len(self.src.shape) == 4 else self.src

    def out(self, k):
        where = device(k % self.count, k // self.count, self.c)
        return push(self.source(k), self.dst.at[self.c, self.p, self.f], self.send.at[k],
                    self.recv.at[self.mine], where)

    def come(self, k):
        where = device(k % self.count, k // self.count, self.c)
        return push(self.source(k), self.dst.at[self.c, k // self.count, k % self.count],
                    self.send.at[k], self.recv.at[k], where)

    def onward(self, k, side):
        here = self.dst.at[side, k // self.count, k % self.count]
        return push(here, here, self.pass_send.at[k], self.pass_recv.at[k],
                    device(self.f, self.p, 1 - self.c))

    def local(self):
        return pltpu.make_async_copy(
            self.source(self.mine), self.dst.at[self.c, self.p, self.f], self.own)

    def start(self):
        looped(1, self.peers, lambda i: self.out(lax.rem(self.mine + i, self.peers)).start())
        self.local().start()

    def forward(self):
        self.local().wait()
        self.onward(self.mine, self.c).start()

        def one(i):
            k = lax.rem(self.mine + self.peers - i, self.peers)
            self.come(k).wait_recv()
            self.onward(k, self.c).start()

        looped(1, self.peers, one)

    def sent(self):
        looped(1, self.peers, lambda i: self.out(lax.rem(self.mine + i, self.peers)).wait_send())

    def finish(self):
        looped(0, self.peers, lambda k: self.onward(k, 1 - self.c).wait_recv())

    def passed(self):
        looped(0, self.peers, lambda k: self.onward(k, self.c).wait_send())


class Gathering:
    def __init__(self, fsdp_count, srcs, dsts, sends, recvs, own):
        self.f, self.y, self.c = place()
        self.count = fsdp_count
        self.planes = fsdp_count // 2
        self.z, self.x = self.f // 2, self.f % 2
        self.srcs, self.dsts, self.sends, self.recvs, self.own = srcs, dsts, sends, recvs, own
        self.x_side = device(self.z * 2 + 1 - self.x, self.y, self.c)
        self.y_side = device(self.f, 1 - self.y, self.c)

    def rows(self, dst, f, k):
        total = dst.shape[0] // self.count
        quarter = total // 4
        return dst.at[pl.ds(pl.multiple_of(f * total + k * quarter, 8), quarter)]

    def copies(self, link, f, k, where, fresh=False):
        out = []
        for n, (src, dst) in enumerate(zip(self.srcs, self.dsts)):
            there = self.rows(dst, f, k)
            quarter = src.shape[0] // 4
            here = src.at[pl.ds(pl.multiple_of(k * quarter, 8), quarter)] if fresh else there
            out.append(push(here, there, self.sends.at[n, link, f, k], self.recvs.at[n, f, k],
                            where))
        return out

    def go(self, *args, **kw):
        for copy in self.copies(*args, **kw):
            copy.start()

    def arrived(self, f, k):
        for copy in self.copies(0, f, k, self.x_side):
            copy.wait_recv()

    def plane(self, j):
        return lax.rem(self.z + j, self.planes)

    def z_out(self, j, k):
        out = []
        z = self.plane(j)
        where = device(2 * z + self.x, self.y, self.c)
        for n, (src, dst) in enumerate(zip(self.srcs, self.dsts)):
            quarter = src.shape[0] // 4
            out.append(push(src.at[pl.ds(pl.multiple_of(k * quarter, 8), quarter)],
                            self.rows(dst, self.f, k), self.sends.at[n, 0, 2 * z + self.x, k],
                            self.recvs.at[n, self.f, k], where))
        return out

    def local(self):
        return [
            pltpu.make_async_copy(
                src, dst.at[pl.ds(pl.multiple_of(self.f * src.shape[0], 8), src.shape[0])],
                self.own.at[n])
            for n, (src, dst) in enumerate(zip(self.srcs, self.dsts))
        ]

    def start_x(self):
        for copy in self.local():
            copy.start()
        for k in (2 * self.y, 2 * self.y + 1, 2 * (1 - self.y) + 1):
            self.go(1, self.f, k, self.x_side, fresh=True)

    def start_z(self):
        def one(j):
            for side in range(2):
                for copy in self.z_out(j, 2 * self.y + side):
                    copy.start()

        looped(1, self.planes, one)

    def start(self):
        self.start_z()
        self.start_x()

    def spread(self, j):
        f = 2 * self.plane(j) + self.x
        for side in range(2):
            k = 2 * self.y + side
            self.arrived(f, k)
            self.go(1, f, k, self.x_side)
            self.go(2, f, k, self.y_side)

    def turn_x(self, j):
        f = 2 * self.plane(j) + 1 - self.x
        self.arrived(f, 2 * self.y)
        self.go(2, f, 2 * self.y, self.y_side)

    def turn_y(self, j):
        f = 2 * self.plane(j) + self.x
        k = 2 * (1 - self.y) + 1
        self.arrived(f, k)
        self.go(1, f, k, self.x_side)

    def events(self):
        out = [functools.partial(self.spread, j) for j in range(1, self.planes)]
        out += [functools.partial(self.turn_x, 0)]
        for j in range(1, self.planes):
            out += [functools.partial(self.turn_x, j), functools.partial(self.turn_y, j)]
        return out

    def finish(self):
        x, y = self.x, self.y
        for copy in self.local():
            copy.wait()

        def one(j):
            other = 2 * self.plane(j) + 1 - x
            self.arrived(other, 2 * y + 1)
            self.arrived(other, 2 * (1 - y) + 1)
            self.arrived(other, 2 * (1 - y))

        looped(0, self.planes, one)

        def two(j):
            self.arrived(2 * self.plane(j) + x, 2 * (1 - y))

        looped(1, self.planes, two)

        for k in (2 * y, 2 * y + 1, 2 * (1 - y) + 1):
            for copy in self.copies(1, self.f, k, self.x_side, fresh=True):
                copy.wait_send()

        def three(j):
            f = 2 * self.plane(j) + x
            for side in range(2):
                k = 2 * y + side
                for copy in (*self.z_out(j, k), *self.copies(1, f, k, self.x_side),
                             *self.copies(2, f, k, self.y_side)):
                    copy.wait_send()
            for copy in self.copies(1, f, 2 * (1 - y) + 1, self.x_side):
                copy.wait_send()

        looped(1, self.planes, three)

        def four(j):
            for copy in self.copies(2, 2 * self.plane(j) + 1 - x, 2 * y, self.y_side):
                copy.wait_send()

        looped(0, self.planes, four)


def build_diagonals(table_ref, band):
    left = jnp.broadcast_to(band[0:1, :], (lanes, lanes))
    right = jnp.broadcast_to(band[3 * lanes - 1 : 3 * lanes, :], (lanes, lanes))
    for half in range(2):
        cols = slice(half * lanes, (half + 1) * lanes)
        first = far - lanes + half * lanes
        for row in range(0, first, lanes):
            table_ref[row : row + lanes, cols] = left
        table_ref[first : first + 3 * lanes, cols] = band
        for row in range(first + 3 * lanes, reach, lanes):
            table_ref[row : row + lanes, cols] = right


def attend_kernel(
    fsdp_count, gathers, bound_ref, idx_ref, small_ref, tok_ref, cot_ref, *refs,
):
    if gathers:
        wq_src, wo_src, wgu_src, wd_src, *refs = refs
    else:
        w_given, *refs = refs
    (xs_ref, cs_ref, qkv_ref, pl_ref, ps_ref, ctx_ref, ctx32_ref, linv_ref, gains_ref, w_ref,
     *refs) = refs
    if gathers:
        wo_ref, wgu_ref, wd_ref, *refs = refs
    (smalls, xa, ca, p_long, p_short, table, mask, band, km, vt, ctx_t, linv_t,
     deal_send, deal_recv, pass_send, pass_recv, own, ctx_send, ctx_recv, p_sem, *refs) = refs
    f, p, c = place()
    rows_all, width = xs_ref.shape
    part = width // 2
    pairs = part // lanes
    short = rows_all - longest
    half = lanes // 2
    sibling = device(f, p, 1 - c)

    greet_all(fsdp_count)
    deals = [
        Dealing(fsdp_count, src, dst, deal_send.at[n], deal_recv.at[n], pass_send.at[n],
                pass_recv.at[n], own.at[n])
        for n, (src, dst) in enumerate(((small_ref, smalls), (tok_ref, xa), (cot_ref, ca)))
    ]
    events = []
    deals[0].start()
    deals[1].start()
    if gathers:
        sends_q, recvs_q, own_q, sends_r, recvs_r, own_r = refs
        first = Gathering(fsdp_count, (wq_src,), (w_ref,), sends_q, recvs_q, own_q)
        rest = Gathering(fsdp_count, (wo_src, wgu_src, wd_src), (wo_ref, wgu_ref, wd_ref),
                         sends_r, recvs_r, own_r)
        first.start()
        rest.start_x()
    deals[0].forward()
    deals[0].finish()

    slice_width = width // fsdp_count

    def gain_of(k, total):
        row = iota((lanes, width), 0)
        spot = jnp.where((iota((lanes, width), 1) == k * slice_width + row) & (row < slice_width),
                         1.0, 0.0).astype(bf16)
        return total + nn(smalls[c, p, k].astype(bf16), spot)

    gains_ref[...] = lax.fori_loop(0, fsdp_count, gain_of, jnp.zeros((8, width), f32))

    wide = 4 * lanes
    place_of = iota((lanes, wide), 1)
    offset = jnp.where(place_of < wide // 2, -place_of, wide - place_of)
    chosen = jnp.where(bucket_index(offset) == iota((lanes, wide), 0), 1.0, 0.0).astype(bf16)
    for side in range(2):
        by_head = nn(smalls[side, c, f].astype(bf16), chosen)
        for h in range(pairs):
            line = jnp.broadcast_to(by_head[2 + h : 3 + h, :], (lanes, wide))
            for d in range(3):
                turned = pltpu.roll(line, d * lanes, 1, stride=1, stride_axis=0)
                band[side * pairs + h, d * lanes : (d + 1) * lanes, :] = turned[:, lanes : 2 * lanes]

    bound = bound_ref[0]
    inside = (iota((short, short), 0) < bound) == (iota((short, short), 1) < bound)
    mask[...] = jnp.where(inside, 0.0, -1e30)

    if gathers:
        for event in first.events()[: first.planes - 1]:
            event()
    deals[1].forward()
    if gathers:
        rest.start_z()
        for event in first.events()[first.planes - 1 :]:
            event()
        events = rest.events()
    else:
        given = pltpu.make_async_copy(w_given, w_ref, own.at[3])
        given.start()
        given.wait()
    deals[2].start()
    deals[1].finish()
    if gathers:
        first.finish()

    xa_rows = xa.shape[0] * xa.shape[1] * xa.shape[2] * xa.shape[3]

    def arrive(i):
        rows = pl.ds(pl.multiple_of(i * block, block), block)
        chosen = one_hot(idx_ref[rows, :], iota((block, xa_rows), 1))
        return rows, chosen

    def tile(i):
        rows, chosen = arrive(i)
        x = nn(chosen, xa[...].reshape(xa_rows, width))
        xs_ref[rows, :] = x.astype(bf16)
        normed = (x * inverse_rms(x) * gains_ref[0:1, :]).astype(bf16)
        for k in range(3):
            cols = slice(k * part, (k + 1) * part)
            qkv_ref[rows, cols] = nn(normed, w_ref[:, cols]).astype(bf16)

    looped(0, rows_all // block, tile)

    def poll(count):
        for _ in range(count):
            if events:
                events.pop(0)()

    own_lane = iota((rows_all, lanes), 1) < half
    for pair in range(pairs):
        cols = [slice(kind * part + pair * lanes, kind * part + (pair + 1) * lanes)
                for kind in range(3)]
        keys = qkv_ref[:, cols[1]]
        vt[...] = jnp.transpose(qkv_ref[:, cols[2]].astype(f32)).astype(bf16)
        for h in range(2):
            build_diagonals(table, band[2 * pair + h])
            km[...] = jnp.where(own_lane == (h == 0), keys, jnp.zeros_like(keys))

            def strip(base, count, out_ref, masked, b):
                here = pl.ds(pl.multiple_of(base + b * block, block), block)
                logits = nt(km[base : base + count, :], qkv_ref[here, cols[0]])
                top_row = pl.multiple_of(far - b * block, block)
                logits = logits + table[pl.ds(top_row, count), :]
                spot = pl.ds(pl.multiple_of(b * block, block), block)
                if masked:
                    logits = logits + mask[:, spot]
                top = jnp.max(logits, axis=0, keepdims=True)
                weights = jnp.exp(logits - top)
                inv = 1.0 / jnp.sum(weights, axis=0, keepdims=True)
                low = weights.astype(bf16)
                spot = pl.ds(pl.multiple_of(h * count + b * block, block), block)
                out_ref[pair % 2, :, spot] = low
                part_rows = slice(h * half, (h + 1) * half)
                ctx_t[part_rows, here] = nn(vt[part_rows, base : base + count], low) * inv
                linv_t[part_rows, here] = jnp.broadcast_to(inv, (half, block))

            if h == 0 and pair >= 2:
                for copy in p_copies(p_long, p_short, pl_ref, ps_ref, p_sem, pair - 2):
                    copy.wait()
            looped(0, longest // block, functools.partial(strip, 0, longest, p_long, False))
            poll(1)
            looped(0, short // block, functools.partial(strip, longest, short, p_short, True))
            poll(1)
        context = jnp.transpose(ctx_t[...])
        spot = c * pairs + pair
        ctx32_ref[:, pair * lanes : (pair + 1) * lanes] = context
        ctx_ref[spot] = context.astype(bf16)
        linv_ref[:, pair * lanes : (pair + 1) * lanes] = jnp.transpose(linv_t[...])
        push(ctx_ref.at[spot], ctx_ref.at[spot], ctx_send.at[pair], ctx_recv.at[pair],
             sibling).start()
        for copy in p_copies(p_long, p_short, pl_ref, ps_ref, p_sem, pair):
            copy.start()
        if pair == pairs - 2:
            deals[2].forward()
    poll(len(events))
    deals[2].finish()

    def cot_tile(i):
        rows, chosen = arrive(i)
        cs_ref[rows, :] = nn(chosen, ca[...].reshape(xa_rows, width)).astype(bf16)

    looped(0, rows_all // block, cot_tile)
    for pair in range(pairs):
        spot = c * pairs + pair
        there = (1 - c) * pairs + pair
        push(ctx_ref.at[spot], ctx_ref.at[spot], ctx_send.at[pair], ctx_recv.at[pair],
             sibling).wait_send()
        push(ctx_ref.at[there], ctx_ref.at[there], ctx_send.at[pair], ctx_recv.at[pair],
             sibling).wait_recv()
    for pair in range(max(0, pairs - 2), pairs):
        for copy in p_copies(p_long, p_short, pl_ref, ps_ref, p_sem, pair):
            copy.wait()
    for deal in deals:
        deal.sent()
        deal.passed()
    if gathers:
        rest.finish()


def p_copies(p_long, p_short, pl_ref, ps_ref, sem, pair):
    return [
        pltpu.make_async_copy(p_long.at[pair % 2], pl_ref.at[pair], sem.at[0, pair]),
        pltpu.make_async_copy(p_short.at[pair % 2], ps_ref.at[pair], sem.at[1, pair]),
    ]


def attend(fsdp_count, gathers, bound, idx_col, small, tokens, cotangent, *weights):
    rows = idx_col.shape[0]
    piece, width = tokens.shape[2:]
    part = width // 2
    pairs = part // lanes
    short = rows - longest
    vm = pl.BlockSpec(memory_space=pltpu.VMEM)
    hbm = pl.BlockSpec(memory_space=pl.ANY)
    dma = pltpu.SemaphoreType.DMA
    arrivals = pltpu.VMEM((2, 2, fsdp_count, piece, width), bf16)
    full = [jax.ShapeDtypeStruct((w.shape[0] * fsdp_count, w.shape[1]), bf16) for w in weights]
    out_shape = [
        jax.ShapeDtypeStruct((rows, width), bf16),
        jax.ShapeDtypeStruct((rows, width), bf16),
        jax.ShapeDtypeStruct((rows, 3 * part), bf16),
        jax.ShapeDtypeStruct((pairs, longest, 2 * longest), bf16),
        jax.ShapeDtypeStruct((pairs, short, 2 * short), bf16),
        jax.ShapeDtypeStruct((2 * pairs, rows, lanes), bf16),
        jax.ShapeDtypeStruct((rows, part), f32),
        jax.ShapeDtypeStruct((rows, part), f32),
        jax.ShapeDtypeStruct((8, width), f32),
        jax.ShapeDtypeStruct((width, 3 * part), bf16),
    ]
    out_specs = [vm, vm, vm, hbm, hbm, vm, vm, vm, vm, vm]
    scratch = [
        pltpu.VMEM((2, 2, fsdp_count, 8, lanes), f32),
        arrivals, arrivals,
        pltpu.VMEM((2, longest, 2 * longest), bf16),
        pltpu.VMEM((2, short, 2 * short), bf16),
        pltpu.VMEM((reach, block), f32),
        pltpu.VMEM((short, short), f32),
        pltpu.VMEM((2 * pairs, 3 * lanes, lanes), f32),
        pltpu.VMEM((rows, lanes), bf16),
        pltpu.VMEM((lanes, rows), bf16),
        pltpu.VMEM((lanes, rows), f32),
        pltpu.VMEM((lanes, rows), f32),
        dma((3, 2 * fsdp_count)), dma((3, 2 * fsdp_count)), dma((3, 2 * fsdp_count)),
        dma((3, 2 * fsdp_count)), dma((4,)), dma((pairs,)), dma((pairs,)), dma((2, pairs)),
    ]
    if gathers:
        out_shape += full[1:]
        out_specs += [hbm] * 3
        scratch += [
            dma((1, 3, fsdp_count, 4)), dma((1, fsdp_count, 4)), dma((1,)),
            dma((3, 3, fsdp_count, 4)), dma((3, fsdp_count, 4)), dma((3,)),
        ]
    return pl.pallas_call(
        functools.partial(attend_kernel, fsdp_count, gathers),
        in_specs=[pl.BlockSpec(memory_space=pltpu.SMEM), vm, vm, hbm, hbm] + [hbm] * len(weights),
        out_specs=tuple(out_specs),
        out_shape=tuple(out_shape),
        scratch_shapes=scratch,
        compiler_params=pltpu.CompilerParams(
            vmem_limit_bytes=vmem_limit, collective_id=0, has_side_effects=True),
        name="attend",
    )(bound, idx_col, small, tokens, cotangent, *weights)


def feed_kernel(
    ctx_ref, xs_ref, cs_ref, wo_ref, gains_ref, wgu_ref, wd_ref,
    out_ref, ggu_ref, gd_ref, datt_ref, dctx_ref, go_ref, ggain_ref,
    mid, nff, hid, dgu, dn, dn_sib, send, recv,
):
    rows_all, width = xs_ref.shape
    ff = wd_ref.shape[0]
    part = width // 2
    lift = math.sqrt(2 / math.pi)
    tiles = rows_all // block
    f, p, c = place()
    sibling = device(f, p, 1 - c)
    gain = gains_ref[1:2, :]
    half_cols = pl.ds(pl.multiple_of(c * part, lanes), part)
    barrier = pltpu.get_barrier_semaphore()
    signal(barrier, sibling)
    pl.semaphore_wait(barrier, 1)

    def exchange(i):
        rows = pl.ds(pl.multiple_of(i * block, block), block)
        return pltpu.make_async_remote_copy(
            src_ref=dn.at[rows, :], dst_ref=dn_sib.at[rows, :], send_sem=send.at[i],
            recv_sem=recv.at[i], device_id=sibling, device_id_type=MESH)

    def tile(i, carry):
        rows = pl.ds(pl.multiple_of(i * block, block), block)
        mixed = jnp.concatenate([ctx_ref[n, rows, :] for n in range(ctx_ref.shape[0])], axis=1)
        middle = xs_ref[rows, :].astype(f32) + nn(mixed, wo_ref[...])
        mid[rows, :] = middle
        normed = (middle * inverse_rms(middle) * gain).astype(bf16)
        nff[rows, :] = normed
        upstream = cs_ref[rows, :]
        gate = nn(normed, wgu_ref[:, :ff])
        up = nn(normed, wgu_ref[:, ff:])
        d_hidden = nt(upstream, wd_ref[...])
        square = gate * gate
        bent = jnp.tanh(lift * gate * (1.0 + 0.044715 * square))
        halved = 0.5 * (1.0 + bent)
        gelu = gate * halved
        slope = halved + 0.5 * gate * (1.0 - bent * bent) * (
            lift * (1.0 + 3 * 0.044715 * square))
        hidden = (gelu * up).astype(bf16)
        hid[rows, :] = hidden
        d_gate = (d_hidden * up * slope).astype(bf16)
        d_up = (d_hidden * gelu).astype(bf16)
        dgu[rows, :ff] = d_gate
        dgu[rows, ff:] = d_up
        dn[rows, :] = (nt(d_gate, wgu_ref[:, :ff]) + nt(d_up, wgu_ref[:, ff:])).astype(bf16)
        exchange(i).start()
        out_ref[rows, :] = (0.5 * middle + nn(hidden, wd_ref[...])).astype(bf16)
        return carry

    lax.fori_loop(0, tiles, tile, 0)

    def down(i, carry):
        cols = pl.ds(pl.multiple_of(i * block, block), block)
        gd_ref[cols, :] = tn(hid[:, cols], cs_ref[...]).astype(bf16)
        return carry

    lax.fori_loop(0, ff // block, down, 0)

    def settle(i, total):
        rows = pl.ds(pl.multiple_of(i * block, block), block)
        exchange(i).wait()
        mine = dn[rows, :].astype(f32)
        grad = mine + dn_sib[rows, :].astype(f32)
        middle = mid[rows, :]
        s = inverse_rms(middle)
        unit = middle * s
        scaled = gain * grad
        d_middle = cs_ref[rows, :].astype(f32) + s * (
            scaled - unit * jnp.mean(scaled * unit, axis=-1, keepdims=True))
        low = d_middle.astype(bf16)
        datt_ref[rows, :] = low
        dctx_ref[rows, :] = nt(low, wo_ref[half_cols, :]).astype(bf16)
        return total + jnp.sum(mine * unit, axis=0, keepdims=True)

    ggain_ref[...] = lax.fori_loop(0, tiles, settle, jnp.zeros((1, width), f32))
    for n in range(0, ctx_ref.shape[0], 2):
        mixed = jnp.concatenate((ctx_ref[n], ctx_ref[n + 1]), axis=1)
        go_ref[n * lanes : (n + 2) * lanes, :] = tn(mixed, datt_ref[:, half_cols]).astype(bf16)

    def gate_up(i, carry):
        cols = pl.ds(pl.multiple_of(i * block, block), block)
        ggu_ref[cols, :] = tn(nff[:, cols], dgu[...]).astype(bf16)
        return carry

    lax.fori_loop(0, width // block, gate_up, 0)


def feed(ctx, xs, cs, w_out, gains, w_gu, w_down):
    rows, width = xs.shape
    ff = w_down.shape[0]
    part = width // 2
    vm = pl.BlockSpec(memory_space=pltpu.VMEM)
    return pl.pallas_call(
        feed_kernel,
        in_specs=[vm] * 7,
        out_specs=(vm,) * 7,
        out_shape=(
            jax.ShapeDtypeStruct((rows, width), bf16),
            jax.ShapeDtypeStruct((width, 2 * ff), bf16),
            jax.ShapeDtypeStruct((ff, width), bf16),
            jax.ShapeDtypeStruct((rows, width), bf16),
            jax.ShapeDtypeStruct((rows, part), bf16),
            jax.ShapeDtypeStruct((width, part), bf16),
            jax.ShapeDtypeStruct((1, width), f32),
        ),
        scratch_shapes=[
            pltpu.VMEM((rows, width), f32),
            pltpu.VMEM((rows, width), bf16),
            pltpu.VMEM((rows, ff), bf16),
            pltpu.VMEM((rows, 2 * ff), bf16),
            pltpu.VMEM((rows, width), bf16),
            pltpu.VMEM((rows, width), bf16),
            pltpu.SemaphoreType.DMA((rows // block,)),
            pltpu.SemaphoreType.DMA((rows // block,)),
        ],
        compiler_params=pltpu.CompilerParams(
            vmem_limit_bytes=vmem_limit, collective_id=2, has_side_effects=True),
        name="feed",
    )(ctx, xs, cs, w_out, gains, w_gu, w_down)


def back_kernel(
    xs_ref, gain_ref, w_ref, datt_ref, dctx_ref, qkv_ref, pl_ref, ps_ref, ctx32_ref, linv_ref,
    y_ref, gqkv_ref, ggain_ref, band_ref,
    normed, dqkv, table, dos, qs, ds_l, ds_s, va, kt, dq_t,
):
    rows_all, width = xs_ref.shape
    pairs = pl.num_programs(0)
    part = pairs * lanes
    step = pl.program_id(0)
    short = rows_all - longest
    half = lanes // 2
    gain_attn = gain_ref[0:1, :]

    def columns(kind):
        return pl.ds(pl.multiple_of(kind * part + step * lanes, lanes), lanes)

    lane = iota((rows_all, lanes), 1)
    queries = qkv_ref[:, columns(0)]
    keys = qkv_ref[:, columns(1)]
    values = qkv_ref[:, columns(2)]
    none = jnp.zeros_like(keys)
    kt[...] = jnp.transpose(keys.astype(f32)).astype(bf16)
    scaled = (dctx_ref[:, columns(0)].astype(f32) * linv_ref[...]).astype(bf16)
    against = scaled.astype(f32) * ctx32_ref[...]
    for h in range(2):
        mine = (lane < half) if h == 0 else (lane >= half)
        spare = half if h == 0 else 0
        delta = jnp.sum(jnp.where(mine, against, 0.0), axis=1, keepdims=True)
        high = delta.astype(bf16).astype(f32)
        rest = delta - high
        extra = jnp.where(lane == spare, -high, jnp.where(lane == spare + 1, -rest, 0.0))
        dos[h] = jnp.where(mine, scaled.astype(f32), extra).astype(bf16)
        qs[h] = jnp.where(mine, queries, none)
        ones = jnp.where((lane == spare) | (lane == spare + 1), 1.0, 0.0)
        va[...] = jnp.where(mine, values.astype(f32), ones).astype(bf16)
        table[...] = jnp.zeros_like(table)

        def strip(base, count, p_ref, ds_ref, b, carry):
            here = pl.ds(pl.multiple_of(base + b * block, block), block)
            spot = pl.ds(pl.multiple_of(h * count + b * block, block), block)
            d_weights = nt(va[base : base + count, :], dos[h, here, :])
            d_logits = p_ref[0, :, spot].astype(f32) * d_weights
            window = pl.ds(pl.multiple_of(far - b * block, block), count)
            table[window, :] = table[window, :] + d_logits
            low = d_logits.astype(bf16)
            ds_ref[:, spot] = low
            part_rows = slice(h * half, (h + 1) * half)
            dq_t[part_rows, here] = nn(kt[part_rows, base : base + count], low)
            return carry

        lax.fori_loop(
            0, longest // block, functools.partial(strip, 0, longest, pl_ref, ds_l), 0)
        lax.fori_loop(
            0, short // block, functools.partial(strip, longest, short, ps_ref, ds_s), 0)
        before = far - lanes
        after = far + 3 * lanes
        band = table[before : before + 3 * lanes, :lanes] + table[far : far + 3 * lanes, lanes:]
        left = jnp.sum(table[:before, :lanes] + table[:before, lanes:], axis=0, keepdims=True)
        left = left + jnp.sum(table[before:far, lanes:], axis=0, keepdims=True)
        right = jnp.sum(table[after:, :lanes] + table[after:, lanes:], axis=0, keepdims=True)
        right = right + jnp.sum(table[after - lanes : after, :lanes], axis=0, keepdims=True)
        row = iota((3 * lanes, lanes), 0)
        band = band + jnp.where(row == 0, left, 0.0) + jnp.where(row == 3 * lanes - 1, right, 0.0)
        band_ref[h] = band

    dqkv[:, columns(0)] = jnp.transpose(dq_t[...]).astype(bf16)
    own = iota((rows_all, lanes), 1) < half
    for base, count, p_ref, ds_ref in ((0, longest, pl_ref, ds_l), (longest, short, ps_ref, ds_s)):
        rows = slice(base, base + count)
        clean = [
            jnp.where(own[rows] == (h == 0), dos[h, rows, :].astype(f32), 0.0).astype(bf16)
            for h in range(2)
        ]
        dqkv[rows, columns(2)] = nn(p_ref[0], jnp.concatenate(clean, axis=0)).astype(bf16)
        both = jnp.concatenate((qs[0, rows, :], qs[1, rows, :]), axis=0)
        dqkv[rows, columns(1)] = nn(ds_ref[...], both).astype(bf16)

    @pl.when(step == pairs - 1)
    def _():
        def tile(i, total):
            rows = pl.ds(pl.multiple_of(i * block, block), block)
            x = xs_ref[rows, :].astype(f32)
            s = inverse_rms(x)
            unit = x * s
            grad = nt(dqkv[rows, :], w_ref[...])
            scaled = gain_attn * grad
            y = 0.5 * datt_ref[rows, :].astype(f32) + s * (
                scaled - unit * jnp.mean(scaled * unit, axis=-1, keepdims=True))
            y_ref[rows, :] = y.astype(bf16)
            normed[rows, :] = (unit * gain_attn).astype(bf16)
            return total + jnp.sum(grad * unit, axis=0, keepdims=True)

        zero = jnp.zeros((1, width), f32)
        ggain_ref[...] = lax.fori_loop(0, rows_all // block, tile, zero)

        def weight(i, carry):
            cols = pl.ds(pl.multiple_of(i * block, block), block)
            gqkv_ref[cols, :] = tn(normed[:, cols], dqkv[...]).astype(bf16)
            return carry

        lax.fori_loop(0, width // block, weight, 0)


def back(xs, gain, w_qkv, datt, dctx, qkv, p_long, p_short, ctx32, linv):
    rows, width = xs.shape
    part = w_qkv.shape[1] // 3
    pairs = part // lanes
    short = rows - longest
    lane_block = pl.BlockSpec((rows, lanes), lambda i: (0, i))
    return pl.pallas_call(
        back_kernel,
        grid=(pairs,),
        in_specs=[
            *(whole_spec(a.shape) for a in (xs, gain, w_qkv, datt, dctx, qkv)),
            pl.BlockSpec((1, longest, 2 * longest), lambda i: (i, 0, 0)),
            pl.BlockSpec((1, short, 2 * short), lambda i: (i, 0, 0)),
            lane_block, lane_block,
        ],
        out_specs=(
            whole_spec((rows, width)),
            whole_spec((width, 3 * part)),
            whole_spec((1, width)),
            pl.BlockSpec((2, 3 * lanes, lanes), lambda i: (i, 0, 0)),
        ),
        out_shape=(
            jax.ShapeDtypeStruct((rows, width), bf16),
            jax.ShapeDtypeStruct((width, 3 * part), bf16),
            jax.ShapeDtypeStruct((1, width), f32),
            jax.ShapeDtypeStruct((2 * pairs, 3 * lanes, lanes), f32),
        ),
        scratch_shapes=[
            pltpu.VMEM((rows, width), bf16),
            pltpu.VMEM((rows, 3 * part), bf16),
            pltpu.VMEM((reach, block), f32),
            pltpu.VMEM((2, rows, lanes), bf16),
            pltpu.VMEM((2, rows, lanes), bf16),
            pltpu.VMEM((longest, 2 * longest), bf16),
            pltpu.VMEM((short, 2 * short), bf16),
            pltpu.VMEM((rows, lanes), bf16),
            pltpu.VMEM((lanes, rows), bf16),
            pltpu.VMEM((lanes, rows), f32),
        ],
        compiler_params=pltpu.CompilerParams(
            dimension_semantics=("arbitrary",), vmem_limit_bytes=vmem_limit),
        name="back",
    )(xs, gain, w_qkv, datt, dctx, qkv, p_long, p_short, ctx32, linv)


def home_kernel(fsdp_count, a_ref, b_ref, ra_ref, rb_ref, send, recv, own):
    f = lax.axis_index("fsdp")
    s = lax.axis_index("sp")
    p, c = s // 2, s % 2
    mine = p * fsdp_count + f
    peers = 2 * fsdp_count
    barrier = pltpu.get_barrier_semaphore()

    def where(k):
        return {"fsdp": k % fsdp_count, "sp": (k // fsdp_count) * 2 + c}

    def greet(i, carry):
        k = lax.rem(mine + i, peers)
        pl.semaphore_signal(barrier, inc=1, device_id=where(k), device_id_type=MESH)
        return carry

    lax.fori_loop(1, peers, greet, 0)
    pl.semaphore_wait(barrier, peers - 1)

    def piece(which, src, dst, k):
        return pltpu.make_async_remote_copy(
            src_ref=src.at[k // fsdp_count, k % fsdp_count],
            dst_ref=dst.at[p, f],
            send_sem=send.at[which, k],
            recv_sem=recv.at[which, mine],
            device_id=where(k),
            device_id_type=MESH,
        )

    def arrived(which, src, dst, k):
        return pltpu.make_async_remote_copy(
            src_ref=src.at[k // fsdp_count, k % fsdp_count],
            dst_ref=dst.at[k // fsdp_count, k % fsdp_count],
            send_sem=send.at[which, k],
            recv_sem=recv.at[which, k],
            device_id=where(k),
            device_id_type=MESH,
        )

    pairs = ((0, a_ref, ra_ref), (1, b_ref, rb_ref))
    for which, src, dst in pairs:

        def start(i, carry):
            piece(which, src, dst, lax.rem(mine + i, peers)).start()
            return carry

        lax.fori_loop(1, peers, start, 0)
        local = pltpu.make_async_copy(src.at[p, f], dst.at[p, f], own.at[which])
        local.start()
        local.wait()
    for which, src, dst in pairs:

        def finish(i, carry):
            k = lax.rem(mine + i, peers)
            arrived(which, src, dst, k).wait_recv()
            piece(which, src, dst, k).wait_send()
            return carry

        lax.fori_loop(1, peers, finish, 0)


def home(first, second):
    fsdp_count, piece, width = first.shape[1:]
    out = jax.ShapeDtypeStruct((2, fsdp_count, piece, width), bf16)
    hbm = pl.BlockSpec(memory_space=pl.ANY)
    sem = pltpu.SemaphoreType.DMA((2, 2 * fsdp_count))
    return pl.pallas_call(
        functools.partial(home_kernel, fsdp_count),
        out_shape=(out, out),
        in_specs=[hbm, hbm],
        out_specs=(hbm, hbm),
        scratch_shapes=[sem, sem, pltpu.SemaphoreType.DMA((2,))],
        compiler_params=pltpu.CompilerParams(collective_id=1, has_side_effects=True),
        name="home",
    )(first, second)


def unslot_kernel(idx_ref, a_ref, b_ref, oa_ref, ob_ref):
    rows_all = a_ref.shape[0]

    def tile(i):
        rows = pl.ds(pl.multiple_of(i * block, block), block)
        chosen = one_hot(iota((block, rows_all), 0) + i * block, idx_ref[...])
        oa_ref[rows, :] = nn(chosen, a_ref[...]).astype(bf16)
        ob_ref[rows, :] = nn(chosen, b_ref[...]).astype(bf16)

    looped(0, oa_ref.shape[0] // block, tile)


def unslot(rows, idx_row, first, second):
    vm = pl.BlockSpec(memory_space=pltpu.VMEM)
    out = jax.ShapeDtypeStruct((rows, first.shape[1]), bf16)
    return pl.pallas_call(
        unslot_kernel,
        in_specs=[vm] * 3,
        out_specs=(vm, vm),
        out_shape=(out, out),
        compiler_params=pltpu.CompilerParams(vmem_limit_bytes=vmem_limit),
        name="unslot",
    )(idx_row, first, second)


def shards(
    tokens, cotangent, lengths, dealing, gain_attn, w_query, w_key, w_value, w_out, bias_table,
    gain_ff, w_gate, w_up, w_down,
):
    fsdp_count = lax.axis_size("fsdp")
    sp_count = lax.axis_size("sp")
    micro_count, token_rows, width = tokens.shape
    piece = token_rows // fsdp_count
    group_rows = token_rows * sp_count
    local_heads = bias_table.shape[1]
    heads = local_heads * sp_count
    part = width // 2
    s = lax.axis_index("sp")
    p, c = s // 2, s % 2
    sibling = [(0, 1), (1, 0), (2, 3), (3, 2)]
    across = [(0, 2), (2, 0), (1, 3), (3, 1)]

    def swap(value):
        return lax.ppermute(value, "sp", sibling)

    full_piece = -(-piece // 8) * 8

    def pieces(value):
        value = value.reshape(micro_count, fsdp_count, piece, width)
        return jnp.pad(value, ((0, 0), (0, 0), (0, full_piece - piece), (0, 0)))

    order = lax.dynamic_index_in_dim(dealing[:, 0], p, 0, keepdims=False)
    length = lax.dynamic_index_in_dim(lengths[:, 0], p, 0, keepdims=False)
    first_long = length[0] == longest
    start = jnp.where(first_long, 0, jnp.where(length[1] == longest, length[0],
                                               length[0] + length[1]))
    bound = jnp.where(first_long, length[1], length[0]).reshape(1)
    short = group_rows - longest
    head_part = lax.dynamic_slice_in_dim(order, start, longest, 0)
    tail = jnp.where(jnp.arange(short) < start, order[:short], order[longest:])
    order = jnp.concatenate((head_part, tail))
    source, within = order // token_rows, order % token_rows
    idx = ((source % 2) * 2 + source // 2) * fsdp_count + within // piece
    idx = idx * full_piece + within % piece

    def half_cols(weight):
        return lax.dynamic_slice_in_dim(weight, c * part, part, 1)

    def half_ff(weight):
        split = weight.reshape(weight.shape[0], fsdp_count, 2, -1)
        return lax.dynamic_index_in_dim(split, c, 2, keepdims=False).reshape(weight.shape[0], -1)

    def gather(value, axis=0):
        return lax.all_gather(value, "fsdp", axis=axis, tiled=True)

    def line(value):
        return jnp.pad(value.astype(f32), ((0, 0), (0, lanes - value.shape[1])))

    small = jnp.concatenate([line(gain_attn[None]), line(gain_ff[None]), line(bias_table.T)])
    small = jnp.pad(small, ((0, 8 - small.shape[0]), (0, 0)))
    down_rows = w_down.shape[0] // 2
    weights = (
        jnp.concatenate([half_cols(w) for w in (w_query, w_key, w_value)], axis=1),
        w_out,
        jnp.concatenate([half_ff(w) for w in (w_gate, w_up)], axis=1),
        lax.dynamic_slice_in_dim(w_down, c * down_rows, down_rows, 0),
    )
    gathers = all(w.shape[0] % 32 == 0 for w in weights)
    if not gathers:
        weights = tuple(gather(w) for w in weights)
    args = (bound, idx.reshape(-1, 1), small, pieces(tokens), pieces(cotangent))
    xs, cs, qkv, p_long, p_short, ctx, ctx32, linv, gains, w_qkv, *late = attend(
        fsdp_count, gathers, *args, *(weights if gathers else weights[:1]))
    wo, w_gu, wd = late if gathers else weights[1:]
    buckets = band_buckets()
    out_part, grad_gu, grad_d, datt, dctx, grad_o, grad_gain_ff = feed(
        ctx, xs, cs, wo, gains, w_gu, wd)
    y, grad_qkv, grad_gain_attn, grad_band = back(
        xs, gains, w_qkv, datt, dctx, qkv, p_long, p_short, ctx32, linv)
    grad_gain = jnp.concatenate((grad_gain_attn, grad_gain_ff))
    back_rows = unslot(4 * fsdp_count * full_piece, idx.reshape(1, -1), out_part, y)
    mine = 2 * fsdp_count * full_piece
    shape = (2, fsdp_count, full_piece, width)

    def join(value):
        kept = lax.dynamic_slice_in_dim(value, c * mine, mine, 0)
        given = lax.dynamic_slice_in_dim(value, (1 - c) * mine, mine, 0)
        return (kept.astype(f32) + swap(given).astype(f32)).astype(bf16).reshape(shape)

    output, grad_tokens = (x[:, :, :piece] for x in home(join(back_rows[0]), join(back_rows[1])))

    def packed(values, unit):
        cut = [v.reshape(fsdp_count, v.shape[0] // fsdp_count, -1, unit) for v in values]
        cut = [jnp.swapaxes(v, 1, 2).reshape(fsdp_count, -1, unit) for v in cut]
        return jnp.concatenate(cut, axis=1)

    def scatter(values, unit):
        whole = packed(values, unit)
        share = lax.psum_scatter(whole, "fsdp", scatter_dimension=0, tiled=True)[0]
        out, at = [], 0
        for v in values:
            rows, count = v.shape[0] // fsdp_count, v.shape[1] // unit
            one = share[at : at + rows * count].reshape(count, rows, unit)
            out.append(jnp.swapaxes(one, 0, 1).reshape(rows, -1))
            at += rows * count
        return out

    shares = scatter((grad_gu, grad_d), 256) + scatter((grad_qkv, grad_o), 384)
    flat = jnp.concatenate([v.reshape(-1) for v in shares])
    flat = (flat.astype(f32) + lax.ppermute(flat, "sp", across).astype(f32)).astype(bf16)
    flat_sib = swap(flat)
    low = jnp.where(c == 0, flat, flat_sib).astype(f32)
    high = jnp.where(c == 0, flat_sib, flat).astype(f32)
    pieces = []
    at = 0
    for v in shares:
        pieces.append([x[at : at + v.size].reshape(v.shape) for x in (low, high)])
        at += v.size
    gu, gd, gqkv, go = pieces
    ff = gu[0].shape[1] // 2

    def ff_cols(which):
        sides = [x[:, which * ff : (which + 1) * ff].reshape(x.shape[0], fsdp_count, 1, -1)
                 for x in gu]
        return jnp.concatenate(sides, axis=2).reshape(gu[0].shape[0], -1)

    def proj(which):
        return jnp.concatenate([x[:, which * part : (which + 1) * part] for x in gqkv], axis=1)

    sums = jnp.stack([
        jnp.sum(jnp.where(buckets[None] == label, grad_band, 0.0), axis=(1, 2))
        for label in range(bias_table.shape[0])
    ])
    spread = jnp.zeros((bias_table.shape[0], heads), f32)
    spread = lax.dynamic_update_slice(spread, sums, (0, c * (heads // 2)))
    small = lax.psum(jnp.concatenate((grad_gain.reshape(-1), spread.reshape(-1))), ("fsdp", "sp"))
    own_gain = width // fsdp_count
    f = lax.axis_index("fsdp")
    gains_grad = lax.dynamic_slice_in_dim(small[: 2 * width].reshape(2, width), f * own_gain,
                                          own_gain, 1)
    bias_grad = lax.dynamic_slice_in_dim(small[2 * width :].reshape(-1, heads), s * local_heads,
                                         local_heads, 1)
    return (
        output.reshape(tokens.shape), grad_tokens.reshape(tokens.shape), gains_grad[0],
        proj(0), proj(1), proj(2), jnp.concatenate(go, axis=1), bias_grad, gains_grad[1],
        ff_cols(0), ff_cols(1), jnp.concatenate(gd, axis=0),
    )


def solution(mesh):
    return jax.shard_map(
        shards,
        mesh=mesh,
        in_specs=(
            P(None, ("fsdp", "sp"), None), P(None, ("fsdp", "sp"), None),
            P(None, "fsdp", None), P(None, "fsdp", None),
            P("fsdp"), P("fsdp", None), P("fsdp", None), P("fsdp", None), P("fsdp", None),
            P(None, "sp"), P("fsdp"), P("fsdp", None), P("fsdp", None), P("fsdp", None),
        ),
        out_specs=(
            P(None, ("fsdp", "sp"), None), P(None, ("fsdp", "sp"), None),
            P("fsdp"), P("fsdp", None), P("fsdp", None), P("fsdp", None), P("fsdp", None),
            P(None, "sp"), P("fsdp"), P("fsdp", None), P("fsdp", None), P("fsdp", None),
        ),
        check_vma=False,
    )
```

time: 639 us -> 597 us (0.934)
  blocking collectives: 68.8 us -> 49.3 us
  local copies, waits for them, and re-layouts: 60.5 us -> 52.1 us
    all_gather x2 -> x0, blocking collectives: 19.6 us -> none  [the longest x1 14.2 us: gather(): return lax.all_gather(value, 'fsdp', axis=axis, tiled=True)]
    pallas_call x3 -> x2, Pallas kernels: 191 us -> 184 us  [the longest x1 137 us: attend(): pl.pallas_call(functools.partial(attend_kernel, fsdp_count, gathers), in_...]
    slice x7 -> x0, local copies, waits for them, and re-layouts: 7.15 us -> none  [the longest x1 4.21 us: shards(): w_gu = rest[:, :2 * ff_wide]]
  transfers between devices with their start and end apart: 9 -> 6, of which waited for: 2 -> 2; matrix products, arithmetic and copies ran while one was open for 9% -> 6% of each run, Pallas kernels for 34% -> 12%
where the time goes in v2:
time: 597 us; the launch traced here: 593 us
  Pallas kernels  305 us (51%)
  waiting for transfers between devices  133 us (22%)
  local copies, waits for them, and re-layouts  52.1 us (9%)
  blocking collectives  49.3 us (8%)
  other arithmetic  31.8 us (5%)
  between operations  19.7 us (3%)
    pallas_call x1, Pallas kernels, attend(): pl.pallas_call(functools.partial(attend_kernel, fsdp_count, gathers), in_...  137 us
    reduce_scatter x2, waiting for transfers between devices, scatter(): share = lax.psum_scatter(whole, 'fsdp', scatter_dimension=0, tiled=True)[0]  133 us
    pallas_call x1, Pallas kernels, home(): pl.pallas_call(functools.partial(home_kernel, fsdp_count), out_shape=(out...  59.2 us
    pallas_call x1, Pallas kernels, back(): pl.pallas_call(back_kernel, grid=(pairs,), in_specs=[*(whole_spec(a.shape...  49.4 us
    psum x1, blocking collectives, shards(): lax.psum(jnp.concatenate((grad_gain.reshape(-1), spread.reshape(-1))), ('...  49.3 us
    pallas_call x1, Pallas kernels, feed(): pl.pallas_call(feed_kernel, in_specs=[vm] * 7, out_specs=(vm,) * 7, out_s...  46.7 us
    pallas_call x1, Pallas kernels, unslot(): pl.pallas_call(unslot_kernel, in_specs=[vm] * 3, out_specs=(vm, vm), out_...  12.5 us
  transfers between devices with their start and end apart: 6, of which 2 were waited for; matrix products, arithmetic and copies ran while one was open for 6% of the time, Pallas kernels for 12%

profile of v2, /device:TPU:14, one launch (start us, length us, event | category | flops | bytes accessed | tf_op | source)
XLA Modules:
  0.0 592.8 jit_solution(16825624217742611306)
XLA Ops:
  16.5 1.3 reshape.1166
  17.8 2.3 dynamic-slice_reduce_fusion
  23.6 3.3 fusion.5.idx_ref
  27.5 137.4 %attend.1 = (bf16[1536,768]{1,0:T(8,128)(2,1)}, bf16[1536,768]{1,0:T(8,128)(2,1)}, bf16[1536,1152]{1,0:T(8,128)(2,1)}, bf16[3,1024,2048]{2,1,0:T(8,128)(2,1)}, b...) custom-call(s32[1]{0:T(128)} %bitcast.6.bound_ref, ...), custom_call_target="tpu_custom_call" | custom-call | tf_op jit(solution)/shard_map/attend/pallas_call | solution.py:550
  165.0 46.7 %feed.1 = (bf16[1536,768]{1,0:T(8,128)(2,1)}, bf16[768,2048]{1,0:T(8,128)(2,1)}, bf16[1024,768]{1,0:T(8,128)(2,1)}, bf16[1536,768]{1,0:T(8,128)(2,1)}, bf16[1536...) custom-call(bf16[6,1536,128]{2,1,0:T(8,128)(2,1)} %get-tuple-element.40.ctx_ref, ...), custom_call_target="tpu_custom_call" | custom-call | tf_op jit(solution)/shard_map/feed/pallas_call | solution.py:657
  211.7 49.4 %back.1 = (bf16[1536,768]{1,0:T(8,128)(2,1)}, bf16[768,1152]{1,0:T(8,128)(2,1)}, f32[1,768]{1,0:T(1,128)}, f32[6,384,128]{2,1,0:T(8,128)}) custom-call(bf16[1536,768]{1,0:T(8,128)(2,1)} %get-tuple-element.41.xs_ref, f32[8,768]{1,0:T(8,128)} %get-tuple-element.44.gains_ref.gain_ref, bf16[768,1152]{1,0:T(8,128)(2,1)} %get-tuple-element.48.w_ref, ...), custom_call_target="tpu_custom_call" | custom-call | tf_op jit(solution)/shard_map/back/pallas_call | solution.py:795
  261.0 3.9 copy.104
  264.9 4.0 reshape.1183
  268.9 2.6 copy.105
  271.6 3.1 pad_maximum_fusion.1
  274.8 1.3 copy-done.5
  277.5 1.1 copy.101
  278.7 3.0 copy.114
  282.5 2.4 pad_maximum_fusion
  285.7 12.5 %unslot.1 = (bf16[1536,768]{1,0:T(8,128)(2,1)}, bf16[1536,768]{1,0:T(8,128)(2,1)}) custom-call(s32[1,1536]{1,0:T(1,128)} %fusion.30.idx_ref, bf16[1536,768]{1,0:T(8,128)(2,1)} %get-tuple-element.47.a_ref, bf16[1536,768]{1,0:T(8,128)(2,1)} %get-tuple-element.56.b_ref), custom_call_target="tpu_custom_call" | custom-call | tf_op jit(solution)/shard_map/unslot/pallas_call | solution.py:926
  298.2 2.5 constant_dynamic-slice_fusion.4
  301.2 1.1 constant_dynamic-slice_fusion.3
  302.4 2.2 broadcast_compare_fusion.15
  304.6 2.8 select_reduce_fusion.18
  307.4 35.6 %reduce-scatter.5.cloned.1.call-done = bf16[1,384,384]{2,1,0:T(8,128)(2,1)} async-done(((bf16[8,384,384]{2,1,0:T(8,128)(2,1)}), bf16[1,384,384]{2,1,0:T(8,128)(2,1)}) %reduce-scatter.5.cloned.1.call-update) | async-done | bytes 294928 | tf_op jit(solution)/shard_map/reduce_scatter | solution.py:1029
  344.4 97.8 %reduce-scatter.3.cloned.1.call-done = bf16[1,1152,256]{2,1,0:T(8,128)(2,1)} async-done(((bf16[8,1152,256]{2,1,0:T(8,128)(2,1)}), bf16[1,1152,256]{2,1,0:T(8,128)(2,1)}) %reduce-scatter.3.cloned.1.call-update) | async-done | bytes 589840 | tf_op jit(solution)/shard_map/reduce_scatter | solution.py:1029
  442.2 1.0 slice.236
  445.3 3.7 select_reduce_fusion
  449.6 49.3 %psum.7 = f32[1920]{0:T(1024)S(1)} all-reduce(f32[1920]{0:T(1024)S(1)} %pad_maximum_fusion.11), channel_id=1, replica_groups=mesh['fsdp'=8,'sp'=4] {'fsdp','sp'}, use_global_device_ids=true, to_apply=%region_32.33 | all-reduce | flops 1920 | bytes 15360 | tf_op jit(solution)/shard_map/psum | solution.py:1066
  500.7 3.1 add_convert_fusion.1
  503.8 2.6 add_convert_fusion
  506.4 59.2 %home.1 = (bf16[2,8,48,768]{3,2,1,0:T(8,128)(2,1)}, bf16[2,8,48,768]{3,2,1,0:T(8,128)(2,1)}) custom-call(bf16[2,8,48,768]{3,2,1,0:T(8,128)(2,1)} %bitcast.105, bf16[2,8,48,768]{3,2,1,0:T(8,128)(2,1)} %bitcast.106), custom_call_target="tpu_custom_call" | custom-call | tf_op jit(solution)/shard_map/home/pallas_call | solution.py:900
  569.8 1.6 slice.220
  574.2 1.5 reshape.1189
  577.4 1.5 reshape.1192
  583.0 1.0 copy.133
  584.7 1.0 copy.134
  (167 shorter events, 31.1 us)
Async XLA Ops:
  7.2 15.7 %copy-start = (bf16[256,768]{1,0:T(8,128)(2,1)S(1)}, bf16[256,768]{1,0:T(8,128)(2,1)}, u32[]{:S(2)}) copy-start(bf16[256,768]{1,0:T(8,128)(2,1)} %param.27) | copy-start | bytes 1179652
  7.2 8.4 %copy-start.32 = (bf16[32,3]{0,1:T(4,128)(2,1)S(1)}, bf16[32,3]{0,1:T(4,128)(2,1)}, u32[]{:S(2)}) copy-start(bf16[32,3]{0,1:T(4,128)(2,1)} %param.23) | copy-start | bytes 580
  7.2 8.4 %copy-start.33 = (bf16[96]{0:T(256)(128)(2,1)S(1)}, bf16[96]{0:T(256)(128)(2,1)}, u32[]{:S(2)}) copy-start(bf16[96]{0:T(256)(128)(2,1)} %param.24) | copy-start | bytes 580
  7.2 8.4 %copy-start.34 = (bf16[96]{0:T(256)(128)(2,1)S(1)}, bf16[96]{0:T(256)(128)(2,1)}, u32[]{:S(2)}) copy-start(bf16[96]{0:T(256)(128)(2,1)} %param.18) | copy-start | bytes 580
  7.2 9.0 %copy-start.17 = (bf16[96,2048]{1,0:T(8,128)(2,1)S(1)}, bf16[96,2048]{1,0:T(8,128)(2,1)}, u32[]{:S(2)}) copy-start(bf16[96,2048]{1,0:T(8,128)(2,1)} %param.26) | copy-start | bytes 1179652
  7.2 335.7 %reduce-scatter.5.cloned.1.call-start = ((), (), s32[]{:S(2)}) async-start(), calls=%async_computation.3 | async-start | bytes 2654208 | tf_op jit(solution)/shard_map/reduce_scatter | solution.py:1029
  268.9 2.6 copy-start.9
  274.7 167.5 %reduce-scatter.3.cloned.1.call-start = ((), (), s32[]{:S(2)}) async-start(), calls=%async_computation.2 | async-start | bytes 5308416 | tf_op jit(solution)/shard_map/reduce_scatter | solution.py:1029
  298.2 3.0 copy-start.3
  300.7 199.9 %collective-permute-start = (bf16[768,768]{1,0:T(8,128)(2,1)}, bf16[768,768]{1,0:T(8,128)(2,1)}, u32[]{:S(2)}, u32[]{:S(2)}) collective-permute-start(bf16[768,768]{1,0:T(8,128)(2,1)} %constant_dynamic-slice_fusion.4), channel_id=1, source_target_pairs={{0,1},{1,0},{2,3},{3,2},{4,5},{5,4},{6,7},{7,6},{8,9},{9,8},{10,11... | collective-permute-start | bytes 3538952 | tf_op jit(solution)/shard_map/ppermute | solution.py:954
  301.2 3.3 copy-start.2
  302.4 201.4 %collective-permute-start.1 = (bf16[768,768]{1,0:T(8,128)(2,1)}, bf16[768,768]{1,0:T(8,128)(2,1)}, u32[]{:S(2)}, u32[]{:S(2)}) collective-permute-start(bf16[768,768]{1,0:T(8,128)(2,1)} %constant_dynamic-slice_fusion.3), channel_id=1, source_target_pairs={{0,1},{1,0},{2,3},{3,2},{4,5},{5,4},{6,7},{7,6},{8,9},{9,8},{10,11... | collective-permute-start | bytes 3538952 | tf_op jit(solution)/shard_map/ppermute | solution.py:954
  444.5 4.5 copy-start.22
  444.5 4.5 copy-start.23
  444.5 4.5 copy-start.24
  444.5 4.5 copy-start.25
  444.5 4.5 copy-start.26
  444.5 4.5 copy-start.27
  444.5 4.5 copy-start.28
  444.6 4.5 copy-start.29
  444.6 4.5 copy-start.30
  444.6 4.5 copy-start.31
  444.6 5.0 copy-start.20
  444.6 5.0 copy-start.21
  444.7 55.1 %collective-permute-start.2 = (bf16[442368]{0:T(1024)(128)(2,1)S(1)}, bf16[442368]{0:T(1024)(128)(2,1)S(1)}, u32[]{:S(2)}, u32[]{:S(2)}) collective-permute-start(bf16[442368]{0:T(1024)(128)(2,1)S(1)} %constant_dynamic-update-slice_fusion), channel_id=1, source_target_pairs={{0,2},{2,0},{1,3},{3,1},{4,6},{6,4},{5,7},{7,5},{8,10},{10,8},{9,1... | collective-permute-start | bytes 2654216 | tf_op jit(solution)/shard_map/ppermute | solution.py:1040
  500.0 65.6 %collective-permute-start.3 = (bf16[442368]{0:T(1024)(128)(2,1)S(1)}, bf16[442368]{0:T(1024)(128)(2,1)S(1)}, u32[]{:S(2)}, u32[]{:S(2)}) collective-permute-start(bf16[442368]{0:T(1024)(128)(2,1)S(1)} %add_convert_fusion.2), channel_id=1, source_target_pairs={{0,1},{1,0},{2,3},{3,2},{4,5},{5,4},{6,7},{7,6},{8,9},{9,8},{10,11... | collective-permute-start | bytes 2654216 | tf_op jit(solution)/shard_map/ppermute | solution.py:954
  500.7 3.1 copy-start.4
  569.0 2.4 copy-start.14
  577.4 2.5 copy-start.10
  577.4 2.5 copy-start.12
  579.9 3.1 copy-start.8
  583.0 2.7 copy-start.1
  (11 other events, 18.4 us)
Sparse Core Ops, SparseCore 0:
  274.8 68.0 reduce-scatter.4
  346.6 95.5 reduce-scatter.2

commit v3 on v2

--- a/solution.py
+++ b/solution.py
@@ -18,7 +18,7 @@
 MESH = pl.DeviceIdType.MESH
 f32 = jnp.float32
 bf16 = jnp.bfloat16
-vmem_limit = 60 * 2**20
+vmem_limit = 62 * 2**20
 
 
 def nn(left, right):
@@ -560,8 +560,8 @@
 
 
 def feed_kernel(
-    ctx_ref, xs_ref, cs_ref, wo_ref, gains_ref, wgu_ref, wd_ref,
-    out_ref, ggu_ref, gd_ref, datt_ref, dctx_ref, go_ref, ggain_ref,
+    ctx_ref, ctx32_ref, linv_ref, xs_ref, cs_ref, wo_ref, gains_ref, wgu_ref, wd_ref,
+    out_ref, ggu_ref, gd_ref, datt_ref, dos_ref, go_ref, ggain_ref,
     mid, nff, hid, dgu, dn, dn_sib, send, recv,
 ):
     rows_all, width = xs_ref.shape
@@ -633,7 +633,19 @@
             scaled - unit * jnp.mean(scaled * unit, axis=-1, keepdims=True))
         low = d_middle.astype(bf16)
         datt_ref[rows, :] = low
-        dctx_ref[rows, :] = nt(low, wo_ref[half_cols, :]).astype(bf16)
+        d_context = nt(low, wo_ref[half_cols, :]).astype(bf16).astype(f32)
+        scaled = (d_context * linv_ref[rows, :]).astype(bf16).astype(f32)
+        against = scaled * ctx32_ref[rows, :]
+        lane = iota((block, lanes), 1)
+        for n in range(dos_ref.shape[0]):
+            cols = slice((n // 2) * lanes, (n // 2 + 1) * lanes)
+            mine_lanes = (lane < lanes // 2) == (n % 2 == 0)
+            spare = lanes // 2 if n % 2 == 0 else 0
+            delta = jnp.sum(jnp.where(mine_lanes, against[:, cols], 0.0), axis=1, keepdims=True)
+            high = delta.astype(bf16).astype(f32)
+            extra = jnp.where(lane == spare, -high,
+                              jnp.where(lane == spare + 1, high - delta, 0.0))
+            dos_ref[n, rows, :] = jnp.where(mine_lanes, scaled[:, cols], extra).astype(bf16)
         return total + jnp.sum(mine * unit, axis=0, keepdims=True)
 
     ggain_ref[...] = lax.fori_loop(0, tiles, settle, jnp.zeros((1, width), f32))
@@ -649,21 +661,21 @@
     lax.fori_loop(0, width // block, gate_up, 0)
 
 
-def feed(ctx, xs, cs, w_out, gains, w_gu, w_down):
+def feed(ctx, ctx32, linv, xs, cs, w_out, gains, w_gu, w_down):
     rows, width = xs.shape
     ff = w_down.shape[0]
     part = width // 2
     vm = pl.BlockSpec(memory_space=pltpu.VMEM)
     return pl.pallas_call(
         feed_kernel,
-        in_specs=[vm] * 7,
+        in_specs=[vm] * 9,
         out_specs=(vm,) * 7,
         out_shape=(
             jax.ShapeDtypeStruct((rows, width), bf16),
             jax.ShapeDtypeStruct((width, 2 * ff), bf16),
             jax.ShapeDtypeStruct((ff, width), bf16),
             jax.ShapeDtypeStruct((rows, width), bf16),
-            jax.ShapeDtypeStruct((rows, part), bf16),
+            jax.ShapeDtypeStruct((ctx.shape[0], rows, lanes), bf16),
             jax.ShapeDtypeStruct((width, part), bf16),
             jax.ShapeDtypeStruct((1, width), f32),
         ),
@@ -680,257 +692,504 @@
         compiler_params=pltpu.CompilerParams(
             vmem_limit_bytes=vmem_limit, collective_id=2, has_side_effects=True),
         name="feed",
-    )(ctx, xs, cs, w_out, gains, w_gu, w_down)
+    )(ctx, ctx32, linv, xs, cs, w_out, gains, w_gu, w_down)
+
+
+class Scattering:
+    def __init__(self, fsdp_count, grads, in_y, in_x, turned, in_z, final, send, recv):
+        self.f, self.y, self.c = place()
+        self.count = fsdp_count
+        self.planes = fsdp_count // 2
+        self.z, self.x = self.f // 2, self.f % 2
+        self.grads, self.in_y, self.in_x = grads, in_y, in_x
+        self.turned, self.in_z, self.final = turned, in_z, final
+        self.send, self.recv = send, recv
+        self.x_side = device(self.z * 2 + 1 - self.x, self.y, self.c)
+        self.y_side = device(self.f, 1 - self.y, self.c)
+        self.sibling = device(self.f, self.y, 1 - self.c)
+
+    def part(self, n, f, k):
+        return self.grads[n].at[f * 4 + k]
+
+    def plane(self, j):
+        return lax.rem(self.z + j, self.planes)
+
+    def order(self):
+        return [*range(1, self.planes), 0]
+
+    def move(self, n, kind, i, j, src, dst, where):
+        return push(src, dst, self.send.at[n, kind, i, j], self.recv.at[n, kind, i, j], where)
+
+    def along_y(self, n, z, x):
+        return self.move(n, 0, z, x, self.part(n, 2 * z + x, 2 * (1 - self.y)),
+                         self.in_y[n].at[z, x], self.y_side)
+
+    def along_x(self, n, z, y):
+        return self.move(n, 1, z, y, self.part(n, 2 * z + 1 - self.x, 2 * y + 1),
+                         self.in_x[n].at[z, y], self.x_side)
+
+    def turn(self, n, z, side):
+        if side == 0:
+            return self.move(n, 2, z, 0, self.in_y[n].at[z, 1 - self.x],
+                             self.turned[n].at[z, 0], self.x_side)
+        return self.move(n, 2, z, 1, self.in_x[n].at[z, 1 - self.y], self.turned[n].at[z, 1],
+                         self.y_side)
+
+    def summed(self, n, z, side):
+        return (self.in_y[n].at[z, self.x], self.in_x[n].at[z, self.y])[side]
+
+    def out_z(self, n, z, side):
+        return push(self.summed(n, z, side), self.in_z[n].at[self.z, side],
+                    self.send.at[n, 3, z, side], self.recv.at[n, 3, self.z, side],
+                    device(2 * z + self.x, self.y, self.c))
+
+    def come_z(self, n, z, side):
+        return push(self.summed(n, z, side), self.in_z[n].at[z, side],
+                    self.send.at[n, 3, z, side], self.recv.at[n, 3, z, side],
+                    device(2 * z + self.x, self.y, self.c))
+
+    def last_y(self, n, side, mine):
+        y = self.y if mine else 1 - self.y
+        here = self.final[n].at[self.c, 2 * y + side]
+        return self.move(n, 4, 0, side, here, here, self.y_side)
+
+    def last_core(self, n, mine):
+        here = self.final[n].at[self.c if mine else 1 - self.c]
+        return self.move(n, 5, 0, 0, here, here, self.sibling)
+
+    def each(self, body):
+        for n in range(len(self.grads)):
+            body(n)
+
+    def start(self):
+        for j in self.order():
+            z = self.plane(j)
+            for n in range(len(self.grads)):
+                for k in range(2):
+                    self.along_y(n, z, k).start()
+                    self.along_x(n, z, k).start()
+
+    def fold(self, j):
+        z = self.plane(j)
+        for n in range(len(self.grads)):
+            for k in range(2):
+                self.along_y(n, z, k).wait_recv()
+                add_to(self.in_y[n].at[z, k], self.part(n, 2 * z + k, 2 * self.y))
+            self.turn(n, z, 0).start()
+            for k in range(2):
+                self.along_x(n, z, k).wait_recv()
+                add_to(self.in_x[n].at[z, k], self.part(n, 2 * z + self.x, 2 * k + 1))
+            self.turn(n, z, 1).start()
+
+    def plane_sum(self, j):
+        z = self.plane(j)
+        for n in range(len(self.grads)):
+            for side in range(2):
+                self.turn(n, z, side).wait_recv()
+                add_to(self.summed(n, z, side), self.turned[n].at[z, side])
+                if j:
+                    self.out_z(n, z, side).start()
+
+    def total(self):
+        for n in range(len(self.grads)):
+            for side in range(2):
+                value = self.summed(n, self.z, side)[...].astype(f32)
+                for j in range(1, self.planes):
+                    z = self.plane(j)
+                    self.come_z(n, z, side).wait_recv()
+                    value = value + self.in_z[n][z, side].astype(f32)
+                self.final[n][self.c, 2 * self.y + side] = value.astype(bf16)
+                self.last_y(n, side, True).start()
+
+    def share(self):
+        for n in range(len(self.grads)):
+            for side in range(2):
+                self.last_y(n, side, False).wait_recv()
+            self.last_core(n, True).start()
+
+    def finish(self):
+        for n in range(len(self.grads)):
+            self.last_core(n, False).wait_recv()
+            self.last_core(n, True).wait_send()
+            for side in range(2):
+                self.last_y(n, side, True).wait_send()
+            for j in range(self.planes):
+                z = self.plane(j)
+                for k in range(2):
+                    self.along_y(n, z, k).wait_send()
+                    self.along_x(n, z, k).wait_send()
+                    self.turn(n, z, k).wait_send()
+                    if j:
+                        self.out_z(n, z, k).wait_send()
+
+    def events(self):
+        order = self.order()
+        out = [functools.partial(self.fold, order[0])]
+        for before, j in zip(order, order[1:]):
+            out += [functools.partial(self.fold, j), functools.partial(self.plane_sum, before)]
+        return out + [functools.partial(self.plane_sum, order[-1]), self.total, self.share]
+
+
+def add_to(here, other):
+    here[...] = (here[...].astype(f32) + other[...].astype(f32)).astype(bf16)
+
+
+class Homing:
+    def __init__(self, fsdp_count, src, dst, send, recv, own):
+        self.f, self.p, self.c = place()
+        self.count = fsdp_count
+        self.src, self.dst, self.send, self.recv, self.own = src, dst, send, recv, own
+
+    def out(self, q, g):
+        return push(self.src.at[q, g], self.dst.at[self.p, self.f], self.send.at[q, g],
+                    self.recv.at[self.p, self.f], device(g, q, self.c))
+
+    def come(self, q, g):
+        return push(self.src.at[q, g], self.dst.at[q, g], self.send.at[q, g],
+                    self.recv.at[q, g], device(g, q, self.c))
+
+    def local(self):
+        return pltpu.make_async_copy(self.src.at[self.p, self.f], self.dst.at[self.p, self.f],
+                                     self.own)
+
+    def start(self, q):
+        for i in range(1, self.count):
+            self.out(q, lax.rem(self.f + i, self.count)).start()
+
+    def start_other(self):
+        self.out(1 - self.p, self.f).start()
+        self.local().start()
+
+    def finish(self):
+        self.local().wait()
+        self.come(1 - self.p, self.f).wait_recv()
+        self.out(1 - self.p, self.f).wait_send()
+        for q in range(2):
+
+            def one(i, q=q):
+                g = lax.rem(self.f + i, self.count)
+                self.come(q, g).wait_recv()
+                self.out(q, g).wait_send()
+
+            looped(1, self.count, one)
 
 
 def back_kernel(
-    xs_ref, gain_ref, w_ref, datt_ref, dctx_ref, qkv_ref, pl_ref, ps_ref, ctx32_ref, linv_ref,
-    y_ref, gqkv_ref, ggain_ref, band_ref,
-    normed, dqkv, table, dos, qs, ds_l, ds_s, va, kt, dq_t,
+    fsdp_count, scatters, idx_ref, xs_ref, gains_ref, ggain_ref, w_ref, dos_ref, qkv_ref, datt_ref,
+    out_ref, pl_ref, ps_ref, *refs,
 ):
+    if scatters:
+        grads = refs[:3]
+        refs = refs[3:]
+    output_ref, tokens_ref, small_ref, *refs = refs
+    if scatters:
+        outs, refs = refs[:7], refs[7:]
+        gqkv_refs, refs = refs[:3], refs[3:]
+    else:
+        gqkv_refs, refs = refs[:3], refs[3:]
+    (ybuf, normed, dqkv, table, qs, ds_l, ds_s, p_l, p_s, acc, va, kt, dq_t, given, taken,
+     smalls, load, p_sem, pass_send, pass_recv, home_send, home_recv, own,
+     small_send, small_recv, small_pass, small_back, *refs) = refs
+    f, p, c = place()
+    sibling = device(f, p, 1 - c)
     rows_all, width = xs_ref.shape
-    pairs = pl.num_programs(0)
-    part = pairs * lanes
-    step = pl.program_id(0)
+    part = width // 2
+    pairs = part // lanes
     short = rows_all - longest
     half = lanes // 2
-    gain_attn = gain_ref[0:1, :]
-
-    def columns(kind):
-        return pl.ds(pl.multiple_of(kind * part + step * lanes, lanes), lanes)
+    gain_attn = gains_ref[0:1, :]
+    tile_rows = taken.shape[2] * taken.shape[3]
+
+    loading = pltpu.make_async_copy(out_ref, ybuf, load)
+    loading.start()
+
+    def p_copies(head):
+        pair, h = head // 2, head % 2
+        return [
+            pltpu.make_async_copy(pl_ref.at[pair, :, h * longest : (h + 1) * longest],
+                                  p_l.at[h], p_sem.at[0, h]),
+            pltpu.make_async_copy(ps_ref.at[pair, :, h * short : (h + 1) * short],
+                                  p_s.at[h], p_sem.at[1, h]),
+        ]
+
+    for head in range(2):
+        for copy in p_copies(head):
+            copy.start()
+    greet_all(fsdp_count)
+    sets = []
+    if scatters:
+        for group in range(1 + pairs):
+            arrays = grads if group == 0 else (gqkv_refs[group - 1],)
+            count = len(arrays)
+            bufs = [refs[k * count : (k + 1) * count] for k in range(5)]
+            send, recv = refs[5 * count : 5 * count + 2]
+            refs = refs[5 * count + 2 :]
+            sets.append(Scattering(fsdp_count, arrays, *bufs, send, recv))
+        sets[0].start()
+    events = sets[0].events() if scatters else []
+
+    def poll(count):
+        for _ in range(count):
+            if events:
+                events.pop(0)()
+
+    def unslot(side, q):
+        first = (side * 2 + q) * tile_rows
+        chosen = one_hot(iota((tile_rows, rows_all), 0) + first, idx_ref[...])
+        return nn(chosen, ybuf[...])
+
+    def pass_over(which, q):
+        return push(given.at[q], taken.at[which, q], pass_send.at[which, q],
+                    pass_recv.at[which, q], sibling)
+
+    homes = [
+        Homing(fsdp_count, taken.at[n], dst, home_send.at[n], home_recv.at[n], own.at[n])
+        for n, dst in enumerate((output_ref, tokens_ref))
+    ]
+
+    def give(which):
+        for q in range(2):
+            given[q] = unslot(1 - c, q).astype(bf16).reshape(given.shape[1:])
+            pass_over(which, q).start()
+
+    def keep(which):
+        for q in range(2):
+            pass_over(which, q).wait_recv()
+            value = unslot(c, q) + taken[which, q].reshape(tile_rows, width).astype(f32)
+            taken[which, q] = value.astype(bf16).reshape(taken.shape[2:])
+            homes[which].start(q)
+        homes[which].start_other()
+        for q in range(2):
+            pass_over(which, q).wait_send()
+
+    loading.wait()
+    give(0)
+
+    def norm_tile(i):
+        rows = pl.ds(pl.multiple_of(i * block, block), block)
+        x = xs_ref[rows, :].astype(f32)
+        normed[rows, :] = (x * inverse_rms(x) * gain_attn).astype(bf16)
+
+    looped(0, rows_all // block, norm_tile)
+    keep(0)
 
     lane = iota((rows_all, lanes), 1)
-    queries = qkv_ref[:, columns(0)]
-    keys = qkv_ref[:, columns(1)]
-    values = qkv_ref[:, columns(2)]
-    none = jnp.zeros_like(keys)
-    kt[...] = jnp.transpose(keys.astype(f32)).astype(bf16)
-    scaled = (dctx_ref[:, columns(0)].astype(f32) * linv_ref[...]).astype(bf16)
-    against = scaled.astype(f32) * ctx32_ref[...]
-    for h in range(2):
-        mine = (lane < half) if h == 0 else (lane >= half)
-        spare = half if h == 0 else 0
-        delta = jnp.sum(jnp.where(mine, against, 0.0), axis=1, keepdims=True)
-        high = delta.astype(bf16).astype(f32)
-        rest = delta - high
-        extra = jnp.where(lane == spare, -high, jnp.where(lane == spare + 1, -rest, 0.0))
-        dos[h] = jnp.where(mine, scaled.astype(f32), extra).astype(bf16)
-        qs[h] = jnp.where(mine, queries, none)
-        ones = jnp.where((lane == spare) | (lane == spare + 1), 1.0, 0.0)
-        va[...] = jnp.where(mine, values.astype(f32), ones).astype(bf16)
-        table[...] = jnp.zeros_like(table)
-
-        def strip(base, count, p_ref, ds_ref, b, carry):
-            here = pl.ds(pl.multiple_of(base + b * block, block), block)
-            spot = pl.ds(pl.multiple_of(h * count + b * block, block), block)
-            d_weights = nt(va[base : base + count, :], dos[h, here, :])
-            d_logits = p_ref[0, :, spot].astype(f32) * d_weights
-            window = pl.ds(pl.multiple_of(far - b * block, block), count)
-            table[window, :] = table[window, :] + d_logits
-            low = d_logits.astype(bf16)
-            ds_ref[:, spot] = low
-            part_rows = slice(h * half, (h + 1) * half)
-            dq_t[part_rows, here] = nn(kt[part_rows, base : base + count], low)
-            return carry
-
-        lax.fori_loop(
-            0, longest // block, functools.partial(strip, 0, longest, pl_ref, ds_l), 0)
-        lax.fori_loop(
-            0, short // block, functools.partial(strip, longest, short, ps_ref, ds_s), 0)
-        before = far - lanes
-        after = far + 3 * lanes
-        band = table[before : before + 3 * lanes, :lanes] + table[far : far + 3 * lanes, lanes:]
-        left = jnp.sum(table[:before, :lanes] + table[:before, lanes:], axis=0, keepdims=True)
-        left = left + jnp.sum(table[before:far, lanes:], axis=0, keepdims=True)
-        right = jnp.sum(table[after:, :lanes] + table[after:, lanes:], axis=0, keepdims=True)
-        right = right + jnp.sum(table[after - lanes : after, :lanes], axis=0, keepdims=True)
-        row = iota((3 * lanes, lanes), 0)
-        band = band + jnp.where(row == 0, left, 0.0) + jnp.where(row == 3 * lanes - 1, right, 0.0)
-        band_ref[h] = band
-
-    dqkv[:, columns(0)] = jnp.transpose(dq_t[...]).astype(bf16)
-    own = iota((rows_all, lanes), 1) < half
-    for base, count, p_ref, ds_ref in ((0, longest, pl_ref, ds_l), (longest, short, ps_ref, ds_s)):
-        rows = slice(base, base + count)
-        clean = [
-            jnp.where(own[rows] == (h == 0), dos[h, rows, :].astype(f32), 0.0).astype(bf16)
-            for h in range(2)
-        ]
-        dqkv[rows, columns(2)] = nn(p_ref[0], jnp.concatenate(clean, axis=0)).astype(bf16)
-        both = jnp.concatenate((qs[0, rows, :], qs[1, rows, :]), axis=0)
-        dqkv[rows, columns(1)] = nn(ds_ref[...], both).astype(bf16)
-
-    @pl.when(step == pairs - 1)
-    def _():
-        def tile(i, total):
-            rows = pl.ds(pl.multiple_of(i * block, block), block)
-            x = xs_ref[rows, :].astype(f32)
-            s = inverse_rms(x)
-            unit = x * s
-            grad = nt(dqkv[rows, :], w_ref[...])
-            scaled = gain_attn * grad
-            y = 0.5 * datt_ref[rows, :].astype(f32) + s * (
-                scaled - unit * jnp.mean(scaled * unit, axis=-1, keepdims=True))
-            y_ref[rows, :] = y.astype(bf16)
-            normed[rows, :] = (unit * gain_attn).astype(bf16)
-            return total + jnp.sum(grad * unit, axis=0, keepdims=True)
-
-        zero = jnp.zeros((1, width), f32)
-        ggain_ref[...] = lax.fori_loop(0, rows_all // block, tile, zero)
-
-        def weight(i, carry):
-            cols = pl.ds(pl.multiple_of(i * block, block), block)
-            gqkv_ref[cols, :] = tn(normed[:, cols], dqkv[...]).astype(bf16)
-            return carry
-
-        lax.fori_loop(0, width // block, weight, 0)
-
-
-def back(xs, gain, w_qkv, datt, dctx, qkv, p_long, p_short, ctx32, linv):
+    buckets = band_buckets()
+    small_ref_rows = iota((lanes // 4, lanes), 1)
+    bias = jnp.zeros((lanes // 4, lanes), f32)
+    for pair in range(pairs):
+        cols = [slice(kind * part + pair * lanes, kind * part + (pair + 1) * lanes)
+                for kind in range(3)]
+        queries = qkv_ref[:, cols[0]]
+        keys = qkv_ref[:, cols[1]]
+        values = qkv_ref[:, cols[2]]
+        kt[...] = jnp.transpose(keys.astype(f32)).astype(bf16)
+        for h in range(2):
+            head = 2 * pair + h
+            own_lanes = (lane < half) == (h == 0)
+            spare = half if h == 0 else 0
+            qs[...] = jnp.where(own_lanes, queries, jnp.zeros_like(queries))
+            ones = jnp.where((lane == spare) | (lane == spare + 1), 1.0, 0.0)
+            va[...] = jnp.where(own_lanes, values.astype(f32), ones).astype(bf16)
+            table[...] = jnp.zeros_like(table)
+            for copy in p_copies(head):
+                copy.wait()
+
+            def strip(base, count, p_buf, ds_buf, b):
+                here = pl.ds(pl.multiple_of(base + b * block, block), block)
+                spot = pl.ds(pl.multiple_of(b * block, block), block)
+                d_weights = nt(va[base : base + count, :], dos_ref[head, here, :])
+                d_logits = p_buf[h, :, spot].astype(f32) * d_weights
+                window = pl.ds(pl.multiple_of(far - b * block, block), count)
+                table[window, :] = table[window, :] + d_logits
+                low = d_logits.astype(bf16)
+                ds_buf[:, spot] = low
+                part_rows = slice(h * half, (h + 1) * half)
+                dq_t[part_rows, here] = nn(kt[part_rows, base : base + count], low)
+
+            looped(0, longest // block, functools.partial(strip, 0, longest, p_l, ds_l))
+            poll(1)
+            looped(0, short // block, functools.partial(strip, longest, short, p_s, ds_s))
+            for base, count, p_buf, ds_buf in ((0, longest, p_l, ds_l), (longest, short, p_s, ds_s)):
+                rows = slice(base, base + count)
+                clean = jnp.where(own_lanes[rows], dos_ref[head, rows, :].astype(f32), 0.0)
+                d_value = nn(p_buf[h], clean.astype(bf16))
+                d_key = nn(ds_buf[...], qs[rows, :])
+                if h == 0:
+                    acc[0, rows, :] = d_value
+                    acc[1, rows, :] = d_key
+                else:
+                    dqkv[rows, cols[2]] = (acc[0, rows, :] + d_value).astype(bf16)
+                    dqkv[rows, cols[1]] = (acc[1, rows, :] + d_key).astype(bf16)
+            if head + 2 < 2 * pairs:
+                for copy in p_copies(head + 2):
+                    copy.start()
+            before = far - lanes
+            after = far + 3 * lanes
+            band = table[before : before + 3 * lanes, :lanes] + table[far : far + 3 * lanes, lanes:]
+            left = jnp.sum(table[:before, :lanes] + table[:before, lanes:], axis=0, keepdims=True)
+            left = left + jnp.sum(table[before:far, lanes:], axis=0, keepdims=True)
+            right = jnp.sum(table[after:, :lanes] + table[after:, lanes:], axis=0, keepdims=True)
+            right = right + jnp.sum(table[after - lanes : after, :lanes], axis=0, keepdims=True)
+            for label in range(lanes // 4):
+                line = jnp.sum(jnp.where(buckets == label, band, 0.0), axis=0, keepdims=True)
+                if label == 15:
+                    line = line + left
+                if label == 31:
+                    line = line + right
+                table[label : label + 1, :lanes] = line
+            sums = jnp.sum(table[: lanes // 4, :lanes], axis=1, keepdims=True)
+            bias = bias + jnp.where(small_ref_rows == c * 2 * pairs + head, sums, 0.0)
+            poll(1)
+        dqkv[:, cols[0]] = jnp.transpose(dq_t[...]).astype(bf16)
+        for kind in range(3):
+            grad = tn(normed[...], dqkv[:, cols[kind]])
+            grad = grad.reshape(*gqkv_refs[pair].shape[:-1], lanes)
+            gqkv_refs[pair][..., kind * lanes : (kind + 1) * lanes] = grad.astype(bf16)
+        if pair == pairs - 1:
+            reload = pltpu.make_async_copy(datt_ref, normed, load)
+            reload.start()
+        if scatters:
+            sets[1 + pair].start()
+            events += sets[1 + pair].events()
+
+    def tile(i, total):
+        rows = slice(i * block, (i + 1) * block)
+        x = xs_ref[rows, :].astype(f32)
+        s = inverse_rms(x)
+        unit = x * s
+        grad = nt(dqkv[rows, :], w_ref[...])
+        scaled = gain_attn * grad
+        y = 0.5 * normed[rows, :].astype(f32) + s * (
+            scaled - unit * jnp.mean(scaled * unit, axis=-1, keepdims=True))
+        ybuf[rows, :] = y.astype(bf16)
+        return total + jnp.sum(grad * unit, axis=0, keepdims=True)
+
+    grad_gain = jnp.zeros((1, width), f32)
+    reload.wait()
+    for i in range(rows_all // block):
+        grad_gain = tile(i, grad_gain)
+    give(1)
+    quarter = lanes // 4
+    small_ref[0:quarter, :] = bias
+    small_ref[quarter:, :] = jnp.zeros((small_ref.shape[0] - quarter, lanes), f32)
+    for j in range(width // lanes):
+        cols = slice(j * lanes, (j + 1) * lanes)
+        small_ref[quarter + j : quarter + j + 1, :] = grad_gain[:, cols]
+        row = quarter + 8 + j
+        small_ref[row : row + 1, :] = ggain_ref[:, cols]
+    dealt = Dealing(fsdp_count, small_ref, smalls, small_send, small_recv, small_pass, small_back,
+                    own.at[2])
+    dealt.start()
+    keep(1)
+    poll(len(events))
+    dealt.forward()
+    dealt.finish()
+    dealt.sent()
+    dealt.passed()
+
+    def gather_small(k, total):
+        return total + smalls[k // (2 * fsdp_count), (k // fsdp_count) % 2, k % fsdp_count]
+
+    small_ref[...] = lax.fori_loop(0, 4 * fsdp_count, gather_small,
+                                   jnp.zeros(small_ref.shape, f32))
+    for group in sets:
+        group.finish()
+    if scatters:
+        gate, up, down, out_w, query, key, value = outs
+        gu, dn, wo = sets[0].final
+        ff = gu.shape[3] // 2
+        cut = ff // fsdp_count
+        for k in range(4):
+            for side in range(2):
+                rows = gu.shape[2]
+                rows = slice(k * rows, (k + 1) * rows)
+                for g in range(fsdp_count):
+                    there = slice((2 * g + side) * cut, (2 * g + side + 1) * cut)
+                    gate[rows, there] = gu[side, k, :, g * cut : (g + 1) * cut].astype(f32)
+                    up[rows, there] = gu[side, k, :, ff + g * cut : ff + (g + 1) * cut].astype(f32)
+                many = dn.shape[2]
+                first = (side * 4 + k) * many
+                down[first : first + many, :] = dn[side, k].astype(f32)
+                out_w[rows, side * part : (side + 1) * part] = wo[side, k].astype(f32)
+                for pair in range(pairs):
+                    [one] = sets[1 + pair].final
+                    there = slice(side * part + pair * lanes, side * part + (pair + 1) * lanes)
+                    for kind, ref in enumerate((query, key, value)):
+                        ref[rows, there] = one[side, k, :, kind * lanes : (kind + 1) * lanes].astype(
+                            f32)
+    for home in homes:
+        home.finish()
+
+
+def back(fsdp_count, piece, scatters, idx_row, xs, gains, ggain, w_qkv, datt, dos, qkv, out,
+         p_long, p_short, grads):
     rows, width = xs.shape
-    part = w_qkv.shape[1] // 3
+    part = width // 2
     pairs = part // lanes
     short = rows - longest
-    lane_block = pl.BlockSpec((rows, lanes), lambda i: (0, i))
+    vm = pl.BlockSpec(memory_space=pltpu.VMEM)
+    hbm = pl.BlockSpec(memory_space=pl.ANY)
+    dma = pltpu.SemaphoreType.DMA
+    shape = (2, fsdp_count, piece, width)
+    own_rows = width // fsdp_count
+    out_shape = [
+        jax.ShapeDtypeStruct(shape, bf16), jax.ShapeDtypeStruct(shape, bf16),
+        jax.ShapeDtypeStruct((48, lanes), f32),
+    ]
+    out_specs = [hbm, hbm, vm]
+    if scatters:
+        ff = grads[0].shape[1]
+        out_shape += [jax.ShapeDtypeStruct((own_rows, ff), f32)] * 2
+        out_shape += [jax.ShapeDtypeStruct((2 * grads[1].shape[0] // fsdp_count, width), f32)]
+        out_shape += [jax.ShapeDtypeStruct((own_rows, width), f32)] * 4
+        out_specs += [vm] * 7
+    gqkv = [jax.ShapeDtypeStruct((width, 3 * lanes), bf16)] * pairs
+    scratch = []
+    if scatters:
+        grads = tuple(g.reshape(4 * fsdp_count, -1, g.shape[1]) for g in grads)
+        scratch = [pltpu.VMEM((4 * fsdp_count, own_rows // 4, 3 * lanes), bf16)] * pairs
+    if not scatters:
+        out_shape += gqkv
+        out_specs += [vm] * pairs
+    scratch += [
+        pltpu.VMEM((rows, width), bf16),
+        pltpu.VMEM((rows, width), bf16),
+        pltpu.VMEM((rows, 3 * part), bf16),
+        pltpu.VMEM((reach, block), f32),
+        pltpu.VMEM((rows, lanes), bf16),
+        pltpu.VMEM((longest, longest), bf16),
+        pltpu.VMEM((short, short), bf16),
+        pltpu.VMEM((2, longest, longest), bf16),
+        pltpu.VMEM((2, short, short), bf16),
+        pltpu.VMEM((2, rows, lanes), f32),
+        pltpu.VMEM((rows, lanes), bf16),
+        pltpu.VMEM((lanes, rows), bf16),
+        pltpu.VMEM((lanes, rows), f32),
+        pltpu.VMEM(shape, bf16),
+        pltpu.VMEM((2, *shape), bf16),
+        pltpu.VMEM((2, 2, fsdp_count, 48, lanes), f32),
+        dma, dma((2, 2)), dma((2, 2)), dma((2, 2)),
+        dma((2, 2, fsdp_count)), dma((2, 2, fsdp_count)), dma((3,)),
+        *[dma((2 * fsdp_count,))] * 4,
+    ]
+    if scatters:
+        planes = fsdp_count // 2
+        for quarters in ([g.shape[1:] for g in grads], *[[(own_rows // 4, 3 * lanes)]] * pairs):
+            for lead in ((planes, 2), (planes, 2), (planes, 2), (planes, 2), (2, 4)):
+                scratch += [pltpu.VMEM((*lead, *q), bf16) for q in quarters]
+            scratch += [dma((len(quarters), 6, planes, 2))] * 2
     return pl.pallas_call(
-        back_kernel,
-        grid=(pairs,),
-        in_specs=[
-            *(whole_spec(a.shape) for a in (xs, gain, w_qkv, datt, dctx, qkv)),
-            pl.BlockSpec((1, longest, 2 * longest), lambda i: (i, 0, 0)),
-            pl.BlockSpec((1, short, 2 * short), lambda i: (i, 0, 0)),
-            lane_block, lane_block,
-        ],
-        out_specs=(
-            whole_spec((rows, width)),
-            whole_spec((width, 3 * part)),
-            whole_spec((1, width)),
-            pl.BlockSpec((2, 3 * lanes, lanes), lambda i: (i, 0, 0)),
-        ),
-        out_shape=(
-            jax.ShapeDtypeStruct((rows, width), bf16),
-            jax.ShapeDtypeStruct((width, 3 * part), bf16),
-            jax.ShapeDtypeStruct((1, width), f32),
-            jax.ShapeDtypeStruct((2 * pairs, 3 * lanes, lanes), f32),
-        ),
-        scratch_shapes=[
-            pltpu.VMEM((rows, width), bf16),
-            pltpu.VMEM((rows, 3 * part), bf16),
-            pltpu.VMEM((reach, block), f32),
-            pltpu.VMEM((2, rows, lanes), bf16),
-            pltpu.VMEM((2, rows, lanes), bf16),
-            pltpu.VMEM((longest, 2 * longest), bf16),
-            pltpu.VMEM((short, 2 * short), bf16),
-            pltpu.VMEM((rows, lanes), bf16),
-            pltpu.VMEM((lanes, rows), bf16),
-            pltpu.VMEM((lanes, rows), f32),
-        ],
+        functools.partial(back_kernel, fsdp_count, scatters),
+        in_specs=[vm] * 7 + [hbm] * 4 + [vm] * (len(grads) if scatters else 0),
+        out_specs=tuple(out_specs),
+        out_shape=tuple(out_shape),
+        scratch_shapes=scratch,
         compiler_params=pltpu.CompilerParams(
-            dimension_semantics=("arbitrary",), vmem_limit_bytes=vmem_limit),
+            vmem_limit_bytes=vmem_limit, collective_id=1, has_side_effects=True),
         name="back",
-    )(xs, gain, w_qkv, datt, dctx, qkv, p_long, p_short, ctx32, linv)
-
-
-def home_kernel(fsdp_count, a_ref, b_ref, ra_ref, rb_ref, send, recv, own):
-    f = lax.axis_index("fsdp")
-    s = lax.axis_index("sp")
-    p, c = s // 2, s % 2
-    mine = p * fsdp_count + f
-    peers = 2 * fsdp_count
-    barrier = pltpu.get_barrier_semaphore()
-
-    def where(k):
-        return {"fsdp": k % fsdp_count, "sp": (k // fsdp_count) * 2 + c}
-
-    def greet(i, carry):
-        k = lax.rem(mine + i, peers)
-        pl.semaphore_signal(barrier, inc=1, device_id=where(k), device_id_type=MESH)
-        return carry
-
-    lax.fori_loop(1, peers, greet, 0)
-    pl.semaphore_wait(barrier, peers - 1)
-
-    def piece(which, src, dst, k):
-        return pltpu.make_async_remote_copy(
-            src_ref=src.at[k // fsdp_count, k % fsdp_count],
-            dst_ref=dst.at[p, f],
-            send_sem=send.at[which, k],
-            recv_sem=recv.at[which, mine],
-            device_id=where(k),
-            device_id_type=MESH,
-        )
-
-    def arrived(which, src, dst, k):
-        return pltpu.make_async_remote_copy(
-            src_ref=src.at[k // fsdp_count, k % fsdp_count],
-            dst_ref=dst.at[k // fsdp_count, k % fsdp_count],
-            send_sem=send.at[which, k],
-            recv_sem=recv.at[which, k],
-            device_id=where(k),
-            device_id_type=MESH,
-        )
-
-    pairs = ((0, a_ref, ra_ref), (1, b_ref, rb_ref))
-    for which, src, dst in pairs:
-
-        def start(i, carry):
-            piece(which, src, dst, lax.rem(mine + i, peers)).start()
-            return carry
-
-        lax.fori_loop(1, peers, start, 0)
-        local = pltpu.make_async_copy(src.at[p, f], dst.at[p, f], own.at[which])
-        local.start()
-        local.wait()
-    for which, src, dst in pairs:
-
-        def finish(i, carry):
-            k = lax.rem(mine + i, peers)
-            arrived(which, src, dst, k).wait_recv()
-            piece(which, src, dst, k).wait_send()
-            return carry
-
-        lax.fori_loop(1, peers, finish, 0)
-
-
-def home(first, second):
-    fsdp_count, piece, width = first.shape[1:]
-    out = jax.ShapeDtypeStruct((2, fsdp_count, piece, width), bf16)
-    hbm = pl.BlockSpec(memory_space=pl.ANY)
-    sem = pltpu.SemaphoreType.DMA((2, 2 * fsdp_count))
-    return pl.pallas_call(
-        functools.partial(home_kernel, fsdp_count),
-        out_shape=(out, out),
-        in_specs=[hbm, hbm],
-        out_specs=(hbm, hbm),
-        scratch_shapes=[sem, sem, pltpu.SemaphoreType.DMA((2,))],
-        compiler_params=pltpu.CompilerParams(collective_id=1, has_side_effects=True),
-        name="home",
-    )(first, second)
-
-
-def unslot_kernel(idx_ref, a_ref, b_ref, oa_ref, ob_ref):
-    rows_all = a_ref.shape[0]
-
-    def tile(i):
-        rows = pl.ds(pl.multiple_of(i * block, block), block)
-        chosen = one_hot(iota((block, rows_all), 0) + i * block, idx_ref[...])
-        oa_ref[rows, :] = nn(chosen, a_ref[...]).astype(bf16)
-        ob_ref[rows, :] = nn(chosen, b_ref[...]).astype(bf16)
-
-    looped(0, oa_ref.shape[0] // block, tile)
-
-
-def unslot(rows, idx_row, first, second):
-    vm = pl.BlockSpec(memory_space=pltpu.VMEM)
-    out = jax.ShapeDtypeStruct((rows, first.shape[1]), bf16)
-    return pl.pallas_call(
-        unslot_kernel,
-        in_specs=[vm] * 3,
-        out_specs=(vm, vm),
-        out_shape=(out, out),
-        compiler_params=pltpu.CompilerParams(vmem_limit_bytes=vmem_limit),
-        name="unslot",
-    )(idx_row, first, second)
+    )(idx_row, xs, gains, ggain, w_qkv, dos, qkv, datt, out, p_long, p_short,
+      *(grads if scatters else ()))
 
 
 def shards(
@@ -947,12 +1206,6 @@
     part = width // 2
     s = lax.axis_index("sp")
     p, c = s // 2, s % 2
-    sibling = [(0, 1), (1, 0), (2, 3), (3, 2)]
-    across = [(0, 2), (2, 0), (1, 3), (3, 1)]
-
-    def swap(value):
-        return lax.ppermute(value, "sp", sibling)
-
     full_piece = -(-piece // 8) * 8
 
     def pieces(value):
@@ -1003,78 +1256,56 @@
         fsdp_count, gathers, *args, *(weights if gathers else weights[:1]))
     wo, w_gu, wd = late if gathers else weights[1:]
     buckets = band_buckets()
-    out_part, grad_gu, grad_d, datt, dctx, grad_o, grad_gain_ff = feed(
-        ctx, xs, cs, wo, gains, w_gu, wd)
-    y, grad_qkv, grad_gain_attn, grad_band = back(
-        xs, gains, w_qkv, datt, dctx, qkv, p_long, p_short, ctx32, linv)
-    grad_gain = jnp.concatenate((grad_gain_attn, grad_gain_ff))
-    back_rows = unslot(4 * fsdp_count * full_piece, idx.reshape(1, -1), out_part, y)
-    mine = 2 * fsdp_count * full_piece
-    shape = (2, fsdp_count, full_piece, width)
-
-    def join(value):
-        kept = lax.dynamic_slice_in_dim(value, c * mine, mine, 0)
-        given = lax.dynamic_slice_in_dim(value, (1 - c) * mine, mine, 0)
-        return (kept.astype(f32) + swap(given).astype(f32)).astype(bf16).reshape(shape)
-
-    output, grad_tokens = (x[:, :, :piece] for x in home(join(back_rows[0]), join(back_rows[1])))
-
-    def packed(values, unit):
-        cut = [v.reshape(fsdp_count, v.shape[0] // fsdp_count, -1, unit) for v in values]
-        cut = [jnp.swapaxes(v, 1, 2).reshape(fsdp_count, -1, unit) for v in cut]
-        return jnp.concatenate(cut, axis=1)
-
-    def scatter(values, unit):
-        whole = packed(values, unit)
-        share = lax.psum_scatter(whole, "fsdp", scatter_dimension=0, tiled=True)[0]
-        out, at = [], 0
-        for v in values:
-            rows, count = v.shape[0] // fsdp_count, v.shape[1] // unit
-            one = share[at : at + rows * count].reshape(count, rows, unit)
-            out.append(jnp.swapaxes(one, 0, 1).reshape(rows, -1))
-            at += rows * count
-        return out
-
-    shares = scatter((grad_gu, grad_d), 256) + scatter((grad_qkv, grad_o), 384)
-    flat = jnp.concatenate([v.reshape(-1) for v in shares])
-    flat = (flat.astype(f32) + lax.ppermute(flat, "sp", across).astype(f32)).astype(bf16)
-    flat_sib = swap(flat)
-    low = jnp.where(c == 0, flat, flat_sib).astype(f32)
-    high = jnp.where(c == 0, flat_sib, flat).astype(f32)
-    pieces = []
-    at = 0
-    for v in shares:
-        pieces.append([x[at : at + v.size].reshape(v.shape) for x in (low, high)])
-        at += v.size
-    gu, gd, gqkv, go = pieces
-    ff = gu[0].shape[1] // 2
-
-    def ff_cols(which):
-        sides = [x[:, which * ff : (which + 1) * ff].reshape(x.shape[0], fsdp_count, 1, -1)
-                 for x in gu]
-        return jnp.concatenate(sides, axis=2).reshape(gu[0].shape[0], -1)
-
-    def proj(which):
-        return jnp.concatenate([x[:, which * part : (which + 1) * part] for x in gqkv], axis=1)
-
-    sums = jnp.stack([
-        jnp.sum(jnp.where(buckets[None] == label, grad_band, 0.0), axis=(1, 2))
-        for label in range(bias_table.shape[0])
-    ])
-    spread = jnp.zeros((bias_table.shape[0], heads), f32)
-    spread = lax.dynamic_update_slice(spread, sums, (0, c * (heads // 2)))
-    small = lax.psum(jnp.concatenate((grad_gain.reshape(-1), spread.reshape(-1))), ("fsdp", "sp"))
+    out_part, grad_gu, grad_d, datt, dos, grad_o, grad_gain_ff = feed(
+        ctx, ctx32, linv, xs, cs, wo, gains, w_gu, wd)
+    output, grad_tokens, small, *grads = back(
+        fsdp_count, full_piece, gathers, idx.reshape(1, -1), xs, gains, grad_gain_ff, w_qkv, datt,
+        dos, qkv, out_part, p_long, p_short, (grad_gu, grad_d, grad_o))
+    output, grad_tokens = (x[:, :, :piece].reshape(tokens.shape) for x in (output, grad_tokens))
     own_gain = width // fsdp_count
     f = lax.axis_index("fsdp")
-    gains_grad = lax.dynamic_slice_in_dim(small[: 2 * width].reshape(2, width), f * own_gain,
-                                          own_gain, 1)
-    bias_grad = lax.dynamic_slice_in_dim(small[2 * width :].reshape(-1, heads), s * local_heads,
-                                         local_heads, 1)
+    labels = bias_table.shape[0]
+    bias_grad = lax.dynamic_slice_in_dim(small[:labels], s * local_heads, local_heads, 1)
+    gain_grads = [
+        lax.dynamic_slice_in_dim(
+            small[first : first + width // lanes].reshape(-1), f * own_gain, own_gain, 0)
+        for first in (labels, labels + 8)
+    ]
+    if not gathers:
+        grads = scatter_rows(fsdp_count, c, (grad_gu, grad_d, grad_o, *grads))
+    grad_gate, grad_up, grad_down, grad_out, grad_query, grad_key, grad_value = grads
     return (
-        output.reshape(tokens.shape), grad_tokens.reshape(tokens.shape), gains_grad[0],
-        proj(0), proj(1), proj(2), jnp.concatenate(go, axis=1), bias_grad, gains_grad[1],
-        ff_cols(0), ff_cols(1), jnp.concatenate(gd, axis=0),
+        output, grad_tokens, gain_grads[0], grad_query, grad_key, grad_value, grad_out, bias_grad,
+        gain_grads[1], grad_gate, grad_up, grad_down,
     )
+
+
+def scatter_rows(fsdp_count, c, partial_grads):
+    sibling = [(0, 1), (1, 0), (2, 3), (3, 2)]
+    across = [(0, 2), (2, 0), (1, 3), (3, 1)]
+    shares = [lax.psum_scatter(v, "fsdp", scatter_dimension=0, tiled=True) for v in partial_grads]
+    shares = [v.astype(f32) + lax.ppermute(v, "sp", across).astype(f32) for v in shares]
+    shares = [v.astype(bf16) for v in shares]
+    others = [lax.ppermute(v, "sp", sibling) for v in shares]
+    sides = [
+        (jnp.where(c == 0, v, w).astype(f32), jnp.where(c == 0, w, v).astype(f32))
+        for v, w in zip(shares, others)
+    ]
+    gu, down, out, *qkv = sides
+    rows = gu[0].shape[0]
+    ff = gu[0].shape[1] // 2
+
+    def ff_cols(which):
+        cut = [x[:, which * ff : (which + 1) * ff].reshape(rows, fsdp_count, 1, -1) for x in gu]
+        return jnp.concatenate(cut, axis=2).reshape(rows, -1)
+
+    def proj(kind):
+        return jnp.concatenate(
+            [pair[side][:, kind * lanes : (kind + 1) * lanes] for side in range(2) for pair in qkv],
+            axis=1)
+
+    return (ff_cols(0), ff_cols(1), jnp.concatenate(down), jnp.concatenate(out, axis=1),
+            proj(0), proj(1), proj(2))
 
 
 def solution(mesh):

time: 597 us -> 410 us (0.69)
  waiting for transfers between devices: 133 us -> 0 us
  Pallas kernels: 305 us -> 369 us
  blocking collectives: 49.3 us -> 0 us
  local copies, waits for them, and re-layouts: 52.1 us -> 22.5 us
  other arithmetic: 31.8 us -> 6.77 us
  between operations: 19.7 us -> 5.87 us
    reduce_scatter x2 -> x0, waiting for transfers between devices: 133 us -> none  [scatter(): share = lax.psum_scatter(whole, 'fsdp', scatter_dimension=0, tiled=True)[0]]
    pallas_call x4 -> x2, Pallas kernels: 168 us -> 232 us  [the longest x1 182 us: back(): pl.pallas_call(functools.partial(back_kernel, fsdp_count, scatters), in_s...]
    psum x1 -> x0, blocking collectives: 49.3 us -> none  [shards(): lax.psum(jnp.concatenate((grad_gain.reshape(-1), spread.reshape(-1))), ('...]
    concatenate x11 -> x0, other arithmetic: 10.9 us -> none  [the longest x2 5.57 us: packed(): return jnp.concatenate(cut, axis=1)]
    reshape x15 -> x1, local copies, waits for them, and re-layouts: 10.5 us -> 0.78 us  [shards(): small[first:first + width // lanes].reshape(-1)]
    slice x27 -> x1, local copies, waits for them, and re-layouts: 9.13 us -> 0.72 us  [shards(): small[:labels]]
    reduce_sum x2 -> x0, other arithmetic: 6.51 us -> none  [shards(): jnp.sum(jnp.where(buckets[None] == label, grad_band, 0.0), axis=(1, 2))]
    convert_element_type x4 -> x0, other arithmetic: 6.12 us -> none  [the longest x2 5.68 us: join(): (kept.astype(f32) + swap(given).astype(f32)).astype(bf16).reshape(shape)]
  transfers between devices with their start and end apart: 6 -> 0, of which waited for: 2 -> 0; matrix products, arithmetic and copies ran while one was open for 6% -> 0% of each run, Pallas kernels for 12% -> 0%
where the time goes in v3:
time: 410 us; the launch traced here: 404 us
  Pallas kernels  369 us (90%)
  local copies, waits for them, and re-layouts  22.5 us (5%)
  other arithmetic  6.77 us (2%)
  between operations  5.87 us (1%)
    pallas_call x1, Pallas kernels, back(): pl.pallas_call(functools.partial(back_kernel, fsdp_count, scatters), in_s...  182 us
    pallas_call x1, Pallas kernels, attend(): pl.pallas_call(functools.partial(attend_kernel, fsdp_count, gathers), in_...  137 us
    pallas_call x1, Pallas kernels, feed(): pl.pallas_call(feed_kernel, in_specs=[vm] * 9, out_specs=(vm,) * 7, out_s...  50 us
    unnamed x34, local copies, waits for them, and re-layouts  9.71 us

profile of v3, /device:TPU:14, one launch (start us, length us, event | category | flops | bytes accessed | tf_op | source)
XLA Modules:
  0.0 403.9 jit_solution(2226945198225889614)
XLA Ops:
  0.7 0.7 constant_dynamic-slice_fusion.8
  1.4 0.6 fusion.25
  6.6 0.7 fusion.21
  7.3 0.6 pad_convert_fusion.small_ref
  7.9 0.7 constant_dynamic-slice_fusion.6
  8.6 0.8 fusion.23
  9.3 0.7 fusion.13.idx_ref
  10.1 0.9 constant_dynamic-slice_fusion.5
  11.0 0.9 constant_dynamic-slice_fusion.3
  12.0 0.7 pad_maximum_fusion.1.refs_0_
  12.7 0.7 constant_dynamic-slice_fusion.2.refs_3_
  13.4 1.3 reshape.564
  14.9 2.3 dynamic-slice_reduce_fusion
  17.3 0.8 pad_maximum_fusion.refs_2_
  19.0 3.2 fusion.5.idx_ref
  22.2 136.9 %attend.1 = (bf16[1536,768]{1,0:T(8,128)(2,1)}, bf16[1536,768]{1,0:T(8,128)(2,1)}, bf16[1536,1152]{1,0:T(8,128)(2,1)}, bf16[3,1024,2048]{2,1,0:T(8,128)(2,1)}, b...) custom-call(s32[1]{0:T(128)} %bitcast.6.bound_ref, ...), custom_call_target="tpu_custom_call" | custom-call | tf_op jit(solution)/shard_map/attend/pallas_call | solution.py:550
  159.2 50.0 %feed.1 = (bf16[1536,768]{1,0:T(8,128)(2,1)}, bf16[768,2048]{1,0:T(8,128)(2,1)}, bf16[1024,768]{1,0:T(8,128)(2,1)}, bf16[1536,768]{1,0:T(8,128)(2,1)}, bf16[6,15...) custom-call(bf16[6,1536,128]{2,1,0:T(8,128)(2,1)} %get-tuple-element.44.ctx_ref, ...), custom_call_target="tpu_custom_call" | custom-call | tf_op jit(solution)/shard_map/feed/pallas_call | solution.py:669
  209.2 181.8 %back.1 = (bf16[2,8,48,768]{3,2,1,0:T(8,128)(2,1)}, bf16[2,8,48,768]{3,2,1,0:T(8,128)(2,1)}, f32[48,128]{1,0:T(8,128)}, f32[96,2048]{1,0:T(8,128)}, f32[96,2048]...) custom-call(s32[1,1536]{1,0:T(1,128)} %fusion.13.idx_ref, ...), custom_call_target="tpu_custom_call" | custom-call | tf_op jit(solution)/shard_map/back/pallas_call | solution.py:1182
  391.0 0.8 slice_bitcast_fusion
  391.8 0.7 slice.41
  392.6 0.7 copy.42
  393.3 0.6 dynamic_slice.50
  393.9 0.6 dynamic_slice.48
  394.4 2.4 copy.62
  396.9 1.0 copy.63
  397.9 0.7 copy.64
  398.6 0.7 copy.65
  399.3 0.7 copy.66
  400.1 0.7 copy.67
  400.8 0.9 copy.68
  401.7 0.9 copy.69
  402.5 0.9 copy.70
  (31 shorter events, 1.4 us)
Async XLA Ops:
  0.6 12.0 %copy-start = (bf16[256,768]{1,0:T(8,128)(2,1)S(1)}, bf16[256,768]{1,0:T(8,128)(2,1)}, u32[]{:S(2)}) copy-start(bf16[256,768]{1,0:T(8,128)(2,1)} %param.27) | copy-start | bytes 1179652
  0.7 14.0 %copy-start.6 = (bf16[96,2048]{1,0:T(8,128)(2,1)S(1)}, bf16[96,2048]{1,0:T(8,128)(2,1)}, u32[]{:S(2)}) copy-start(bf16[96,2048]{1,0:T(8,128)(2,1)} %param.26) | copy-start | bytes 1179652
  391.0 5.9 %copy-start.2 = (bf16[2,8,48,768]{3,2,1,0:T(8,128)(2,1)S(1)}, bf16[2,8,48,768]{3,2,1,0:T(8,128)(2,1)}, u32[]{:S(2)}) copy-start(bf16[2,8,48,768]{3,2,1,0:T(8,128)(2,1)} %get-tuple-element.63) | copy-start | bytes 3538948
  394.4 3.5 copy-start.10
  394.4 4.2 %copy-start.9 = (f32[96,768]{1,0:T(8,128)S(1)}, f32[96,768]{1,0:T(8,128)}, u32[]{:S(2)}) copy-start(f32[96,768]{1,0:T(8,128)} %get-tuple-element.139) | copy-start | bytes 884740
  394.4 4.9 %copy-start.8 = (f32[96,768]{1,0:T(8,128)S(1)}, f32[96,768]{1,0:T(8,128)}, u32[]{:S(2)}) copy-start(f32[96,768]{1,0:T(8,128)} %get-tuple-element.140) | copy-start | bytes 884740
  396.9 3.2 copy-start.7
  396.9 3.9 copy-start.5
  397.9 3.8 copy-start.4
  398.6 3.9 copy-start.3
  400.1 3.4 copy-start.1
